TPU v7x, 32 devices: a whole 2x2x4 slice. The times are simulated.
32 devices in a mesh: layer: 2 (over core), row: 2 (over y), col: 8 (over z, x).
Axes of the slice: x: 2, y: 2, z: 4, core: 2. Of those that a mesh axis runs over, the one named last changes fastest.
Arguments:
- amplitudes: bfloat16 [64, 128, 128], P(('row', 'col')), may hold values from -6 to 6
- integrals: bfloat16 [4096, 128, 128], P(('layer', 'row', 'col')), may hold values from -0.1875 to 0.1875
- amp_index: int32 [512, 48], P(('layer', 'row', 'col')), may hold values from 0 to 7
- left_index: int32 [512, 48], P(('layer', 'row', 'col')), may hold values from 0 to 127, as said below
- right_index: int32 [512, 48], P(('layer', 'row', 'col')), may hold values from 0 to 127, as said below
- dest_col: int32 [256, 1], P(('row', 'col')), may hold values from 0 to 7; in each aligned block of 16 rows (0 to 15, 16 to 31, ...) at most 2 rows name the same one
- owner_slot: int32 [256], P(('row', 'col')), may hold values from 0 to 7
Outputs:
- ladder: float32 [128, 128, 128], P(('row', 'col'))
Inputs may be any that keep to these rules, and one draw needn't show every extreme that they name: `dest_col`: among the 16 result tiles of one index of row and col, no owner column appears more than 2 times, and some column appears exactly 2 times. A term's amplitude tile is number amp_index among the tiles of the devices with the same col index, counted row by row. A term's left and right integral tiles belong to one auxiliary function: left_index // 2 == right_index // 2. right_index // 2 == left_index // 2 for every term.
All inputs are finite; a program needn't handle non-finite values.
Results may differ from a plain program's by a relative error of at most 0.0029.
Values may be sent and summed in bfloat16 or wider, within the bound.
No kernel may reach another device: no remote copies, remote signals or barrier semaphores. Data moves between devices by JAX's collectives and lax.ppermute only.
A program may use at most 64 MiB of HBM per device.

v0:
```python
import jax
import jax.numpy as jnp
from jax import lax
from jax.sharding import PartitionSpec as P

OWN = 8
CAP = 2


def select_tiles(stack_flat, picks, count, tile_edge):
    onehot = (picks[:, None] == jnp.arange(count, dtype=jnp.int32)[None, :]).astype(jnp.bfloat16)
    chosen = jnp.dot(onehot, stack_flat, preferred_element_type=jnp.float32).astype(jnp.bfloat16)
    return chosen.reshape(picks.shape[0], tile_edge, tile_edge)


def shards(amplitudes, integrals, amp_index, left_index, right_index, dest_col, owner_slot):
    columns = lax.axis_size("col")
    slot_count = dest_col.shape[0]
    tile_edge = integrals.shape[1]
    gathered = lax.all_gather(amplitudes, "row", axis=0, tiled=True)
    amp_total = gathered.shape[0]
    int_total = integrals.shape[0]
    amp_flat = gathered.reshape(amp_total, tile_edge * tile_edge)
    int_flat = integrals.reshape(int_total, tile_edge * tile_edge)

    def one_slot(operand_list):
        amp_ids, left_ids, right_ids = operand_list
        amp_tiles = select_tiles(amp_flat, amp_ids, amp_total, tile_edge)
        right_tiles = select_tiles(int_flat, right_ids, int_total, tile_edge)
        middle_product = jnp.einsum(
            "tcd,ted->tce", amp_tiles, right_tiles, preferred_element_type=jnp.float32
        ).astype(jnp.bfloat16)
        left_tile_blocks = select_tiles(int_flat, left_ids, int_total, tile_edge)
        return jnp.einsum(
            "dov,dvh->oh", left_tile_blocks, middle_product, preferred_element_type=jnp.float32
        )

    partials = lax.map(one_slot, (amp_index, left_index, right_index))
    target = dest_col[:, 0]
    counter = jnp.arange(slot_count, dtype=jnp.int32)
    earlier = (target[:, None] == target[None, :]) & (counter[None, :] < counter[:, None])
    position_in = jnp.sum(earlier.astype(jnp.int32), axis=1)
    position = target * CAP + position_in
    placing = (position[None, :] == jnp.arange(columns * CAP, dtype=jnp.int32)[:, None]).astype(
        jnp.float32
    )
    buffer = jnp.dot(
        placing,
        partials.reshape(slot_count, tile_edge * tile_edge),
        precision=lax.Precision.HIGHEST,
        preferred_element_type=jnp.float32,
    )
    buffer = buffer.reshape(columns, CAP, tile_edge, tile_edge)
    labels = (
        jnp.full((columns * CAP,), OWN, jnp.int32)
        .at[position]
        .set(owner_slot)
        .reshape(columns, CAP)
    )
    tiles_in, labels_in = (
        lax.all_to_all(buffer, "col", split_axis=0, concat_axis=0, tiled=True),
        lax.all_to_all(labels, "col", split_axis=0, concat_axis=0, tiled=True),
    )
    flattened = tiles_in.reshape(-1, tile_edge * tile_edge)
    owner_mask = (
        labels_in.reshape(-1)[:, None] == jnp.arange(OWN, dtype=jnp.int32)[None, :]
    ).astype(jnp.float32)
    owned_tiles = jnp.dot(
        owner_mask.T, flattened, precision=lax.Precision.HIGHEST, preferred_element_type=jnp.float32
    )
    owned_tiles = lax.psum(owned_tiles, "layer")
    return owned_tiles.reshape(OWN, tile_edge, tile_edge)


def solution(mesh):
    placed = (
        P(("row", "col"), None, None),
        P(("layer", "row", "col"), None, None),
        P(("layer", "row", "col"), None),
        P(("layer", "row", "col"), None),
        P(("layer", "row", "col"), None),
        P(("row", "col"), None),
        P(("row", "col")),
    )
    return jax.shard_map(
        shards, mesh=mesh, in_specs=placed, out_specs=P(("row", "col"), None, None), check_vma=False
    )
```

profile of v0, /device:TPU:0, one launch (start us, length us, event | category | flops | bytes accessed | tf_op | source)
XLA Modules:
  0.0 289.0 jit_solution(7846869162697204029)
XLA Ops:
  9.5 7.3 %all-to-all-start = ((s32[8,1,2]{2,1,0:T(1,128)}), s32[8,1,2]{2,1,0:T(1,128)S(1)}, u32[]{:S(2)}, u32[]{:S(2)}) async-start(s32[8,1,2]{2,1,0:T(1,128)} %bitcast.8), calls=%async_computation | async-start | bytes 8192 | tf_op jit(solution)/shard_map/all_to_all | solution.py:62
  17.5 7.7 %copy.42 = bf16[16,8,128,128]{3,1,2,0:T(8,128)(2,1)} copy(bf16[16,8,128,128]{3,2,1,0:T(8,128)(2,1)} %bitcast.106) | data formatting | bytes 8388608
  25.2 5.6 %all_gather.3 = bf16[8,128,128]{2,1,0:T(8,128)(2,1)S(1)} all-gather(bf16[4,128,128]{2,1,0:T(8,128)(2,1)S(1)} %copy-done.1), channel_id=1, replica_groups=mesh['layer'=2,'row'=2,'col'=8] {'row'}, dimensions={0}, use_global_device_ids=true | all-gather | bytes 393216 | tf_op jit(solution)/shard_map/all_gather | solution.py:20
  31.0 195.7 %while.10 = (s32[]{:T(128)}, f32[16,128,128]{2,1,0:T(8,128)}, s32[16,48]{1,0:T(8,128)}, bf16[128,16384]{1,0:T(8,128)(2,1)}, s32[16,48]{1,0:T(8,128)}, /*index=5*...) while((s32[]{:T(128)}, f32[16,128,128]{2,1,0:T(8,128)}, s32[16,48]{1,0:T(8,128)}, ...), condition=%wide.region_3.4_spmd, body=%wide.region_2.3_spmd.sunk | while | flops 821047680 | bytes 44370232 | solution.py:38
  31.7 2.9 %fusion.50 = bf16[6,8,128,128]{3,1,2,0:T(8,128)(2,1)S(1)} fusion(bf16[128,16384]{1,0:T(8,128)(2,1)} %get-tuple-element.125, s32[48]{0:T(128)S(1)} %get-tuple-element.104), kind=kOutput, calls=%fused_computation.5.clone.1 | convolution fusion | flops 202119168 | bytes 5767360 | tf_op jit(solution)/shard_map/while/body/eval_jaxpr/dot_general | solution.py:12
  36.1 0.9 fusion.52
  38.0 1.6 copy.49
  39.6 3.7 %fusion.54 = f32[16,128,128]{2,1,0:T(8,128)} fusion(f32[16,128,128]{2,1,0:T(8,128)} %get-tuple-element.115, s32[]{:T(128)} %get-tuple-element.114, bf16[48,128,128]{2,1,0:T(8,128)(2,1)S(1)} %bitcast.102, bf16[48,128,128]{2,1,0:T(8,128)(2,1)S(1)} %bitcast.103, bf16[48,128,128]{2,1,0:T(8,128)(2,1)} %bitcast.104), kind=kOutput, calls=%fused_computation.10.clone.1 | convolution fusion | flops 403439616 | bytes 4784640 | tf_op jit(solution)/shard_map/while/body/eval_jaxpr/dov,dvh->oh/dot_general | solution.py:34
  43.9 2.9 %fusion.50 = bf16[6,8,128,128]{3,1,2,0:T(8,128)(2,1)S(1)} fusion(bf16[128,16384]{1,0:T(8,128)(2,1)} %get-tuple-element.125, s32[48]{0:T(128)S(1)} %get-tuple-element.104), kind=kOutput, calls=%fused_computation.5.clone.1 | convolution fusion | flops 202119168 | bytes 5767360 | tf_op jit(solution)/shard_map/while/body/eval_jaxpr/dot_general | solution.py:12
  48.3 0.9 fusion.52
  50.2 1.6 copy.49
  51.8 3.7 %fusion.54 = f32[16,128,128]{2,1,0:T(8,128)} fusion(f32[16,128,128]{2,1,0:T(8,128)} %get-tuple-element.115, s32[]{:T(128)} %get-tuple-element.114, bf16[48,128,128]{2,1,0:T(8,128)(2,1)S(1)} %bitcast.102, bf16[48,128,128]{2,1,0:T(8,128)(2,1)S(1)} %bitcast.103, bf16[48,128,128]{2,1,0:T(8,128)(2,1)} %bitcast.104), kind=kOutput, calls=%fused_computation.10.clone.1 | convolution fusion | flops 403439616 | bytes 4784640 | tf_op jit(solution)/shard_map/while/body/eval_jaxpr/dov,dvh->oh/dot_general | solution.py:34
  56.2 2.9 %fusion.50 = bf16[6,8,128,128]{3,1,2,0:T(8,128)(2,1)S(1)} fusion(bf16[128,16384]{1,0:T(8,128)(2,1)} %get-tuple-element.125, s32[48]{0:T(128)S(1)} %get-tuple-element.104), kind=kOutput, calls=%fused_computation.5.clone.1 | convolution fusion | flops 202119168 | bytes 5767360 | tf_op jit(solution)/shard_map/while/body/eval_jaxpr/dot_general | solution.py:12
  62.5 1.6 copy.49
  64.0 3.7 %fusion.54 = f32[16,128,128]{2,1,0:T(8,128)} fusion(f32[16,128,128]{2,1,0:T(8,128)} %get-tuple-element.115, s32[]{:T(128)} %get-tuple-element.114, bf16[48,128,128]{2,1,0:T(8,128)(2,1)S(1)} %bitcast.102, bf16[48,128,128]{2,1,0:T(8,128)(2,1)S(1)} %bitcast.103, bf16[48,128,128]{2,1,0:T(8,128)(2,1)} %bitcast.104), kind=kOutput, calls=%fused_computation.10.clone.1 | convolution fusion | flops 403439616 | bytes 4784640 | tf_op jit(solution)/shard_map/while/body/eval_jaxpr/dov,dvh->oh/dot_general | solution.py:34
  68.4 2.9 %fusion.50 = bf16[6,8,128,128]{3,1,2,0:T(8,128)(2,1)S(1)} fusion(bf16[128,16384]{1,0:T(8,128)(2,1)} %get-tuple-element.125, s32[48]{0:T(128)S(1)} %get-tuple-element.104), kind=kOutput, calls=%fused_computation.5.clone.1 | convolution fusion | flops 202119168 | bytes 5767360 | tf_op jit(solution)/shard_map/while/body/eval_jaxpr/dot_general | solution.py:12
  74.7 1.6 copy.49
  76.3 3.7 %fusion.54 = f32[16,128,128]{2,1,0:T(8,128)} fusion(f32[16,128,128]{2,1,0:T(8,128)} %get-tuple-element.115, s32[]{:T(128)} %get-tuple-element.114, bf16[48,128,128]{2,1,0:T(8,128)(2,1)S(1)} %bitcast.102, bf16[48,128,128]{2,1,0:T(8,128)(2,1)S(1)} %bitcast.103, bf16[48,128,128]{2,1,0:T(8,128)(2,1)} %bitcast.104), kind=kOutput, calls=%fused_computation.10.clone.1 | convolution fusion | flops 403439616 | bytes 4784640 | tf_op jit(solution)/shard_map/while/body/eval_jaxpr/dov,dvh->oh/dot_general | solution.py:34
  80.6 2.9 %fusion.50 = bf16[6,8,128,128]{3,1,2,0:T(8,128)(2,1)S(1)} fusion(bf16[128,16384]{1,0:T(8,128)(2,1)} %get-tuple-element.125, s32[48]{0:T(128)S(1)} %get-tuple-element.104), kind=kOutput, calls=%fused_computation.5.clone.1 | convolution fusion | flops 202119168 | bytes 5767360 | tf_op jit(solution)/shard_map/while/body/eval_jaxpr/dot_general | solution.py:12
  86.9 1.6 copy.49
  88.5 3.7 %fusion.54 = f32[16,128,128]{2,1,0:T(8,128)} fusion(f32[16,128,128]{2,1,0:T(8,128)} %get-tuple-element.115, s32[]{:T(128)} %get-tuple-element.114, bf16[48,128,128]{2,1,0:T(8,128)(2,1)S(1)} %bitcast.102, bf16[48,128,128]{2,1,0:T(8,128)(2,1)S(1)} %bitcast.103, bf16[48,128,128]{2,1,0:T(8,128)(2,1)} %bitcast.104), kind=kOutput, calls=%fused_computation.10.clone.1 | convolution fusion | flops 403439616 | bytes 4784640 | tf_op jit(solution)/shard_map/while/body/eval_jaxpr/dov,dvh->oh/dot_general | solution.py:34
  92.9 2.9 %fusion.50 = bf16[6,8,128,128]{3,1,2,0:T(8,128)(2,1)S(1)} fusion(bf16[128,16384]{1,0:T(8,128)(2,1)} %get-tuple-element.125, s32[48]{0:T(128)S(1)} %get-tuple-element.104), kind=kOutput, calls=%fused_computation.5.clone.1 | convolution fusion | flops 202119168 | bytes 5767360 | tf_op jit(solution)/shard_map/while/body/eval_jaxpr/dot_general | solution.py:12
  99.1 1.6 copy.49
  100.7 3.7 %fusion.54 = f32[16,128,128]{2,1,0:T(8,128)} fusion(f32[16,128,128]{2,1,0:T(8,128)} %get-tuple-element.115, s32[]{:T(128)} %get-tuple-element.114, bf16[48,128,128]{2,1,0:T(8,128)(2,1)S(1)} %bitcast.102, bf16[48,128,128]{2,1,0:T(8,128)(2,1)S(1)} %bitcast.103, bf16[48,128,128]{2,1,0:T(8,128)(2,1)} %bitcast.104), kind=kOutput, calls=%fused_computation.10.clone.1 | convolution fusion | flops 403439616 | bytes 4784640 | tf_op jit(solution)/shard_map/while/body/eval_jaxpr/dov,dvh->oh/dot_general | solution.py:34
  105.1 2.9 %fusion.50 = bf16[6,8,128,128]{3,1,2,0:T(8,128)(2,1)S(1)} fusion(bf16[128,16384]{1,0:T(8,128)(2,1)} %get-tuple-element.125, s32[48]{0:T(128)S(1)} %get-tuple-element.104), kind=kOutput, calls=%fused_computation.5.clone.1 | convolution fusion | flops 202119168 | bytes 5767360 | tf_op jit(solution)/shard_map/while/body/eval_jaxpr/dot_general | solution.py:12
  111.4 1.6 copy.49
  113.0 3.7 %fusion.54 = f32[16,128,128]{2,1,0:T(8,128)} fusion(f32[16,128,128]{2,1,0:T(8,128)} %get-tuple-element.115, s32[]{:T(128)} %get-tuple-element.114, bf16[48,128,128]{2,1,0:T(8,128)(2,1)S(1)} %bitcast.102, bf16[48,128,128]{2,1,0:T(8,128)(2,1)S(1)} %bitcast.103, bf16[48,128,128]{2,1,0:T(8,128)(2,1)} %bitcast.104), kind=kOutput, calls=%fused_computation.10.clone.1 | convolution fusion | flops 403439616 | bytes 4784640 | tf_op jit(solution)/shard_map/while/body/eval_jaxpr/dov,dvh->oh/dot_general | solution.py:34
  117.3 2.9 %fusion.50 = bf16[6,8,128,128]{3,1,2,0:T(8,128)(2,1)S(1)} fusion(bf16[128,16384]{1,0:T(8,128)(2,1)} %get-tuple-element.125, s32[48]{0:T(128)S(1)} %get-tuple-element.104), kind=kOutput, calls=%fused_computation.5.clone.1 | convolution fusion | flops 202119168 | bytes 5767360 | tf_op jit(solution)/shard_map/while/body/eval_jaxpr/dot_general | solution.py:12
  123.6 1.6 copy.49
  125.2 3.7 %fusion.54 = f32[16,128,128]{2,1,0:T(8,128)} fusion(f32[16,128,128]{2,1,0:T(8,128)} %get-tuple-element.115, s32[]{:T(128)} %get-tuple-element.114, bf16[48,128,128]{2,1,0:T(8,128)(2,1)S(1)} %bitcast.102, bf16[48,128,128]{2,1,0:T(8,128)(2,1)S(1)} %bitcast.103, bf16[48,128,128]{2,1,0:T(8,128)(2,1)} %bitcast.104), kind=kOutput, calls=%fused_computation.10.clone.1 | convolution fusion | flops 403439616 | bytes 4784640 | tf_op jit(solution)/shard_map/while/body/eval_jaxpr/dov,dvh->oh/dot_general | solution.py:34
  129.6 2.9 %fusion.50 = bf16[6,8,128,128]{3,1,2,0:T(8,128)(2,1)S(1)} fusion(bf16[128,16384]{1,0:T(8,128)(2,1)} %get-tuple-element.125, s32[48]{0:T(128)S(1)} %get-tuple-element.104), kind=kOutput, calls=%fused_computation.5.clone.1 | convolution fusion | flops 202119168 | bytes 5767360 | tf_op jit(solution)/shard_map/while/body/eval_jaxpr/dot_general | solution.py:12
  135.8 1.6 copy.49
  137.4 3.7 %fusion.54 = f32[16,128,128]{2,1,0:T(8,128)} fusion(f32[16,128,128]{2,1,0:T(8,128)} %get-tuple-element.115, s32[]{:T(128)} %get-tuple-element.114, bf16[48,128,128]{2,1,0:T(8,128)(2,1)S(1)} %bitcast.102, bf16[48,128,128]{2,1,0:T(8,128)(2,1)S(1)} %bitcast.103, bf16[48,128,128]{2,1,0:T(8,128)(2,1)} %bitcast.104), kind=kOutput, calls=%fused_computation.10.clone.1 | convolution fusion | flops 403439616 | bytes 4784640 | tf_op jit(solution)/shard_map/while/body/eval_jaxpr/dov,dvh->oh/dot_general | solution.py:34
  141.8 2.9 %fusion.50 = bf16[6,8,128,128]{3,1,2,0:T(8,128)(2,1)S(1)} fusion(bf16[128,16384]{1,0:T(8,128)(2,1)} %get-tuple-element.125, s32[48]{0:T(128)S(1)} %get-tuple-element.104), kind=kOutput, calls=%fused_computation.5.clone.1 | convolution fusion | flops 202119168 | bytes 5767360 | tf_op jit(solution)/shard_map/while/body/eval_jaxpr/dot_general | solution.py:12
  146.2 0.9 fusion.52
  148.1 1.6 copy.49
  149.6 3.7 %fusion.54 = f32[16,128,128]{2,1,0:T(8,128)} fusion(f32[16,128,128]{2,1,0:T(8,128)} %get-tuple-element.115, s32[]{:T(128)} %get-tuple-element.114, bf16[48,128,128]{2,1,0:T(8,128)(2,1)S(1)} %bitcast.102, bf16[48,128,128]{2,1,0:T(8,128)(2,1)S(1)} %bitcast.103, bf16[48,128,128]{2,1,0:T(8,128)(2,1)} %bitcast.104), kind=kOutput, calls=%fused_computation.10.clone.1 | convolution fusion | flops 403439616 | bytes 4784640 | tf_op jit(solution)/shard_map/while/body/eval_jaxpr/dov,dvh->oh/dot_general | solution.py:34
  154.0 2.9 %fusion.50 = bf16[6,8,128,128]{3,1,2,0:T(8,128)(2,1)S(1)} fusion(bf16[128,16384]{1,0:T(8,128)(2,1)} %get-tuple-element.125, s32[48]{0:T(128)S(1)} %get-tuple-element.104), kind=kOutput, calls=%fused_computation.5.clone.1 | convolution fusion | flops 202119168 | bytes 5767360 | tf_op jit(solution)/shard_map/while/body/eval_jaxpr/dot_general | solution.py:12
  160.3 1.6 copy.49
  161.9 3.7 %fusion.54 = f32[16,128,128]{2,1,0:T(8,128)} fusion(f32[16,128,128]{2,1,0:T(8,128)} %get-tuple-element.115, s32[]{:T(128)} %get-tuple-element.114, bf16[48,128,128]{2,1,0:T(8,128)(2,1)S(1)} %bitcast.102, bf16[48,128,128]{2,1,0:T(8,128)(2,1)S(1)} %bitcast.103, bf16[48,128,128]{2,1,0:T(8,128)(2,1)} %bitcast.104), kind=kOutput, calls=%fused_computation.10.clone.1 | convolution fusion | flops 403439616 | bytes 4784640 | tf_op jit(solution)/shard_map/while/body/eval_jaxpr/dov,dvh->oh/dot_general | solution.py:34
  166.3 2.9 %fusion.50 = bf16[6,8,128,128]{3,1,2,0:T(8,128)(2,1)S(1)} fusion(bf16[128,16384]{1,0:T(8,128)(2,1)} %get-tuple-element.125, s32[48]{0:T(128)S(1)} %get-tuple-element.104), kind=kOutput, calls=%fused_computation.5.clone.1 | convolution fusion | flops 202119168 | bytes 5767360 | tf_op jit(solution)/shard_map/while/body/eval_jaxpr/dot_general | solution.py:12
  172.5 1.6 copy.49
  174.1 3.7 %fusion.54 = f32[16,128,128]{2,1,0:T(8,128)} fusion(f32[16,128,128]{2,1,0:T(8,128)} %get-tuple-element.115, s32[]{:T(128)} %get-tuple-element.114, bf16[48,128,128]{2,1,0:T(8,128)(2,1)S(1)} %bitcast.102, bf16[48,128,128]{2,1,0:T(8,128)(2,1)S(1)} %bitcast.103, bf16[48,128,128]{2,1,0:T(8,128)(2,1)} %bitcast.104), kind=kOutput, calls=%fused_computation.10.clone.1 | convolution fusion | flops 403439616 | bytes 4784640 | tf_op jit(solution)/shard_map/while/body/eval_jaxpr/dov,dvh->oh/dot_general | solution.py:34
  178.5 2.9 %fusion.50 = bf16[6,8,128,128]{3,1,2,0:T(8,128)(2,1)S(1)} fusion(bf16[128,16384]{1,0:T(8,128)(2,1)} %get-tuple-element.125, s32[48]{0:T(128)S(1)} %get-tuple-element.104), kind=kOutput, calls=%fused_computation.5.clone.1 | convolution fusion | flops 202119168 | bytes 5767360 | tf_op jit(solution)/shard_map/while/body/eval_jaxpr/dot_general | solution.py:12
  182.8 0.9 fusion.52
  184.8 1.6 copy.49
  186.3 3.7 %fusion.54 = f32[16,128,128]{2,1,0:T(8,128)} fusion(f32[16,128,128]{2,1,0:T(8,128)} %get-tuple-element.115, s32[]{:T(128)} %get-tuple-element.114, bf16[48,128,128]{2,1,0:T(8,128)(2,1)S(1)} %bitcast.102, bf16[48,128,128]{2,1,0:T(8,128)(2,1)S(1)} %bitcast.103, bf16[48,128,128]{2,1,0:T(8,128)(2,1)} %bitcast.104), kind=kOutput, calls=%fused_computation.10.clone.1 | convolution fusion | flops 403439616 | bytes 4784640 | tf_op jit(solution)/shard_map/while/body/eval_jaxpr/dov,dvh->oh/dot_general | solution.py:34
  190.7 2.9 %fusion.50 = bf16[6,8,128,128]{3,1,2,0:T(8,128)(2,1)S(1)} fusion(bf16[128,16384]{1,0:T(8,128)(2,1)} %get-tuple-element.125, s32[48]{0:T(128)S(1)} %get-tuple-element.104), kind=kOutput, calls=%fused_computation.5.clone.1 | convolution fusion | flops 202119168 | bytes 5767360 | tf_op jit(solution)/shard_map/while/body/eval_jaxpr/dot_general | solution.py:12
  195.1 0.9 fusion.52
  197.0 1.6 copy.49
  198.6 3.7 %fusion.54 = f32[16,128,128]{2,1,0:T(8,128)} fusion(f32[16,128,128]{2,1,0:T(8,128)} %get-tuple-element.115, s32[]{:T(128)} %get-tuple-element.114, bf16[48,128,128]{2,1,0:T(8,128)(2,1)S(1)} %bitcast.102, bf16[48,128,128]{2,1,0:T(8,128)(2,1)S(1)} %bitcast.103, bf16[48,128,128]{2,1,0:T(8,128)(2,1)} %bitcast.104), kind=kOutput, calls=%fused_computation.10.clone.1 | convolution fusion | flops 403439616 | bytes 4784640 | tf_op jit(solution)/shard_map/while/body/eval_jaxpr/dov,dvh->oh/dot_general | solution.py:34
  202.9 2.9 %fusion.50 = bf16[6,8,128,128]{3,1,2,0:T(8,128)(2,1)S(1)} fusion(bf16[128,16384]{1,0:T(8,128)(2,1)} %get-tuple-element.125, s32[48]{0:T(128)S(1)} %get-tuple-element.104), kind=kOutput, calls=%fused_computation.5.clone.1 | convolution fusion | flops 202119168 | bytes 5767360 | tf_op jit(solution)/shard_map/while/body/eval_jaxpr/dot_general | solution.py:12
  209.2 1.6 copy.49
  210.8 3.7 %fusion.54 = f32[16,128,128]{2,1,0:T(8,128)} fusion(f32[16,128,128]{2,1,0:T(8,128)} %get-tuple-element.115, s32[]{:T(128)} %get-tuple-element.114, bf16[48,128,128]{2,1,0:T(8,128)(2,1)S(1)} %bitcast.102, bf16[48,128,128]{2,1,0:T(8,128)(2,1)S(1)} %bitcast.103, bf16[48,128,128]{2,1,0:T(8,128)(2,1)} %bitcast.104), kind=kOutput, calls=%fused_computation.10.clone.1 | convolution fusion | flops 403439616 | bytes 4784640 | tf_op jit(solution)/shard_map/while/body/eval_jaxpr/dov,dvh->oh/dot_general | solution.py:34
  215.2 2.9 %fusion.50 = bf16[6,8,128,128]{3,1,2,0:T(8,128)(2,1)S(1)} fusion(bf16[128,16384]{1,0:T(8,128)(2,1)} %get-tuple-element.125, s32[48]{0:T(128)S(1)} %get-tuple-element.104), kind=kOutput, calls=%fused_computation.5.clone.1 | convolution fusion | flops 202119168 | bytes 5767360 | tf_op jit(solution)/shard_map/while/body/eval_jaxpr/dot_general | solution.py:12
  221.4 1.6 copy.49
  223.0 3.7 %fusion.54 = f32[16,128,128]{2,1,0:T(8,128)} fusion(f32[16,128,128]{2,1,0:T(8,128)} %get-tuple-element.115, s32[]{:T(128)} %get-tuple-element.114, bf16[48,128,128]{2,1,0:T(8,128)(2,1)S(1)} %bitcast.102, bf16[48,128,128]{2,1,0:T(8,128)(2,1)S(1)} %bitcast.103, bf16[48,128,128]{2,1,0:T(8,128)(2,1)} %bitcast.104), kind=kOutput, calls=%fused_computation.10.clone.1 | convolution fusion | flops 403439616 | bytes 4784640 | tf_op jit(solution)/shard_map/while/body/eval_jaxpr/dov,dvh->oh/dot_general | solution.py:34
  226.7 2.4 fusion.14
  229.1 1.2 copy.18
  230.3 6.0 %all-to-all-start.1 = ((f32[8,2,128,128]{3,2,1,0:T(8,128)}), f32[8,2,128,128]{3,2,1,0:T(8,128)S(1)}, u32[]{:S(2)}, u32[]{:S(2)}) async-start(f32[8,2,128,128]{3,2,1,0:T(8,128)} %copy.18), calls=%async_computation.1 | async-start | bytes 2097152 | tf_op jit(solution)/shard_map/all_to_all | solution.py:61
  237.6 23.0 %all-to-all-done.1 = f32[8,2,128,128]{3,2,1,0:T(8,128)S(1)} async-done(((f32[8,2,128,128]{3,2,1,0:T(8,128)}), f32[8,2,128,128]{3,2,1,0:T(8,128)S(1)}, u32[]{:S(2)}, u32[]{:S(2)}) %all-to-all-start.1) | async-done | bytes 1048608 | tf_op jit(solution)/shard_map/all_to_all | solution.py:61
  260.5 1.1 convolution_bitcast_fusion
  262.6 17.7 %all-reduce.2.cloned.1.call-done = f32[8,128,128]{2,1,0:T(8,128)} async-done(((f32[8,128,128]{2,1,0:T(8,128)}), f32[8,128,128]{2,1,0:T(8,128)}) %all-reduce.2.cloned.1.call-update) | async-done | bytes 524304 | tf_op jit(solution)/shard_map/psum | solution.py:71
  280.3 1.9 copy.58
  (140 shorter events, 65.5 us)
Async XLA Ops:
  9.5 220.7 %all-to-all-start = ((s32[8,1,2]{2,1,0:T(1,128)}), s32[8,1,2]{2,1,0:T(1,128)S(1)}, u32[]{:S(2)}, u32[]{:S(2)}) async-start(s32[8,1,2]{2,1,0:T(1,128)} %bitcast.8), calls=%async_computation | async-start | bytes 8192 | tf_op jit(solution)/shard_map/all_to_all | solution.py:62
  17.5 7.7 %copy-start.1 = (bf16[4,128,128]{2,1,0:T(8,128)(2,1)S(1)}, bf16[4,128,128]{2,1,0:T(8,128)(2,1)}, u32[]{:S(2)}) copy-start(bf16[4,128,128]{2,1,0:T(8,128)(2,1)} %param.9) | copy-start | bytes 393220
  35.0 2.2 copy-start
  47.3 2.2 copy-start
  59.5 2.2 copy-start
  71.7 2.2 copy-start
  84.0 2.2 copy-start
  96.2 2.2 copy-start
  108.4 2.2 copy-start
  120.7 2.2 copy-start
  132.9 2.2 copy-start
  145.1 2.2 copy-start
  157.4 2.2 copy-start
  169.6 2.2 copy-start
  181.8 2.2 copy-start
  194.0 2.2 copy-start
  206.3 2.2 copy-start
  218.5 2.2 copy-start
  230.3 30.3 %all-to-all-start.1 = ((f32[8,2,128,128]{3,2,1,0:T(8,128)}), f32[8,2,128,128]{3,2,1,0:T(8,128)S(1)}, u32[]{:S(2)}, u32[]{:S(2)}) async-start(f32[8,2,128,128]{3,2,1,0:T(8,128)} %copy.18), calls=%async_computation.1 | async-start | bytes 2097152 | tf_op jit(solution)/shard_map/all_to_all | solution.py:61
  236.3 44.1 %all-reduce.2.cloned.1.call-start = ((), (), s32[]{:S(2)}) async-start(), calls=%async_computation.2 | async-start | bytes 1048576 | tf_op jit(solution)/shard_map/psum | solution.py:71
Sparse Core Ops, SparseCore 0:
  262.7 17.5 all-reduce.1
where the time goes:
time: 291 us; the launch traced here: 289 us
  matrix products  130 us (45%)
  local copies, waits for them, and re-layouts  81.8 us (28%)
  waiting for transfers between devices  40.7 us (14%)
  between operations  13.4 us (5%)
  starting transfers between devices  13.3 us (5%)
  blocking collectives  5.63 us (2%)
    dot_general x48, matrix products, select_tiles(): jnp.dot(onehot, stack_flat, preferred_element_type=jnp.float32)  68.2 us
    dot_general x16, matrix products, one_slot(): jnp.einsum('dov,dvh->oh', left_tile_blocks, middle_product, preferred_ele...  58.8 us
    while x80, local copies, waits for them, and re-layouts  41.7 us
    eq x32, local copies, waits for them, and re-layouts, select_tiles(): picks[:, None] == jnp.arange(count, dtype=jnp.int32)[None, :]  26.3 us
    all_to_all x1, waiting for transfers between devices, shards(): lax.all_to_all(buffer, 'col', split_axis=0, concat_axis=0, tiled=True)  23 us
    psum x1, waiting for transfers between devices, shards(): owned_tiles = lax.psum(owned_tiles, 'layer')  17.7 us
    unnamed x5, local copies, waits for them, and re-layouts  9.76 us
    all_to_all x1, starting transfers between devices, shards(): lax.all_to_all(labels, 'col', split_axis=0, concat_axis=0, tiled=True)  7.25 us
  transfers between devices with their start and end apart: 3, of which 2 were waited for; matrix products, arithmetic and copies ran while one was open for 71% of the time, Pallas kernels for 0%

commit v1 on v0

v1 whole, which is shorter than its diff:
```python
import functools

import jax
import jax.numpy as jnp
from jax import lax
from jax.experimental import pallas as pl
from jax.experimental.pallas import tpu as pltpu
from jax.sharding import PartitionSpec as P

OWN = 8
CAP = 2
LABEL_ROWS = 16
F32 = jnp.float32
BF16 = jnp.bfloat16
VMEM_BYTES = 56 << 20


def smem():
    return pl.BlockSpec(memory_space=pltpu.SMEM)


def vmem():
    return pl.BlockSpec(memory_space=pltpu.VMEM)


def transpose_kernel(tiles, flipped):
    count = tiles.shape[0]
    step = 8

    def body(i, carry):
        for j in range(step):
            flipped[i * step + j] = tiles[i * step + j].T
        return carry

    lax.fori_loop(0, count // step, body, 0)


def flip_tiles(integrals):
    return pl.pallas_call(
        transpose_kernel,
        out_shape=jax.ShapeDtypeStruct(integrals.shape, integrals.dtype),
        in_specs=[vmem()],
        out_specs=vmem(),
        compiler_params=pltpu.CompilerParams(vmem_limit_bytes=VMEM_BYTES),
        name="flip_tiles",
    )(integrals)


def ladder_kernel(
    columns, unroll, rank_of_layer, amp_ids, left_ids, right_ids, dest, labels, place,
    own_amp, other_amp, tiles, flipped, out, *rest,
):
    if len(rest) == 4:
        label_out, amps, slot_of, seen = rest
    else:
        label_out = None
        amps, slot_of, seen = rest
    slot_count, terms = amp_ids.shape
    amp_dev = own_amp.shape[0]
    layer = place[0]
    row = place[1]
    rank = layer if rank_of_layer else 1 - layer
    if other_amp is None:
        amps[...] = own_amp[...]
    else:
        amps[pl.ds(row * amp_dev, amp_dev)] = own_amp[...]
        amps[pl.ds((1 - row) * amp_dev, amp_dev)] = other_amp[...]
    for d in range(columns):
        slot_of[d] = 0
        seen[d] = 0

    def scan(k, carry):
        d = dest[k, 0]
        count = seen[d]
        seen[d] = count + 1

        @pl.when(count == rank)
        def _():
            slot_of[d] = k

        return carry

    lax.fori_loop(0, slot_count, scan, 0)

    def body(i, carry):
        for u in range(unroll):
            d = i * unroll + u
            k = slot_of[d]
            lefts = [tiles[left_ids[k, t]] for t in range(terms)]
            middles = [
                jnp.dot(
                    amps[amp_ids[k, t]], flipped[right_ids[k, t]], preferred_element_type=F32
                ).astype(BF16)
                for t in range(terms)
            ]
            out[d] = jnp.dot(
                jnp.concatenate(lefts, axis=1),
                jnp.concatenate(middles, axis=0),
                preferred_element_type=F32,
            )
            if label_out is not None:
                label = jnp.where(seen[d] > rank, labels[k], OWN).astype(F32)
                label_out[d] = jnp.full(label_out.shape[1:], label, F32).astype(BF16)
        return carry

    lax.fori_loop(0, columns // unroll, body, 0)


def owner_kernel(near, far, out):
    edge = out.shape[1]
    sources = near.shape[0]
    for chunk in range(edge // 32):
        rows = pl.ds(chunk * 32, 32)
        totals = [jnp.zeros((32, edge), F32) for _ in range(OWN)]
        for c in range(sources):
            for ref in (near, far):
                label = ref[c, edge : edge + LABEL_ROWS, :].astype(F32)
                label = jnp.concatenate([label] * (32 // LABEL_ROWS), axis=0)
                tile = ref[c, rows, :].astype(F32)
                for s in range(OWN):
                    totals[s] = totals[s] + jnp.where(label == s, tile, 0.0)
        for s in range(OWN):
            out[s, rows, :] = totals[s]


def swap(array, axis):
    size = lax.axis_size(axis)
    return lax.ppermute(array, axis, [(i, i ^ 1) for i in range(size)])


def shards(amplitudes, integrals, amp_index, left_index, right_index, dest_col, owner_slot):
    columns = lax.axis_size("col")
    rows = lax.axis_size("row")
    edge = integrals.shape[1]
    if rows == 2:
        amp_parts = (amplitudes, swap(amplitudes, "row"))
    else:
        amp_parts = (lax.all_gather(amplitudes, "row", axis=0, tiled=True),)
    amp_total = rows * amplitudes.shape[0]
    flipped = flip_tiles(integrals)
    place = jnp.stack([lax.axis_index("layer"), lax.axis_index("row")]).astype(jnp.int32)

    def ladder(keep):
        def kernel(*refs):
            head, tail = refs[:7], refs[7:]
            if rows != 2:
                tail = (None,) + tail
            return ladder_kernel(columns, 4, keep, *head, *tail)

        tile_out = jax.ShapeDtypeStruct((columns, edge, edge), F32)
        label_out = jax.ShapeDtypeStruct((columns, LABEL_ROWS, edge), BF16)
        return pl.pallas_call(
            kernel,
            out_shape=(tile_out, label_out) if keep else tile_out,
            in_specs=[smem()] * 6 + [vmem()] * (len(amp_parts) + 2),
            out_specs=(vmem(), vmem()) if keep else vmem(),
            scratch_shapes=[
                pltpu.VMEM((amp_total, edge, edge), BF16),
                pltpu.SMEM((columns,), jnp.int32),
                pltpu.SMEM((columns,), jnp.int32),
            ],
            cost_estimate=pl.CostEstimate(
                flops=columns * amp_index.shape[1] * 4 * edge**3, bytes_accessed=8 << 20, transcendentals=0
            ),
            compiler_params=pltpu.CompilerParams(vmem_limit_bytes=VMEM_BYTES),
            name="ladder_keep" if keep else "ladder_send",
        )(amp_index, left_index, right_index, dest_col, owner_slot, place, *amp_parts, integrals, flipped)

    sent = ladder(False)
    received = swap(sent, "layer")
    kept, labels = ladder(True)
    packed = jnp.concatenate([(kept + received).astype(BF16), labels], axis=1)
    near = lax.all_to_all(packed, "col", split_axis=0, concat_axis=0, tiled=True)
    far = swap(near, "layer")
    return pl.pallas_call(
        owner_kernel,
        out_shape=jax.ShapeDtypeStruct((OWN, edge, edge), F32),
        in_specs=[vmem(), vmem()],
        out_specs=vmem(),
        compiler_params=pltpu.CompilerParams(vmem_limit_bytes=VMEM_BYTES),
        name="owner_sum",
    )(near, far)


def solution(mesh):
    placed = (
        P(("row", "col"), None, None),
        P(("layer", "row", "col"), None, None),
        P(("layer", "row", "col"), None),
        P(("layer", "row", "col"), None),
        P(("layer", "row", "col"), None),
        P(("row", "col"), None),
        P(("row", "col")),
    )
    return jax.shard_map(
        shards, mesh=mesh, in_specs=placed, out_specs=P(("row", "col"), None, None), check_vma=False
    )
```

time: 291 us -> 58.5 us (0.20)
  matrix products: 130 us -> 0 us
  local copies, waits for them, and re-layouts: 81.8 us -> 2.69 us
  waiting for transfers between devices: 40.7 us -> 1.58 us
  Pallas kernels: 0 us -> 31.8 us
  between operations: 13.4 us -> 0.02 us
  blocking collectives: 5.63 us -> 16.6 us
  starting transfers between devices: 13.3 us -> 2.97 us
    dot_general x66 -> x0, matrix products: 130 us -> none  [the longest x48 68.2 us: select_tiles(): jnp.dot(onehot, stack_flat, preferred_element_type=jnp.float32)]
    while x80 -> x0, local copies, waits for them, and re-layouts: 41.7 us -> none
    pallas_call x0 -> x4, Pallas kernels: none -> 31.8 us  [the longest x2 23.1 us: ladder(): pl.pallas_call(kernel, out_shape=(tile_out, label_out) if keep else tile_...]
    eq x33 -> x0, local copies, waits for them, and re-layouts: 26.4 us -> none  [the longest x32 26.3 us: select_tiles(): picks[:, None] == jnp.arange(count, dtype=jnp.int32)[None, :]]
    all_to_all x2 -> x0, waiting for transfers between devices: 23 us -> none  [the longest x1 23 us: shards(): lax.all_to_all(buffer, 'col', split_axis=0, concat_axis=0, tiled=True)]
    psum x1 -> x0, waiting for transfers between devices: 17.7 us -> none  [shards(): owned_tiles = lax.psum(owned_tiles, 'layer')]
    all_to_all x0 -> x1, blocking collectives: none -> 16.6 us  [shards(): lax.all_to_all(packed, 'col', split_axis=0, concat_axis=0, tiled=True)]
    all_to_all x2 -> x0, starting transfers between devices: 13.2 us -> none  [the longest x1 7.25 us: shards(): lax.all_to_all(labels, 'col', split_axis=0, concat_axis=0, tiled=True)]
  transfers between devices with their start and end apart: 3 -> 3, of which waited for: 2 -> 1; matrix products, arithmetic and copies ran while one was open for 71% -> 3% of each run, Pallas kernels for 0% -> 30%
where the time goes in v1:
time: 58.5 us; the launch traced here: 58.2 us
  Pallas kernels  31.8 us (54%)
  blocking collectives  16.6 us (28%)
  starting transfers between devices  2.97 us (5%)
  local copies, waits for them, and re-layouts  2.69 us (5%)
  other arithmetic  2.46 us (4%)
  waiting for transfers between devices  1.58 us (3%)
    pallas_call x2, Pallas kernels, ladder(): pl.pallas_call(kernel, out_shape=(tile_out, label_out) if keep else tile_...  23.1 us
    all_to_all x1, blocking collectives, shards(): lax.all_to_all(packed, 'col', split_axis=0, concat_axis=0, tiled=True)  16.6 us
    pallas_call x1, Pallas kernels, flip_tiles(): pl.pallas_call(transpose_kernel, out_shape=jax.ShapeDtypeStruct(integrals...  6.08 us
    ppermute x3, starting transfers between devices, swap(): return lax.ppermute(array, axis, [(i, i ^ 1) for i in range(size)])  2.97 us
    unnamed x7, local copies, waits for them, and re-layouts  2.69 us
    pallas_call x1, Pallas kernels, shards(): pl.pallas_call(owner_kernel, out_shape=jax.ShapeDtypeStruct((OWN, edge, e...  2.62 us
    ppermute x3, waiting for transfers between devices, swap(): return lax.ppermute(array, axis, [(i, i ^ 1) for i in range(size)])  1.58 us
  transfers between devices with their start and end apart: 3, of which 1 were waited for; matrix products, arithmetic and copies ran while one was open for 3% of the time, Pallas kernels for 30%

profile of v1, /device:TPU:0, one launch (start us, length us, event | category | flops | bytes accessed | tf_op | source)
XLA Modules:
  0.0 58.2 jit_solution(9714397768407686682)
XLA Ops:
  0.0 3.0 %collective-permute-start = (bf16[4,128,128]{2,1,0:T(8,128)(2,1)}, bf16[4,128,128]{2,1,0:T(8,128)(2,1)S(1)}, u32[]{:S(2)}, u32[]{:S(2)}) collective-permute-start(bf16[4,128,128]{2,1,0:T(8,128)(2,1)} %refs_6_.3), channel_id=1, source_target_pairs={{0,8},{8,0},{1,9},{9,1},{2,10},{10,2},{3,11},{11,3},{4,12},{12,4},... | collective-permute-start | bytes 393224 | tf_op jit(solution)/shard_map/ppermute | solution.py:128
  3.0 1.3 %copy.8.refs_3_ = s32[16,1]{1,0:T(8,128)} copy(s32[16,1]{0,1:T(1,128)} %param.12) | data formatting | bytes 128 | tf_op args[5]
  4.3 6.1 %flip_tiles.1.refs_9_ = bf16[128,128,128]{2,1,0:T(8,128)(2,1)} custom-call(bf16[128,128,128]{2,1,0:T(8,128)(2,1)} %refs_8_.3), custom_call_target="tpu_custom_call" | custom-call | tf_op jit(solution)/shard_map/flip_tiles/pallas_call | solution.py:39
  10.4 0.6 pad_add_fusion.refs_5_
  11.0 0.0 collective-permute-done.refs_7_
  11.0 0.0 copy-start.2
  11.0 0.6 %copy-done.2 = bf16[4,128,128]{2,1,0:T(8,128)(2,1)} copy-done((bf16[4,128,128]{2,1,0:T(8,128)(2,1)}, bf16[4,128,128]{2,1,0:T(8,128)(2,1)S(1)}, u32[]{:S(2)}) %copy-start.2) | copy-done | bytes 131096
  11.6 11.6 %ladder_send.1 = f32[8,128,128]{2,1,0:T(8,128)} custom-call(s32[16,48]{1,0:T(8,128)} %refs_0_.3, s32[16,48]{1,0:T(8,128)} %refs_1_.3, s32[16,48]{1,0:T(8,128)} %refs_2_.3, s32[16,1]{1,0:T(8,128)} %copy.8.refs_3_, s32[16]{0:T(128)} %refs_4_.3, s32[2]{0:T(128)} %pad_add_fusion.refs_5_, bf16[4,128,128]{2,1,0:T(8,128)(2,1)} %refs_6_.3, ...), custom_call_target="tpu_custom_call" | custom-call | flops 3221225472 | bytes 8388608 | tf_op jit(solution)/shard_map/ladder_send/pallas_call | solution.py:152
  23.2 0.0 collective-permute-start.1
  23.2 11.6 %ladder_keep.1 = (f32[8,128,128]{2,1,0:T(8,128)}, bf16[8,16,128]{2,1,0:T(8,128)(2,1)}) custom-call(s32[16,48]{1,0:T(8,128)} %refs_0_.3, s32[16,48]{1,0:T(8,128)} %refs_1_.3, s32[16,48]{1,0:T(8,128)} %refs_2_.3, s32[16,1]{1,0:T(8,128)} %copy.8.refs_3_, s32[16]{0:T(128)} %refs_4_.3, s32[2]{0:T(128)} %pad_add_fusion.refs_5_, bf16[4,128,128]{2,1,0:T(8,128)(2,1)} %refs_6_.3, ...), custom_call_target="tpu_custom_call" | custom-call | flops 3221225472 | bytes 8388608 | tf_op jit(solution)/shard_map/ladder_keep/pallas_call | solution.py:152
  34.7 0.0 collective-permute-done.1
  34.7 1.1 %add_convert_fusion = bf16[8,128,128]{2,1,0:T(8,128)(2,1)S(1)} fusion(f32[8,128,128]{2,1,0:T(8,128)} %get-tuple-element.7, f32[8,128,128]{2,1,0:T(8,128)S(1)} %collective-permute-done.1), kind=kLoop, calls=%fused_computation | loop fusion | flops 262144 | bytes 1310720 | tf_op jit(solution)/shard_map/convert_element_type | solution.py:172
  35.8 0.8 %pad_maximum_fusion = bf16[8,144,128]{2,1,0:T(8,128)(2,1)S(1)} fusion(bf16[8,16,128]{2,1,0:T(8,128)(2,1)} %get-tuple-element.8, bf16[8,128,128]{2,1,0:T(8,128)(2,1)S(1)} %add_convert_fusion), kind=kLoop, calls=%fused_computation.1 | loop fusion | flops 589824 | bytes 589824 | tf_op jit(solution)/shard_map/concatenate | solution.py:172
  36.6 16.6 %all_to_all.5.near = bf16[8,144,128]{2,1,0:T(8,128)(2,1)S(1)} all-to-all(bf16[8,144,128]{2,1,0:T(8,128)(2,1)S(1)} %pad_maximum_fusion), channel_id=1, replica_groups=mesh['layer'=2,'row'=2,'col'=8] {'col'}, dimensions={0} | all-to-all | bytes 589824 | tf_op jit(solution)/shard_map/all_to_all | solution.py:173
  53.2 0.0 copy-start
  53.2 0.0 collective-permute-start.2
  53.2 1.6 %collective-permute-done.2.far = bf16[8,144,128]{2,1,0:T(8,128)(2,1)S(1)} collective-permute-done((bf16[8,144,128]{2,1,0:T(8,128)(2,1)S(1)}, bf16[8,144,128]{2,1,0:T(8,128)(2,1)S(1)}, u32[]{:S(2)}, u32[]{:S(2)}) %collective-permute-start.2) | collective-permute-done | bytes 294944 | tf_op jit(solution)/shard_map/ppermute | solution.py:128
  54.8 0.0 copy-done
  54.8 0.0 copy-start.1
  54.8 0.7 %copy-done.1 = bf16[8,144,128]{2,1,0:T(8,128)(2,1)} copy-done((bf16[8,144,128]{2,1,0:T(8,128)(2,1)}, bf16[8,144,128]{2,1,0:T(8,128)(2,1)S(1)}, u32[]{:S(2)}) %copy-start.1) | copy-done | bytes 294936
  55.5 2.6 %owner_sum.1 = f32[8,128,128]{2,1,0:T(8,128)} custom-call(bf16[8,144,128]{2,1,0:T(8,128)(2,1)} %copy-done, bf16[8,144,128]{2,1,0:T(8,128)(2,1)} %copy-done.1), custom_call_target="tpu_custom_call" | custom-call | tf_op jit(solution)/shard_map/owner_sum/pallas_call | solution.py:175
Async XLA Ops:
  0.0 11.0 %collective-permute-start = (bf16[4,128,128]{2,1,0:T(8,128)(2,1)}, bf16[4,128,128]{2,1,0:T(8,128)(2,1)S(1)}, u32[]{:S(2)}, u32[]{:S(2)}) collective-permute-start(bf16[4,128,128]{2,1,0:T(8,128)(2,1)} %refs_6_.3), channel_id=1, source_target_pairs={{0,8},{8,0},{1,9},{9,1},{2,10},{10,2},{3,11},{11,3},{4,12},{12,4},... | collective-permute-start | bytes 393224 | tf_op jit(solution)/shard_map/ppermute | solution.py:128
  11.0 0.6 %copy-start.2 = (bf16[4,128,128]{2,1,0:T(8,128)(2,1)}, bf16[4,128,128]{2,1,0:T(8,128)(2,1)S(1)}, u32[]{:S(2)}) copy-start(bf16[4,128,128]{2,1,0:T(8,128)(2,1)S(1)} %collective-permute-done.refs_7_) | copy-start | bytes 393220
  23.2 11.6 %collective-permute-start.1 = (f32[8,128,128]{2,1,0:T(8,128)}, f32[8,128,128]{2,1,0:T(8,128)S(1)}, u32[]{:S(2)}, u32[]{:S(2)}) collective-permute-start(f32[8,128,128]{2,1,0:T(8,128)} %ladder_send.1), channel_id=1, source_target_pairs={{0,16},{16,0},{1,17},{17,1},{2,18},{18,2},{3,19},{19,3},{4,20},{20... | collective-permute-start | bytes 1572872 | tf_op jit(solution)/shard_map/ppermute | solution.py:128
  53.2 1.6 %copy-start = (bf16[8,144,128]{2,1,0:T(8,128)(2,1)}, bf16[8,144,128]{2,1,0:T(8,128)(2,1)S(1)}, u32[]{:S(2)}) copy-start(bf16[8,144,128]{2,1,0:T(8,128)(2,1)S(1)} %all_to_all.5.near) | copy-start | bytes 884740
  53.2 1.6 %collective-permute-start.2 = (bf16[8,144,128]{2,1,0:T(8,128)(2,1)S(1)}, bf16[8,144,128]{2,1,0:T(8,128)(2,1)S(1)}, u32[]{:S(2)}, u32[]{:S(2)}) collective-permute-start(bf16[8,144,128]{2,1,0:T(8,128)(2,1)S(1)} %all_to_all.5.near), channel_id=1, source_target_pairs={{0,16},{16,0},{1,17},{17,1},{2,18},{18,2},{3,19},{19,3},{4,20},{20... | collective-permute-start | bytes 884744 | tf_op jit(solution)/shard_map/ppermute | solution.py:128
  54.8 0.7 %copy-start.1 = (bf16[8,144,128]{2,1,0:T(8,128)(2,1)}, bf16[8,144,128]{2,1,0:T(8,128)(2,1)S(1)}, u32[]{:S(2)}) copy-start(bf16[8,144,128]{2,1,0:T(8,128)(2,1)S(1)} %collective-permute-done.2.far) | copy-start | bytes 884740

commit v2 on v1

--- a/solution.py
+++ b/solution.py
@@ -12,7 +12,7 @@
 LABEL_ROWS = 16
 F32 = jnp.float32
 BF16 = jnp.bfloat16
-VMEM_BYTES = 56 << 20
+VMEM_BYTES = 24 << 20
 
 
 def smem():
@@ -23,32 +23,52 @@
     return pl.BlockSpec(memory_space=pltpu.VMEM)
 
 
-def transpose_kernel(tiles, flipped):
+def held(shape, dtype):
+    return pltpu.VMEM(shape, dtype)
+
+
+def in_vmem(array):
+    return pltpu.with_memory_space_constraint(array, pltpu.VMEM)
+
+
+def prepare_kernel(source, tiles, flipped, arrived):
     count = tiles.shape[0]
-    step = 8
-
-    def body(i, carry):
-        for j in range(step):
-            flipped[i * step + j] = tiles[i * step + j].T
-        return carry
-
-    lax.fori_loop(0, count // step, body, 0)
-
-
-def flip_tiles(integrals):
+    chunks = arrived.shape[0]
+    step = count // chunks
+
+    def copy(i):
+        span = pl.ds(i * step, step)
+        return pltpu.make_async_copy(source.at[span], tiles.at[span], arrived.at[i])
+
+    for i in range(chunks):
+        copy(i).start()
+    for i in range(chunks):
+        copy(i).wait()
+
+        def body(j, carry):
+            for u in range(4):
+                flipped[i * step + j * 4 + u] = tiles[i * step + j * 4 + u].T
+            return carry
+
+        lax.fori_loop(0, step // 4, body, 0)
+
+
+def prepare(integrals):
+    shape = integrals.shape
     return pl.pallas_call(
-        transpose_kernel,
-        out_shape=jax.ShapeDtypeStruct(integrals.shape, integrals.dtype),
-        in_specs=[vmem()],
-        out_specs=vmem(),
+        prepare_kernel,
+        out_shape=(held(shape, BF16), held(shape, BF16)),
+        in_specs=[pl.BlockSpec(memory_space=pltpu.HBM)],
+        out_specs=(vmem(), vmem()),
+        scratch_shapes=[pltpu.SemaphoreType.DMA((8,))],
         compiler_params=pltpu.CompilerParams(vmem_limit_bytes=VMEM_BYTES),
-        name="flip_tiles",
-    )(integrals)
+        name="load_and_flip",
+    )(pltpu.with_memory_space_constraint(integrals, pltpu.HBM))
 
 
 def ladder_kernel(
-    columns, unroll, rank_of_layer, amp_ids, left_ids, right_ids, dest, labels, place,
-    own_amp, other_amp, tiles, flipped, out, *rest,
+    columns, unroll, rank_of_layer, amp_ids, left_ids, right_ids, dest, labels, own_amp, other_amp,
+    tiles, flipped, out, *rest,
 ):
     if len(rest) == 4:
         label_out, amps, slot_of, seen = rest
@@ -57,8 +77,8 @@
         amps, slot_of, seen = rest
     slot_count, terms = amp_ids.shape
     amp_dev = own_amp.shape[0]
-    layer = place[0]
-    row = place[1]
+    layer = lax.axis_index("layer")
+    row = lax.axis_index("row")
     rank = layer if rank_of_layer else 1 - layer
     if other_amp is None:
         amps[...] = own_amp[...]
@@ -70,7 +90,7 @@
         seen[d] = 0
 
     def scan(k, carry):
-        d = dest[k, 0]
+        d = dest[k]
         count = seen[d]
         seen[d] = count + 1
 
@@ -123,6 +143,13 @@
             out[s, rows, :] = totals[s]
 
 
+def merge_kernel(kept, received, labels, packed):
+    edge = kept.shape[1]
+    for c in range(kept.shape[0]):
+        packed[c, :edge] = (kept[c] + received[c]).astype(BF16)
+        packed[c, edge:] = labels[c]
+
+
 def swap(array, axis):
     size = lax.axis_size(axis)
     return lax.ppermute(array, axis, [(i, i ^ 1) for i in range(size)])
@@ -137,22 +164,23 @@
     else:
         amp_parts = (lax.all_gather(amplitudes, "row", axis=0, tiled=True),)
     amp_total = rows * amplitudes.shape[0]
-    flipped = flip_tiles(integrals)
-    place = jnp.stack([lax.axis_index("layer"), lax.axis_index("row")]).astype(jnp.int32)
+    tiles, flipped = prepare(integrals)
+    params = pltpu.CompilerParams(vmem_limit_bytes=VMEM_BYTES)
+    target = dest_col.reshape(-1)
 
     def ladder(keep):
         def kernel(*refs):
-            head, tail = refs[:7], refs[7:]
+            head, tail = refs[:6], refs[6:]
             if rows != 2:
                 tail = (None,) + tail
             return ladder_kernel(columns, 4, keep, *head, *tail)
 
-        tile_out = jax.ShapeDtypeStruct((columns, edge, edge), F32)
-        label_out = jax.ShapeDtypeStruct((columns, LABEL_ROWS, edge), BF16)
+        tile_out = held((columns, edge, edge), F32)
+        label_out = held((columns, LABEL_ROWS, edge), BF16)
         return pl.pallas_call(
             kernel,
             out_shape=(tile_out, label_out) if keep else tile_out,
-            in_specs=[smem()] * 6 + [vmem()] * (len(amp_parts) + 2),
+            in_specs=[smem()] * 5 + [vmem()] * (len(amp_parts) + 2),
             out_specs=(vmem(), vmem()) if keep else vmem(),
             scratch_shapes=[
                 pltpu.VMEM((amp_total, edge, edge), BF16),
@@ -160,16 +188,26 @@
                 pltpu.SMEM((columns,), jnp.int32),
             ],
             cost_estimate=pl.CostEstimate(
-                flops=columns * amp_index.shape[1] * 4 * edge**3, bytes_accessed=8 << 20, transcendentals=0
+                flops=columns * amp_index.shape[1] * 4 * edge**3, bytes_accessed=1 << 20, transcendentals=0
             ),
-            compiler_params=pltpu.CompilerParams(vmem_limit_bytes=VMEM_BYTES),
+            compiler_params=params,
             name="ladder_keep" if keep else "ladder_send",
-        )(amp_index, left_index, right_index, dest_col, owner_slot, place, *amp_parts, integrals, flipped)
+        )(
+            amp_index, left_index, right_index, target, owner_slot,
+            *[in_vmem(part) for part in amp_parts], in_vmem(tiles), in_vmem(flipped),
+        )
 
     sent = ladder(False)
     received = swap(sent, "layer")
     kept, labels = ladder(True)
-    packed = jnp.concatenate([(kept + received).astype(BF16), labels], axis=1)
+    packed = pl.pallas_call(
+        merge_kernel,
+        out_shape=held((columns, edge + LABEL_ROWS, edge), BF16),
+        in_specs=[vmem()] * 3,
+        out_specs=vmem(),
+        compiler_params=params,
+        name="merge_layers",
+    )(in_vmem(kept), in_vmem(received), in_vmem(labels))
     near = lax.all_to_all(packed, "col", split_axis=0, concat_axis=0, tiled=True)
     far = swap(near, "layer")
     return pl.pallas_call(
@@ -177,9 +215,9 @@
         out_shape=jax.ShapeDtypeStruct((OWN, edge, edge), F32),
         in_specs=[vmem(), vmem()],
         out_specs=vmem(),
-        compiler_params=pltpu.CompilerParams(vmem_limit_bytes=VMEM_BYTES),
+        compiler_params=params,
         name="owner_sum",
-    )(near, far)
+    )(in_vmem(near), in_vmem(far))
 
 
 def solution(mesh):

time: 58.5 us -> 43.4 us (0.74)
  Pallas kernels: 31.8 us -> 21.8 us
  local copies, waits for them, and re-layouts: 2.69 us -> 0.02 us
  other arithmetic: 2.46 us -> 0 us
    pallas_call x2, Pallas kernels: 23.1 us -> 16.2 us  [ladder(): pl.pallas_call(kernel, out_shape=(tile_out, label_out) if keep else tile_...]
    unnamed x7 -> x12, local copies, waits for them, and re-layouts: 2.69 us -> 0.02 us
    pallas_call x1 -> x2, Pallas kernels: 6.08 us -> 3.99 us  [the longest x1 3.94 us: prepare(): pl.pallas_call(prepare_kernel, out_shape=(held(shape, BF16), held(shape,...]
    convert_element_type x1 -> x0, other arithmetic: 1.1 us -> none  [shards(): packed = jnp.concatenate([(kept + received).astype(BF16), labels], axis=1)]
    pallas_call x1, Pallas kernels: 2.62 us -> 1.58 us  [shards(): pl.pallas_call(owner_kernel, out_shape=jax.ShapeDtypeStruct((OWN, edge, e...]
    concatenate x1 -> x0, other arithmetic: 0.78 us -> none  [shards(): packed = jnp.concatenate([(kept + received).astype(BF16), labels], axis=1)]
  transfers between devices with their start and end apart: 3 -> 3, of which waited for: 1 -> 1; matrix products, arithmetic and copies ran while one was open for 3% -> 0% of each run, Pallas kernels for 30% -> 28%
where the time goes in v2:
time: 43.4 us; the launch traced here: 43.2 us
  Pallas kernels  21.8 us (50%)
  blocking collectives  16.6 us (38%)
  starting transfers between devices  3.12 us (7%)
  waiting for transfers between devices  1.58 us (4%)
    all_to_all x1, blocking collectives, shards(): lax.all_to_all(packed, 'col', split_axis=0, concat_axis=0, tiled=True)  16.6 us
    pallas_call x2, Pallas kernels, ladder(): pl.pallas_call(kernel, out_shape=(tile_out, label_out) if keep else tile_...  16.2 us
    pallas_call x1, Pallas kernels, prepare(): pl.pallas_call(prepare_kernel, out_shape=(held(shape, BF16), held(shape,...  3.94 us
    ppermute x3, starting transfers between devices, swap(): return lax.ppermute(array, axis, [(i, i ^ 1) for i in range(size)])  3.12 us
    ppermute x3, waiting for transfers between devices, swap(): return lax.ppermute(array, axis, [(i, i ^ 1) for i in range(size)])  1.58 us
    pallas_call x1, Pallas kernels, shards(): pl.pallas_call(owner_kernel, out_shape=jax.ShapeDtypeStruct((OWN, edge, e...  1.58 us
  transfers between devices with their start and end apart: 3, of which 1 were waited for; matrix products, arithmetic and copies ran while one was open for 0% of the time, Pallas kernels for 28%

profile of v2, /device:TPU:0, one launch (start us, length us, event | category | flops | bytes accessed | tf_op | source)
XLA Modules:
  0.0 43.2 jit_solution(14292167942818368348)
XLA Ops:
  0.0 0.0 copy-start
  0.0 0.0 copy-start.4
  0.0 0.0 copy-start.2
  0.0 0.0 copy-start.3
  0.0 0.0 copy-start.5
  0.0 0.0 copy-start.1
  0.0 3.0 %collective-permute-start = (bf16[4,128,128]{2,1,0:T(8,128)(2,1)}, bf16[4,128,128]{2,1,0:T(8,128)(2,1)S(1)}, u32[]{:S(2)}, u32[]{:S(2)}) collective-permute-start(bf16[4,128,128]{2,1,0:T(8,128)(2,1)} %refs_5_.3), channel_id=1, source_target_pairs={{0,8},{8,0},{1,9},{9,1},{2,10},{10,2},{3,11},{11,3},{4,12},{12,4},... | collective-permute-start | bytes 393224 | tf_op jit(solution)/shard_map/ppermute | solution.py:155
  3.1 3.9 %load_and_flip.1 = (bf16[128,128,128]{2,1,0:T(8,128)(2,1)S(1)}, bf16[128,128,128]{2,1,0:T(8,128)(2,1)S(1)}) custom-call(bf16[128,128,128]{2,1,0:T(8,128)(2,1)} %source.1), custom_call_target="tpu_custom_call" | custom-call | tf_op jit(solution)/shard_map/load_and_flip/pallas_call | solution.py:58
  7.0 0.0 collective-permute-done.refs_6_
  7.0 0.0 copy-done
  7.0 0.0 copy-done.4
  7.0 0.0 copy-done.2
  7.1 0.0 copy-done.3
  7.1 0.0 copy-done.5
  7.1 0.0 copy-done.1
  7.1 8.1 %ladder_send.1 = f32[8,128,128]{2,1,0:T(8,128)S(1)} custom-call(s32[16,48]{1,0:T(8,128)S(1)} %copy-done.1, s32[16,48]{1,0:T(8,128)S(1)} %copy-done.2, s32[16,48]{1,0:T(8,128)S(1)} %copy-done.3, s32[16]{0:T(128)S(1)} %bitcast.1, s32[16]{0:T(128)S(1)} %copy-done.5, bf16[4,128,128]{2,1,0:T(8,128)(2,1)S(1)} %copy-done, ...), custom_call_target="tpu_custom_call" | custom-call | flops 3221225472 | bytes 1048576 | tf_op jit(solution)/shard_map/ladder_send/pallas_call | solution.py:180
  15.2 0.1 collective-permute-start.1
  15.3 8.1 %ladder_keep.1 = (f32[8,128,128]{2,1,0:T(8,128)S(1)}, bf16[8,16,128]{2,1,0:T(8,128)(2,1)S(1)}) custom-call(s32[16,48]{1,0:T(8,128)S(1)} %copy-done.1, s32[16,48]{1,0:T(8,128)S(1)} %copy-done.2, s32[16,48]{1,0:T(8,128)S(1)} %copy-done.3, s32[16]{0:T(128)S(1)} %bitcast.2, s32[16]{0:T(128)S(1)} %copy-done.5, bf16[4,128,128]{2,1,0:T(8,128)(2,1)S(1)} %copy-done, ...), custom_call_target="tpu_custom_call" | custom-call | flops 3221225472 | bytes 1048576 | tf_op jit(solution)/shard_map/ladder_keep/pallas_call | solution.py:180
  23.4 0.0 collective-permute-done.1.received
  23.4 0.1 merge_layers.1
  23.4 16.6 %all_to_all.5.near = bf16[8,144,128]{2,1,0:T(8,128)(2,1)S(1)} all-to-all(bf16[8,144,128]{2,1,0:T(8,128)(2,1)S(1)} %merge_layers.1), channel_id=1, replica_groups=mesh['layer'=2,'row'=2,'col'=8] {'col'}, dimensions={0} | all-to-all | bytes 589824 | tf_op jit(solution)/shard_map/all_to_all | solution.py:211
  40.0 0.0 collective-permute-start.2
  40.0 1.6 %collective-permute-done.2.far = bf16[8,144,128]{2,1,0:T(8,128)(2,1)S(1)} collective-permute-done((bf16[8,144,128]{2,1,0:T(8,128)(2,1)S(1)}, bf16[8,144,128]{2,1,0:T(8,128)(2,1)S(1)}, u32[]{:S(2)}, u32[]{:S(2)}) %collective-permute-start.2) | collective-permute-done | bytes 294944 | tf_op jit(solution)/shard_map/ppermute | solution.py:155
  41.6 1.6 %owner_sum.1 = f32[8,128,128]{2,1,0:T(8,128)} custom-call(bf16[8,144,128]{2,1,0:T(8,128)(2,1)S(1)} %all_to_all.5.near, bf16[8,144,128]{2,1,0:T(8,128)(2,1)S(1)} %collective-permute-done.2.far), custom_call_target="tpu_custom_call" | custom-call | tf_op jit(solution)/shard_map/owner_sum/pallas_call | solution.py:213
Async XLA Ops:
  0.0 7.0 %copy-start = (bf16[4,128,128]{2,1,0:T(8,128)(2,1)S(1)}, bf16[4,128,128]{2,1,0:T(8,128)(2,1)}, u32[]{:S(2)}) copy-start(bf16[4,128,128]{2,1,0:T(8,128)(2,1)} %refs_5_.3) | copy-start | bytes 393220
  0.0 7.0 %copy-start.4 = (s32[16,1]{0,1:T(1,128)S(1)}, s32[16,1]{0,1:T(1,128)}, u32[]{:S(2)}) copy-start(s32[16,1]{0,1:T(1,128)} %param.12) | copy-start | bytes 196
  0.0 7.0 %copy-start.2 = (s32[16,48]{1,0:T(8,128)S(1)}, s32[16,48]{1,0:T(8,128)}, u32[]{:S(2)}) copy-start(s32[16,48]{1,0:T(8,128)} %refs_1_.3) | copy-start | bytes 9220
  0.0 7.1 %copy-start.3 = (s32[16,48]{1,0:T(8,128)S(1)}, s32[16,48]{1,0:T(8,128)}, u32[]{:S(2)}) copy-start(s32[16,48]{1,0:T(8,128)} %refs_2_.3) | copy-start | bytes 9220
  0.0 7.1 %copy-start.5 = (s32[16]{0:T(128)S(1)}, s32[16]{0:T(128)}, u32[]{:S(2)}) copy-start(s32[16]{0:T(128)} %refs_4_.3) | copy-start | bytes 196
  0.0 7.1 %copy-start.1 = (s32[16,48]{1,0:T(8,128)S(1)}, s32[16,48]{1,0:T(8,128)}, u32[]{:S(2)}) copy-start(s32[16,48]{1,0:T(8,128)} %refs_0_.3) | copy-start | bytes 9220
  0.0 7.0 %collective-permute-start = (bf16[4,128,128]{2,1,0:T(8,128)(2,1)}, bf16[4,128,128]{2,1,0:T(8,128)(2,1)S(1)}, u32[]{:S(2)}, u32[]{:S(2)}) collective-permute-start(bf16[4,128,128]{2,1,0:T(8,128)(2,1)} %refs_5_.3), channel_id=1, source_target_pairs={{0,8},{8,0},{1,9},{9,1},{2,10},{10,2},{3,11},{11,3},{4,12},{12,4},... | collective-permute-start | bytes 393224 | tf_op jit(solution)/shard_map/ppermute | solution.py:155
  15.2 8.2 %collective-permute-start.1 = (f32[8,128,128]{2,1,0:T(8,128)S(1)}, f32[8,128,128]{2,1,0:T(8,128)S(1)}, u32[]{:S(2)}, u32[]{:S(2)}) collective-permute-start(f32[8,128,128]{2,1,0:T(8,128)S(1)} %ladder_send.1), channel_id=1, source_target_pairs={{0,16},{16,0},{1,17},{17,1},{2,18},{18,2},{3,19},{19,3},{4,20},{20... | collective-permute-start | bytes 1572872 | tf_op jit(solution)/shard_map/ppermute | solution.py:155
  40.0 1.6 %collective-permute-start.2 = (bf16[8,144,128]{2,1,0:T(8,128)(2,1)S(1)}, bf16[8,144,128]{2,1,0:T(8,128)(2,1)S(1)}, u32[]{:S(2)}, u32[]{:S(2)}) collective-permute-start(bf16[8,144,128]{2,1,0:T(8,128)(2,1)S(1)} %all_to_all.5.near), channel_id=1, source_target_pairs={{0,16},{16,0},{1,17},{17,1},{2,18},{18,2},{3,19},{19,3},{4,20},{20... | collective-permute-start | bytes 884744 | tf_op jit(solution)/shard_map/ppermute | solution.py:155

commit v3 on v0

v3 whole, which is shorter than its diff:
```python
import functools

import jax
import jax.numpy as jnp
from jax import lax
from jax.experimental import pallas as pl
from jax.experimental.pallas import tpu as pltpu
from jax.sharding import PartitionSpec as P

OWN = 8
CAP = 2
LABEL_ROWS = 8
F32 = jnp.float32
BF16 = jnp.bfloat16
VMEM_BYTES = 24 << 20


def smem():
    return pl.BlockSpec(memory_space=pltpu.SMEM)


def vmem():
    return pl.BlockSpec(memory_space=pltpu.VMEM)


def held(shape, dtype):
    return pltpu.VMEM(shape, dtype)


def in_vmem(array):
    return pltpu.with_memory_space_constraint(array, pltpu.VMEM)


def params():
    return pltpu.CompilerParams(vmem_limit_bytes=VMEM_BYTES)


def exchange_rounds(columns):
    far = list(range(columns - 1, 3, -1))
    pairs = [(far[i], far[i + 1]) for i in range(0, len(far), 2)]
    return pairs + [(3, 0), (1, 2)]


def prepare_kernel(
    bits, source, amp_ids, left_ids, right_ids, dest, labels,
    tiles, flipped, table, label_blocks, packed, seen, arrived,
):
    count = tiles.shape[0]
    chunks = arrived.shape[0]
    step = count // chunks
    columns = label_blocks.shape[0]

    def copy(i):
        span = pl.ds(i * step, step)
        return pltpu.make_async_copy(source.at[span], tiles.at[span], arrived.at[i])

    for i in range(chunks):
        copy(i).start()

    packed[...] = (amp_ids[...] << (2 * bits)) | (left_ids[...] << bits) | right_ids[...]
    table[...] = jnp.zeros(table.shape, jnp.int32)
    label_blocks[...] = jnp.full(label_blocks.shape, OWN, F32)
    for d in range(columns):
        seen[d] = 0
    me = lax.axis_index("col")
    for k in range(packed.shape[0]):
        offset = dest[k] ^ me
        rank = seen[offset]
        seen[offset] = rank + 1
        table[pl.ds(offset * CAP + rank, 1), :] = packed[pl.ds(k, 1), :]
        spot = pl.ds(pl.multiple_of(rank * LABEL_ROWS, LABEL_ROWS), LABEL_ROWS)
        label_blocks[offset, spot, :] = jnp.full((LABEL_ROWS, label_blocks.shape[2]), labels[k].astype(F32))

    for i in range(chunks):
        copy(i).wait()
        for j in range(step):
            flipped[i * step + j] = tiles[i * step + j].T


def prepare(columns, bits, integrals, amp_index, left_index, right_index, target, owner_slot):
    shape = integrals.shape
    slots, terms = amp_index.shape
    return pl.pallas_call(
        functools.partial(prepare_kernel, bits),
        out_shape=(
            held(shape, BF16),
            held(shape, BF16),
            held((columns * CAP, terms), jnp.int32),
            held((columns, CAP * LABEL_ROWS, shape[2]), F32),
        ),
        in_specs=[pl.BlockSpec(memory_space=pltpu.HBM)] + [vmem()] * 3 + [smem()] * 2,
        out_specs=(vmem(),) * 4,
        scratch_shapes=[
            pltpu.VMEM((slots, terms), jnp.int32),
            pltpu.SMEM((columns,), jnp.int32),
            pltpu.SemaphoreType.DMA((8,)),
        ],
        compiler_params=params(),
        name="load_and_flip",
    )(
        pltpu.with_memory_space_constraint(integrals, pltpu.HBM),
        in_vmem(amp_index), in_vmem(left_index), in_vmem(right_index), target, owner_slot,
    )


def pick(pair, layer):
    return jnp.where(layer == 0, pair[0], pair[1])


def ladder_kernel(bits, keeps, sends, parts, waits, *refs):
    table = refs[0]
    amp_parts = refs[1 : 1 + parts]
    tiles, flipped = refs[1 + parts : 3 + parts]
    outs, amps = refs[3 + parts + waits : -1], refs[-1]
    terms = table.shape[1]
    layer = lax.axis_index("layer")
    amp_dev = amp_parts[0].shape[0]
    if parts == 1:
        amps[...] = amp_parts[0][...]
    else:
        row = lax.axis_index("row")
        amps[pl.ds(row * amp_dev, amp_dev)] = amp_parts[0][...]
        amps[pl.ds((1 - row) * amp_dev, amp_dev)] = amp_parts[1][...]
    mask = (1 << bits) - 1
    picked = [(outs[0], i, pick(pair, layer)) for i, pair in enumerate(keeps)]
    picked += [(outs[-1], i, pick(pair, 1 - layer)) for i, pair in enumerate(sends)]
    for out, i, offset in picked:
        for rank in range(CAP):
            slot = offset * CAP + rank
            lefts, middles = [], []
            for t in range(terms):
                word = table[slot, t]
                lefts.append(tiles[(word >> bits) & mask])
                middles.append(
                    jnp.dot(
                        amps[word >> (2 * bits)], flipped[word & mask], preferred_element_type=F32
                    ).astype(BF16)
                )
            out[i * CAP + rank] = jnp.dot(
                jnp.concatenate(lefts, axis=1),
                jnp.concatenate(middles, axis=0),
                preferred_element_type=F32,
            )


def merge_kernel(pair, kept, received, label_blocks, packed):
    edge = kept.shape[1]
    for rank in range(CAP):
        packed[rank * edge : (rank + 1) * edge] = (kept[rank] + received[rank]).astype(BF16)
    packed[CAP * edge :] = label_blocks[pick(pair, lax.axis_index("layer"))].astype(BF16)


def owner_kernel(count, *refs):
    packs, out = refs[:count], refs[-1]
    base = refs[count] if len(refs) == count + 2 else None
    edge = out.shape[1]
    height = 32
    for chunk in range(edge // height):
        rows = pl.ds(chunk * height, height)
        totals = [jnp.zeros((height, edge), F32) if base is None else base[s, rows, :] for s in range(OWN)]
        for pack in packs:
            marks = pack[CAP * edge : CAP * (edge + LABEL_ROWS), :].astype(F32)
            for rank in range(CAP):
                mark = marks[rank * LABEL_ROWS : (rank + 1) * LABEL_ROWS]
                mark = jnp.concatenate([mark] * (height // LABEL_ROWS), axis=0)
                tile = pack[pl.ds(rank * edge + chunk * height, height), :].astype(F32)
                for s in range(OWN):
                    totals[s] = totals[s] + jnp.where(mark == s, tile, 0.0)
        for s in range(OWN):
            out[s, rows, :] = totals[s]


def swap(array, axis):
    size = lax.axis_size(axis)
    return lax.ppermute(array, axis, [(i, i ^ 1) for i in range(size)])


def shards(amplitudes, integrals, amp_index, left_index, right_index, dest_col, owner_slot):
    columns = lax.axis_size("col")
    rows = lax.axis_size("row")
    edge = integrals.shape[1]
    bits = (integrals.shape[0] - 1).bit_length()
    if rows == 2:
        amp_parts = (amplitudes, swap(amplitudes, "row"))
    else:
        amp_parts = (lax.all_gather(amplitudes, "row", axis=0, tiled=True),)
    amp_total = rows * amplitudes.shape[0]
    tiles, flipped, table, label_blocks = prepare(
        columns, bits, integrals, amp_index, left_index, right_index, dest_col.reshape(-1), owner_slot
    )
    rounds = exchange_rounds(columns)

    def ladder(keeps, sends, after):
        groups = [len(group) * CAP for group in (keeps, sends) if group]
        return pl.pallas_call(
            functools.partial(ladder_kernel, bits, keeps, sends, len(amp_parts), len(after)),
            out_shape=tuple(held((slots, edge, edge), F32) for slots in groups),
            in_specs=[smem()] + [vmem()] * (len(amp_parts) + 2) + [pl.BlockSpec(memory_space=pl.ANY)] * len(after),
            out_specs=(vmem(),) * len(groups),
            scratch_shapes=[pltpu.VMEM((amp_total, edge, edge), BF16)],
            cost_estimate=pl.CostEstimate(
                flops=sum(groups) * table.shape[1] * 4 * edge**3, bytes_accessed=1 << 20, transcendentals=0
            ),
            compiler_params=params(),
            name="ladder",
        )(table, *[in_vmem(part) for part in amp_parts], in_vmem(tiles), in_vmem(flipped), *after)

    def merge(pair, kept, received):
        return pl.pallas_call(
            functools.partial(merge_kernel, pair),
            out_shape=held((CAP * (edge + LABEL_ROWS), edge), BF16),
            in_specs=[vmem()] * 3,
            out_specs=vmem(),
            compiler_params=params(),
            name="merge_layers",
        )(in_vmem(kept), in_vmem(received), in_vmem(label_blocks))

    def deliver(pair, pack):
        route = [
            (layer * columns + c, layer * columns + (c ^ pair[layer])) for layer in range(2) for c in range(columns)
        ]
        near = lax.ppermute(pack, ("layer", "col"), route)
        return near, swap(near, "layer")

    def owner_sum(packs, base, shape):
        extra = () if base is None else (base,)
        return pl.pallas_call(
            functools.partial(owner_kernel, len(packs)),
            out_shape=shape,
            in_specs=[vmem()] * (len(packs) + len(extra)),
            out_specs=vmem(),
            compiler_params=params(),
            name="owner_sum",
        )(*[in_vmem(pack) for pack in packs], *[in_vmem(array) for array in extra])

    packs = []
    after = []
    (sent,) = ladder([], rounds[:1], after)
    received = swap(sent, "layer")
    for i, pair in enumerate(rounds):
        nexts = rounds[i + 1 : i + 2]
        kept, *sent = ladder([pair], nexts, after)
        pack = merge(pair, kept, received)
        if nexts:
            received = swap(sent[0], "layer")
        after = [pack] + [both[0] for both in packs[-1:]]
        packs.append(deliver(pair, pack))
    early = [pack for both in packs[:-1] for pack in both]
    base = owner_sum(early, None, held((OWN, edge, edge), F32))
    return owner_sum(list(packs[-1]), base, jax.ShapeDtypeStruct((OWN, edge, edge), F32))


def solution(mesh):
    placed = (
        P(("row", "col"), None, None),
        P(("layer", "row", "col"), None, None),
        P(("layer", "row", "col"), None),
        P(("layer", "row", "col"), None),
        P(("layer", "row", "col"), None),
        P(("row", "col"), None),
        P(("row", "col")),
    )
    return jax.shard_map(
        shards, mesh=mesh, in_specs=placed, out_specs=P(("row", "col"), None, None), check_vma=False
    )
```

time: 291 us -> 43.4 us (0.15)
  matrix products: 130 us -> 0 us
  local copies, waits for them, and re-layouts: 81.8 us -> 3.4 us
  waiting for transfers between devices: 40.7 us -> 3.84 us
  Pallas kernels: 0 us -> 22.3 us
  between operations: 13.4 us -> 0.17 us
  blocking collectives: 5.63 us -> 0 us
    dot_general x66 -> x0, matrix products: 130 us -> none  [the longest x48 68.2 us: select_tiles(): jnp.dot(onehot, stack_flat, preferred_element_type=jnp.float32)]
    while x80 -> x0, local copies, waits for them, and re-layouts: 41.7 us -> none
    eq x33 -> x0, local copies, waits for them, and re-layouts: 26.4 us -> none  [the longest x32 26.3 us: select_tiles(): picks[:, None] == jnp.arange(count, dtype=jnp.int32)[None, :]]
    all_to_all x2 -> x0, waiting for transfers between devices: 23 us -> none  [the longest x1 23 us: shards(): lax.all_to_all(buffer, 'col', split_axis=0, concat_axis=0, tiled=True)]
    pallas_call x0 -> x12, Pallas kernels: none -> 22.3 us  [the longest x5 17.6 us: ladder(): pl.pallas_call(functools.partial(ladder_kernel, bits, keeps, sends, len(a...]
    psum x1 -> x0, waiting for transfers between devices: 17.7 us -> none  [shards(): owned_tiles = lax.psum(owned_tiles, 'layer')]
    ppermute x0 -> x13, starting transfers between devices: none -> 13.3 us  [the longest x4 8.58 us: deliver(): near = lax.ppermute(pack, ('layer', 'col'), route)]
    all_to_all x2 -> x0, starting transfers between devices: 13.2 us -> none  [the longest x1 7.25 us: shards(): lax.all_to_all(labels, 'col', split_axis=0, concat_axis=0, tiled=True)]
  transfers between devices with their start and end apart: 3 -> 13, of which waited for: 2 -> 3; matrix products, arithmetic and copies ran while one was open for 71% -> 0% of each run, Pallas kernels for 0% -> 44%
where the time goes in v3:
time: 43.4 us; the launch traced here: 43 us
  Pallas kernels  22.3 us (51%)
  starting transfers between devices  13.3 us (31%)
  waiting for transfers between devices  3.84 us (9%)
  local copies, waits for them, and re-layouts  3.4 us (8%)
    pallas_call x5, Pallas kernels, ladder(): pl.pallas_call(functools.partial(ladder_kernel, bits, keeps, sends, len(a...  17.6 us
    ppermute x4, starting transfers between devices, deliver(): near = lax.ppermute(pack, ('layer', 'col'), route)  8.58 us
    ppermute x9, starting transfers between devices, swap(): return lax.ppermute(array, axis, [(i, i ^ 1) for i in range(size)])  4.73 us
    unnamed x12, local copies, waits for them, and re-layouts  3.4 us
    pallas_call x1, Pallas kernels, prepare(): pl.pallas_call(functools.partial(prepare_kernel, bits), out_shape=(held(s...  3.18 us
    ppermute x4, waiting for transfers between devices, deliver(): near = lax.ppermute(pack, ('layer', 'col'), route)  3.06 us
    pallas_call x2, Pallas kernels, owner_sum(): pl.pallas_call(functools.partial(owner_kernel, len(packs)), out_shape=sha...  1.44 us
  transfers between devices with their start and end apart: 13, of which 3 were waited for; matrix products, arithmetic and copies ran while one was open for 0% of the time, Pallas kernels for 44%

profile of v3, /device:TPU:0, one launch (start us, length us, event | category | flops | bytes accessed | tf_op | source)
XLA Modules:
  0.0 43.0 jit_solution(12164667443147014745)
XLA Ops:
  0.0 0.0 copy-start
  0.0 3.0 %collective-permute-start = (bf16[4,128,128]{2,1,0:T(8,128)(2,1)}, bf16[4,128,128]{2,1,0:T(8,128)(2,1)S(1)}, u32[]{:S(2)}, u32[]{:S(2)}) collective-permute-start(bf16[4,128,128]{2,1,0:T(8,128)(2,1)} %refs_1_.9), channel_id=1, source_target_pairs={{0,8},{8,0},{1,9},{9,1},{2,10},{10,2},{3,11},{11,3},{4,12},{12,4},... | collective-permute-start | bytes 393224 | tf_op jit(solution)/shard_map/ppermute | solution.py:175
  3.0 0.0 copy-start.1
  3.0 0.7 %copy-done.1 = s32[16,48]{1,0:T(8,128)S(1)} copy-done((s32[16,48]{1,0:T(8,128)S(1)}, s32[16,48]{1,0:T(8,128)}, u32[]{:S(2)}) %copy-start.1) | copy-done | bytes 3096
  3.7 0.0 copy-start.2
  3.7 0.7 %copy-done.2 = s32[16,48]{1,0:T(8,128)S(1)} copy-done((s32[16,48]{1,0:T(8,128)S(1)}, s32[16,48]{1,0:T(8,128)}, u32[]{:S(2)}) %copy-start.2) | copy-done | bytes 3096
  4.4 0.0 copy-start.3
  4.4 0.7 %copy-done.3 = s32[16,48]{1,0:T(8,128)S(1)} copy-done((s32[16,48]{1,0:T(8,128)S(1)}, s32[16,48]{1,0:T(8,128)}, u32[]{:S(2)}) %copy-start.3) | copy-done | bytes 3096
  5.1 0.0 copy-start.4
  5.1 0.7 %copy-done.4 = s32[16,1]{0,1:T(1,128)S(1)} copy-done((s32[16,1]{0,1:T(1,128)S(1)}, s32[16,1]{0,1:T(1,128)}, u32[]{:S(2)}) %copy-start.4) | copy-done | bytes 88
  5.7 0.0 copy-start.5
  5.7 0.7 %copy-done.5 = s32[16]{0:T(128)S(1)} copy-done((s32[16]{0:T(128)S(1)}, s32[16]{0:T(128)}, u32[]{:S(2)}) %copy-start.5) | copy-done | bytes 88
  6.4 3.2 %load_and_flip.1 = (bf16[128,128,128]{2,1,0:T(8,128)(2,1)S(1)}, bf16[128,128,128]{2,1,0:T(8,128)(2,1)S(1)}, s32[16,48]{1,0:T(8,128)S(1)}, f32[8,16,128]{2,1,0:T(8,128)S(1)}) custom-call(bf16[128,128,128]{2,1,0:T(8,128)(2,1)} %source.1, s32[16,48]{1,0:T(8,128)S(1)} %copy-done.1, s32[16,48]{1,0:T(8,128)S(1)} %copy-done.2, s32[16,48]{1,0:T(8,128)S(1)} %copy-done.3, ...), custom_call_target="tpu_custom_call" | custom-call | tf_op jit(solution)/shard_map/load_and_flip/pallas_call | solution.py:83
  9.6 0.0 collective-permute-done.refs_2_
  9.6 0.0 copy-done
  9.6 2.5 %ladder.6 = f32[2,128,128]{2,1,0:T(8,128)S(1)} custom-call(s32[16,48]{1,0:T(8,128)S(1)} %get-tuple-element.15.refs_0_, bf16[4,128,128]{2,1,0:T(8,128)(2,1)S(1)} %copy-done, bf16[4,128,128]{2,1,0:T(8,128)(2,1)S(1)} %collective-permute-done.refs_2_, bf16[128,128,128]{2,1,0:T(8,128)(2,1)S(1)} %get-tuple-element.16.refs_3_, ...), custom_call_target="tpu_custom_call" | custom-call | flops 805306368 | bytes 1048576 | tf_op jit(solution)/shard_map/ladder/pallas_call | solution.py:195
  12.1 0.1 collective-permute-start.1
  12.2 4.1 %ladder.5 = (f32[2,128,128]{2,1,0:T(8,128)S(1)}, f32[2,128,128]{2,1,0:T(8,128)S(1)}) custom-call(s32[16,48]{1,0:T(8,128)S(1)} %get-tuple-element.15.refs_0_, bf16[4,128,128]{2,1,0:T(8,128)(2,1)S(1)} %copy-done, bf16[4,128,128]{2,1,0:T(8,128)(2,1)S(1)} %collective-permute-done.refs_2_, bf16[128,128,128]{2,1,0:T(8,128)(2,1)S(1)} %get-tuple-element.16.refs_3_, ...), custom_call_target="tpu_custom_call" | custom-call | flops 1610612736 | bytes 1048576 | tf_op jit(solution)/shard_map/ladder/pallas_call | solution.py:195
  16.3 0.6 %collective-permute-start.2 = (f32[2,128,128]{2,1,0:T(8,128)S(1)}, f32[2,128,128]{2,1,0:T(8,128)S(1)}, u32[]{:S(2)}, u32[]{:S(2)}) collective-permute-start(f32[2,128,128]{2,1,0:T(8,128)S(1)} %get-tuple-element.21), channel_id=1, source_target_pairs={{0,16},{16,0},{1,17},{17,1},{2,18},{18,2},{3,19},{19,3},{4,20},{20... | collective-permute-start | bytes 393224 | tf_op jit(solution)/shard_map/ppermute | solution.py:175
  16.9 0.0 collective-permute-done.1.received
  16.9 4.6 %collective-permute-start.3 = (bf16[272,128]{1,0:T(8,128)(2,1)S(1)}, bf16[272,128]{1,0:T(8,128)(2,1)S(1)}, u32[]{:S(2)}, u32[]{:S(2)}) collective-permute-start(bf16[272,128]{1,0:T(8,128)(2,1)S(1)} %merge_layers.4.refs_5_), channel_id=1, source_target_pairs={{0,7},{1,6},{2,5},{3,4},{4,3},{5,2},{6,1},{7,0},{16,22},{17,23},{1... | collective-permute-start | bytes 208904 | tf_op jit(solution)/shard_map/ppermute | solution.py:222
  21.5 4.1 %ladder.7 = (f32[2,128,128]{2,1,0:T(8,128)S(1)}, f32[2,128,128]{2,1,0:T(8,128)S(1)}) custom-call(s32[16,48]{1,0:T(8,128)S(1)} %get-tuple-element.15.refs_0_, bf16[4,128,128]{2,1,0:T(8,128)(2,1)S(1)} %copy-done, bf16[4,128,128]{2,1,0:T(8,128)(2,1)S(1)} %collective-permute-done.refs_2_, bf16[128,128,128]{2,1,0:T(8,128)(2,1)S(1)} %get-tuple-element.16.refs_3_, ...), custom_call_target="tpu_custom_call" | custom-call | flops 1610612736 | bytes 1048576 | tf_op jit(solution)/shard_map/ladder/pallas_call | solution.py:195
  25.6 0.1 collective-permute-start.4
  25.7 0.0 collective-permute-done.2.received
  25.7 0.1 collective-permute-start.5
  25.8 0.0 collective-permute-done.3.refs_6_.refs_0_
  25.8 4.3 %ladder.8 = (f32[2,128,128]{2,1,0:T(8,128)S(1)}, f32[2,128,128]{2,1,0:T(8,128)S(1)}) custom-call(s32[16,48]{1,0:T(8,128)S(1)} %get-tuple-element.15.refs_0_, bf16[4,128,128]{2,1,0:T(8,128)(2,1)S(1)} %copy-done, bf16[4,128,128]{2,1,0:T(8,128)(2,1)S(1)} %collective-permute-done.refs_2_, bf16[128,128,128]{2,1,0:T(8,128)(2,1)S(1)} %get-tuple-element.16.refs_3_, ...), custom_call_target="tpu_custom_call" | custom-call | flops 1610612736 | bytes 1048576 | tf_op jit(solution)/shard_map/ladder/pallas_call | solution.py:195
  30.2 0.6 %collective-permute-start.6 = (f32[2,128,128]{2,1,0:T(8,128)S(1)}, f32[2,128,128]{2,1,0:T(8,128)S(1)}, u32[]{:S(2)}, u32[]{:S(2)}) collective-permute-start(f32[2,128,128]{2,1,0:T(8,128)S(1)} %get-tuple-element.24), channel_id=1, source_target_pairs={{0,16},{16,0},{1,17},{17,1},{2,18},{18,2},{3,19},{19,3},{4,20},{20... | collective-permute-start | bytes 393224 | tf_op jit(solution)/shard_map/ppermute | solution.py:175
  30.7 0.0 collective-permute-done.4.received
  30.7 3.1 %collective-permute-start.11 = (bf16[272,128]{1,0:T(8,128)(2,1)S(1)}, bf16[272,128]{1,0:T(8,128)(2,1)S(1)}, u32[]{:S(2)}, u32[]{:S(2)}) collective-permute-start(bf16[272,128]{1,0:T(8,128)(2,1)S(1)} %merge_layers.6.refs_5_), channel_id=1, source_target_pairs={{0,3},{1,2},{2,1},{3,0},{4,7},{5,6},{6,5},{7,4},{16,16},{17,17},{1... | collective-permute-start | bytes 208904 | tf_op jit(solution)/shard_map/ppermute | solution.py:222
  33.9 0.0 collective-permute-done.5.refs_6_.refs_2_
  33.9 2.5 %ladder.9.kept = f32[2,128,128]{2,1,0:T(8,128)S(1)} custom-call(s32[16,48]{1,0:T(8,128)S(1)} %get-tuple-element.15.refs_0_, bf16[4,128,128]{2,1,0:T(8,128)(2,1)S(1)} %copy-done, bf16[4,128,128]{2,1,0:T(8,128)(2,1)S(1)} %collective-permute-done.refs_2_, bf16[128,128,128]{2,1,0:T(8,128)(2,1)S(1)} %get-tuple-element.16.refs_3_, ...), custom_call_target="tpu_custom_call" | custom-call | flops 805306368 | bytes 1048576 | tf_op jit(solution)/shard_map/ladder/pallas_call | solution.py:195
  36.4 0.0 collective-permute-done.6.received
  36.4 0.8 %collective-permute-start.7 = (bf16[272,128]{1,0:T(8,128)(2,1)S(1)}, bf16[272,128]{1,0:T(8,128)(2,1)S(1)}, u32[]{:S(2)}, u32[]{:S(2)}) collective-permute-start(bf16[272,128]{1,0:T(8,128)(2,1)S(1)} %merge_layers.7), channel_id=1, source_target_pairs={{0,1},{1,0},{2,3},{3,2},{4,5},{5,4},{6,7},{7,6},{16,18},{17,19},{1... | collective-permute-start | bytes 208904 | tf_op jit(solution)/shard_map/ppermute | solution.py:222
  37.2 0.0 collective-permute-start.9
  37.2 0.5 %collective-permute-start.10 = (bf16[272,128]{1,0:T(8,128)(2,1)S(1)}, bf16[272,128]{1,0:T(8,128)(2,1)S(1)}, u32[]{:S(2)}, u32[]{:S(2)}) collective-permute-start(bf16[272,128]{1,0:T(8,128)(2,1)S(1)} %collective-permute-done.5.refs_6_.refs_2_), channel_id=1, source_target_pairs={{0,16},{16,0},{1,17},{17,1},{2,18},{18,2},{3,19},{19,3},{4,20},{20... | collective-permute-start | bytes 208904 | tf_op jit(solution)/shard_map/ppermute | solution.py:175
  37.7 0.7 %collective-permute-done.11.refs_4_ = bf16[272,128]{1,0:T(8,128)(2,1)S(1)} collective-permute-done((bf16[272,128]{1,0:T(8,128)(2,1)S(1)}, bf16[272,128]{1,0:T(8,128)(2,1)S(1)}, u32[]{:S(2)}, u32[]{:S(2)}) %collective-permute-start.11) | collective-permute-done | bytes 69664 | tf_op jit(solution)/shard_map/ppermute | solution.py:222
  38.4 0.0 collective-permute-start.12
  38.4 2.3 %collective-permute-done.7.refs_0_ = bf16[272,128]{1,0:T(8,128)(2,1)S(1)} collective-permute-done((bf16[272,128]{1,0:T(8,128)(2,1)S(1)}, bf16[272,128]{1,0:T(8,128)(2,1)S(1)}, u32[]{:S(2)}, u32[]{:S(2)}) %collective-permute-start.7) | collective-permute-done | bytes 69664 | tf_op jit(solution)/shard_map/ppermute | solution.py:222
  40.8 0.0 collective-permute-start.8
  40.8 0.0 collective-permute-done.9.refs_1_
  40.8 0.0 collective-permute-done.10.refs_3_
  40.8 0.0 collective-permute-done.12.refs_5_
  40.8 0.5 %owner_sum.2.refs_2_ = f32[8,128,128]{2,1,0:T(8,128)S(1)} custom-call(bf16[272,128]{1,0:T(8,128)(2,1)S(1)} %collective-permute-done.3.refs_6_.refs_0_, bf16[272,128]{1,0:T(8,128)(2,1)S(1)} %collective-permute-done.9.refs_1_, bf16[272,128]{1,0:T(8,128)(2,1)S(1)} %collective-permute-done.5.refs_6_.refs_2_, ...), custom_call_target="tpu_custom_call" | custom-call | tf_op jit(solution)/shard_map/owner_sum/pallas_call | solution.py:227
  41.3 0.8 %collective-permute-done.8.refs_1_ = bf16[272,128]{1,0:T(8,128)(2,1)S(1)} collective-permute-done((bf16[272,128]{1,0:T(8,128)(2,1)S(1)}, bf16[272,128]{1,0:T(8,128)(2,1)S(1)}, u32[]{:S(2)}, u32[]{:S(2)}) %collective-permute-start.8) | collective-permute-done | bytes 69664 | tf_op jit(solution)/shard_map/ppermute | solution.py:175
  42.0 1.0 %owner_sum.3 = f32[8,128,128]{2,1,0:T(8,128)} custom-call(bf16[272,128]{1,0:T(8,128)(2,1)S(1)} %collective-permute-done.7.refs_0_, bf16[272,128]{1,0:T(8,128)(2,1)S(1)} %collective-permute-done.8.refs_1_, f32[8,128,128]{2,1,0:T(8,128)S(1)} %owner_sum.2.refs_2_), custom_call_target="tpu_custom_call" | custom-call | tf_op jit(solution)/shard_map/owner_sum/pallas_call | solution.py:227
  (4 shorter events, 0.1 us)
Async XLA Ops:
  0.0 9.6 %copy-start = (bf16[4,128,128]{2,1,0:T(8,128)(2,1)S(1)}, bf16[4,128,128]{2,1,0:T(8,128)(2,1)}, u32[]{:S(2)}) copy-start(bf16[4,128,128]{2,1,0:T(8,128)(2,1)} %refs_1_.9) | copy-start | bytes 393220
  0.0 9.6 %collective-permute-start = (bf16[4,128,128]{2,1,0:T(8,128)(2,1)}, bf16[4,128,128]{2,1,0:T(8,128)(2,1)S(1)}, u32[]{:S(2)}, u32[]{:S(2)}) collective-permute-start(bf16[4,128,128]{2,1,0:T(8,128)(2,1)} %refs_1_.9), channel_id=1, source_target_pairs={{0,8},{8,0},{1,9},{9,1},{2,10},{10,2},{3,11},{11,3},{4,12},{12,4},... | collective-permute-start | bytes 393224 | tf_op jit(solution)/shard_map/ppermute | solution.py:175
  3.0 0.7 %copy-start.1 = (s32[16,48]{1,0:T(8,128)S(1)}, s32[16,48]{1,0:T(8,128)}, u32[]{:S(2)}) copy-start(s32[16,48]{1,0:T(8,128)} %amp_ids.1) | copy-start | bytes 9220
  3.7 0.7 %copy-start.2 = (s32[16,48]{1,0:T(8,128)S(1)}, s32[16,48]{1,0:T(8,128)}, u32[]{:S(2)}) copy-start(s32[16,48]{1,0:T(8,128)} %left_ids.1) | copy-start | bytes 9220
  4.4 0.7 %copy-start.3 = (s32[16,48]{1,0:T(8,128)S(1)}, s32[16,48]{1,0:T(8,128)}, u32[]{:S(2)}) copy-start(s32[16,48]{1,0:T(8,128)} %right_ids.1) | copy-start | bytes 9220
  5.1 0.7 %copy-start.4 = (s32[16,1]{0,1:T(1,128)S(1)}, s32[16,1]{0,1:T(1,128)}, u32[]{:S(2)}) copy-start(s32[16,1]{0,1:T(1,128)} %param.12) | copy-start | bytes 196
  5.7 0.7 %copy-start.5 = (s32[16]{0:T(128)S(1)}, s32[16]{0:T(128)}, u32[]{:S(2)}) copy-start(s32[16]{0:T(128)} %labels.1) | copy-start | bytes 196
  12.1 4.8 %collective-permute-start.1 = (f32[2,128,128]{2,1,0:T(8,128)S(1)}, f32[2,128,128]{2,1,0:T(8,128)S(1)}, u32[]{:S(2)}, u32[]{:S(2)}) collective-permute-start(f32[2,128,128]{2,1,0:T(8,128)S(1)} %ladder.6), channel_id=1, source_target_pairs={{0,16},{16,0},{1,17},{17,1},{2,18},{18,2},{3,19},{19,3},{4,20},{20... | collective-permute-start | bytes 393224 | tf_op jit(solution)/shard_map/ppermute | solution.py:175
  16.3 9.4 %collective-permute-start.2 = (f32[2,128,128]{2,1,0:T(8,128)S(1)}, f32[2,128,128]{2,1,0:T(8,128)S(1)}, u32[]{:S(2)}, u32[]{:S(2)}) collective-permute-start(f32[2,128,128]{2,1,0:T(8,128)S(1)} %get-tuple-element.21), channel_id=1, source_target_pairs={{0,16},{16,0},{1,17},{17,1},{2,18},{18,2},{3,19},{19,3},{4,20},{20... | collective-permute-start | bytes 393224 | tf_op jit(solution)/shard_map/ppermute | solution.py:175
  16.9 8.9 %collective-permute-start.3 = (bf16[272,128]{1,0:T(8,128)(2,1)S(1)}, bf16[272,128]{1,0:T(8,128)(2,1)S(1)}, u32[]{:S(2)}, u32[]{:S(2)}) collective-permute-start(bf16[272,128]{1,0:T(8,128)(2,1)S(1)} %merge_layers.4.refs_5_), channel_id=1, source_target_pairs={{0,7},{1,6},{2,5},{3,4},{4,3},{5,2},{6,1},{7,0},{16,22},{17,23},{1... | collective-permute-start | bytes 208904 | tf_op jit(solution)/shard_map/ppermute | solution.py:222
  25.6 5.1 %collective-permute-start.4 = (f32[2,128,128]{2,1,0:T(8,128)S(1)}, f32[2,128,128]{2,1,0:T(8,128)S(1)}, u32[]{:S(2)}, u32[]{:S(2)}) collective-permute-start(f32[2,128,128]{2,1,0:T(8,128)S(1)} %get-tuple-element.23), channel_id=1, source_target_pairs={{0,16},{16,0},{1,17},{17,1},{2,18},{18,2},{3,19},{19,3},{4,20},{20... | collective-permute-start | bytes 393224 | tf_op jit(solution)/shard_map/ppermute | solution.py:175
  25.7 8.1 %collective-permute-start.5 = (bf16[272,128]{1,0:T(8,128)(2,1)S(1)}, bf16[272,128]{1,0:T(8,128)(2,1)S(1)}, u32[]{:S(2)}, u32[]{:S(2)}) collective-permute-start(bf16[272,128]{1,0:T(8,128)(2,1)S(1)} %merge_layers.5.refs_5_), channel_id=1, source_target_pairs={{0,5},{1,4},{2,7},{3,6},{4,1},{5,0},{6,3},{7,2},{16,20},{17,21},{1... | collective-permute-start | bytes 208904 | tf_op jit(solution)/shard_map/ppermute | solution.py:222
  30.2 6.2 %collective-permute-start.6 = (f32[2,128,128]{2,1,0:T(8,128)S(1)}, f32[2,128,128]{2,1,0:T(8,128)S(1)}, u32[]{:S(2)}, u32[]{:S(2)}) collective-permute-start(f32[2,128,128]{2,1,0:T(8,128)S(1)} %get-tuple-element.24), channel_id=1, source_target_pairs={{0,16},{16,0},{1,17},{17,1},{2,18},{18,2},{3,19},{19,3},{4,20},{20... | collective-permute-start | bytes 393224 | tf_op jit(solution)/shard_map/ppermute | solution.py:175
  30.7 7.7 %collective-permute-start.11 = (bf16[272,128]{1,0:T(8,128)(2,1)S(1)}, bf16[272,128]{1,0:T(8,128)(2,1)S(1)}, u32[]{:S(2)}, u32[]{:S(2)}) collective-permute-start(bf16[272,128]{1,0:T(8,128)(2,1)S(1)} %merge_layers.6.refs_5_), channel_id=1, source_target_pairs={{0,3},{1,2},{2,1},{3,0},{4,7},{5,6},{6,5},{7,4},{16,16},{17,17},{1... | collective-permute-start | bytes 208904 | tf_op jit(solution)/shard_map/ppermute | solution.py:222
  36.4 4.4 %collective-permute-start.7 = (bf16[272,128]{1,0:T(8,128)(2,1)S(1)}, bf16[272,128]{1,0:T(8,128)(2,1)S(1)}, u32[]{:S(2)}, u32[]{:S(2)}) collective-permute-start(bf16[272,128]{1,0:T(8,128)(2,1)S(1)} %merge_layers.7), channel_id=1, source_target_pairs={{0,1},{1,0},{2,3},{3,2},{4,5},{5,4},{6,7},{7,6},{16,18},{17,19},{1... | collective-permute-start | bytes 208904 | tf_op jit(solution)/shard_map/ppermute | solution.py:222
  37.2 3.6 %collective-permute-start.9 = (bf16[272,128]{1,0:T(8,128)(2,1)S(1)}, bf16[272,128]{1,0:T(8,128)(2,1)S(1)}, u32[]{:S(2)}, u32[]{:S(2)}) collective-permute-start(bf16[272,128]{1,0:T(8,128)(2,1)S(1)} %collective-permute-done.3.refs_6_.refs_0_), channel_id=1, source_target_pairs={{0,16},{16,0},{1,17},{17,1},{2,18},{18,2},{3,19},{19,3},{4,20},{20... | collective-permute-start | bytes 208904 | tf_op jit(solution)/shard_map/ppermute | solution.py:175
  37.2 3.6 %collective-permute-start.10 = (bf16[272,128]{1,0:T(8,128)(2,1)S(1)}, bf16[272,128]{1,0:T(8,128)(2,1)S(1)}, u32[]{:S(2)}, u32[]{:S(2)}) collective-permute-start(bf16[272,128]{1,0:T(8,128)(2,1)S(1)} %collective-permute-done.5.refs_6_.refs_2_), channel_id=1, source_target_pairs={{0,16},{16,0},{1,17},{17,1},{2,18},{18,2},{3,19},{19,3},{4,20},{20... | collective-permute-start | bytes 208904 | tf_op jit(solution)/shard_map/ppermute | solution.py:175
  38.4 2.3 %collective-permute-start.12 = (bf16[272,128]{1,0:T(8,128)(2,1)S(1)}, bf16[272,128]{1,0:T(8,128)(2,1)S(1)}, u32[]{:S(2)}, u32[]{:S(2)}) collective-permute-start(bf16[272,128]{1,0:T(8,128)(2,1)S(1)} %collective-permute-done.11.refs_4_), channel_id=1, source_target_pairs={{0,16},{16,0},{1,17},{17,1},{2,18},{18,2},{3,19},{19,3},{4,20},{20... | collective-permute-start | bytes 208904 | tf_op jit(solution)/shard_map/ppermute | solution.py:175
  40.8 1.3 %collective-permute-start.8 = (bf16[272,128]{1,0:T(8,128)(2,1)S(1)}, bf16[272,128]{1,0:T(8,128)(2,1)S(1)}, u32[]{:S(2)}, u32[]{:S(2)}) collective-permute-start(bf16[272,128]{1,0:T(8,128)(2,1)S(1)} %collective-permute-done.7.refs_0_), channel_id=1, source_target_pairs={{0,16},{16,0},{1,17},{17,1},{2,18},{18,2},{3,19},{19,3},{4,20},{20... | collective-permute-start | bytes 208904 | tf_op jit(solution)/shard_map/ppermute | solution.py:175

commit v4 on v3

--- a/solution.py
+++ b/solution.py
@@ -38,31 +38,42 @@
 def exchange_rounds(columns):
     far = list(range(columns - 1, 3, -1))
     pairs = [(far[i], far[i + 1]) for i in range(0, len(far), 2)]
-    return pairs + [(3, 0), (1, 2)]
+    return pairs + [(2, 3), (1, 0)]
 
 
 def prepare_kernel(
-    bits, source, amp_ids, left_ids, right_ids, dest, labels,
-    tiles, flipped, table, label_blocks, packed, seen, arrived,
+    bits, source, amp_ids, left_ids, right_ids, dest_in, labels_in,
+    tiles, flipped, table, label_blocks, ids, packed, dest, labels, seen, arrived, ready,
 ):
     count = tiles.shape[0]
     chunks = arrived.shape[0]
     step = count // chunks
     columns = label_blocks.shape[0]
+    small = [
+        pltpu.make_async_copy(src, dst, ready.at[i])
+        for i, (src, dst) in enumerate(
+            [(dest_in, dest), (labels_in, labels)]
+            + [(src, ids.at[i]) for i, src in enumerate((amp_ids, left_ids, right_ids))]
+        )
+    ]
 
     def copy(i):
         span = pl.ds(i * step, step)
         return pltpu.make_async_copy(source.at[span], tiles.at[span], arrived.at[i])
 
+    for transfer in small:
+        transfer.start()
     for i in range(chunks):
         copy(i).start()
 
-    packed[...] = (amp_ids[...] << (2 * bits)) | (left_ids[...] << bits) | right_ids[...]
     table[...] = jnp.zeros(table.shape, jnp.int32)
     label_blocks[...] = jnp.full(label_blocks.shape, OWN, F32)
     for d in range(columns):
         seen[d] = 0
     me = lax.axis_index("col")
+    for transfer in small:
+        transfer.wait()
+    packed[...] = (ids[0] << (2 * bits)) | (ids[1] << bits) | ids[2]
     for k in range(packed.shape[0]):
         offset = dest[k] ^ me
         rank = seen[offset]
@@ -80,6 +91,7 @@
 def prepare(columns, bits, integrals, amp_index, left_index, right_index, target, owner_slot):
     shape = integrals.shape
     slots, terms = amp_index.shape
+    operands = (integrals, amp_index, left_index, right_index, target, owner_slot)
     return pl.pallas_call(
         functools.partial(prepare_kernel, bits),
         out_shape=(
@@ -88,19 +100,20 @@
             held((columns * CAP, terms), jnp.int32),
             held((columns, CAP * LABEL_ROWS, shape[2]), F32),
         ),
-        in_specs=[pl.BlockSpec(memory_space=pltpu.HBM)] + [vmem()] * 3 + [smem()] * 2,
+        in_specs=[pl.BlockSpec(memory_space=pltpu.HBM)] * len(operands),
         out_specs=(vmem(),) * 4,
         scratch_shapes=[
+            pltpu.VMEM((3, slots, terms), jnp.int32),
             pltpu.VMEM((slots, terms), jnp.int32),
+            pltpu.SMEM((slots,), jnp.int32),
+            pltpu.SMEM((slots,), jnp.int32),
             pltpu.SMEM((columns,), jnp.int32),
             pltpu.SemaphoreType.DMA((8,)),
+            pltpu.SemaphoreType.DMA((5,)),
         ],
         compiler_params=params(),
         name="load_and_flip",
-    )(
-        pltpu.with_memory_space_constraint(integrals, pltpu.HBM),
-        in_vmem(amp_index), in_vmem(left_index), in_vmem(right_index), target, owner_slot,
-    )
+    )(*[pltpu.with_memory_space_constraint(array, pltpu.HBM) for array in operands])
 
 
 def pick(pair, layer):
@@ -143,11 +156,14 @@
             )
 
 
-def merge_kernel(pair, kept, received, label_blocks, packed):
+def merge_kernel(pairs, first, kept, received, label_blocks, *packs):
     edge = kept.shape[1]
-    for rank in range(CAP):
-        packed[rank * edge : (rank + 1) * edge] = (kept[rank] + received[rank]).astype(BF16)
-    packed[CAP * edge :] = label_blocks[pick(pair, lax.axis_index("layer"))].astype(BF16)
+    layer = lax.axis_index("layer")
+    for i, (pair, packed) in enumerate(zip(pairs, packs)):
+        for rank in range(CAP):
+            total = kept[i * CAP + rank] + received[(first + i) * CAP + rank]
+            packed[rank * edge : (rank + 1) * edge] = total.astype(BF16)
+        packed[CAP * edge :] = label_blocks[pick(pair, layer)].astype(BF16)
 
 
 def owner_kernel(count, *refs):
@@ -205,22 +221,24 @@
             name="ladder",
         )(table, *[in_vmem(part) for part in amp_parts], in_vmem(tiles), in_vmem(flipped), *after)
 
-    def merge(pair, kept, received):
+    def merge(pairs, first, kept, received):
+        pack = held((CAP * (edge + LABEL_ROWS), edge), BF16)
         return pl.pallas_call(
-            functools.partial(merge_kernel, pair),
-            out_shape=held((CAP * (edge + LABEL_ROWS), edge), BF16),
+            functools.partial(merge_kernel, pairs, first),
+            out_shape=(pack,) * len(pairs),
             in_specs=[vmem()] * 3,
-            out_specs=vmem(),
+            out_specs=(vmem(),) * len(pairs),
             compiler_params=params(),
             name="merge_layers",
         )(in_vmem(kept), in_vmem(received), in_vmem(label_blocks))
 
-    def deliver(pair, pack):
+    def send(pair, pack, cross):
         route = [
-            (layer * columns + c, layer * columns + (c ^ pair[layer])) for layer in range(2) for c in range(columns)
+            (layer * columns + c, (layer ^ cross) * columns + (c ^ pair[layer]))
+            for layer in range(2)
+            for c in range(columns)
         ]
-        near = lax.ppermute(pack, ("layer", "col"), route)
-        return near, swap(near, "layer")
+        return lax.ppermute(pack, ("layer", "col"), route)
 
     def owner_sum(packs, base, shape):
         extra = () if base is None else (base,)
@@ -229,25 +247,26 @@
             out_shape=shape,
             in_specs=[vmem()] * (len(packs) + len(extra)),
             out_specs=vmem(),
+            cost_estimate=pl.CostEstimate(flops=1 << 24, bytes_accessed=4 << 20, transcendentals=0),
             compiler_params=params(),
             name="owner_sum",
         )(*[in_vmem(pack) for pack in packs], *[in_vmem(array) for array in extra])
 
-    packs = []
-    after = []
-    (sent,) = ladder([], rounds[:1], after)
+    stages = [rounds[:-2], rounds[-2:]]
+    (sent,) = ladder([], rounds, [])
     received = swap(sent, "layer")
-    for i, pair in enumerate(rounds):
-        nexts = rounds[i + 1 : i + 2]
-        kept, *sent = ladder([pair], nexts, after)
-        pack = merge(pair, kept, received)
-        if nexts:
-            received = swap(sent[0], "layer")
-        after = [pack] + [both[0] for both in packs[-1:]]
-        packs.append(deliver(pair, pack))
-    early = [pack for both in packs[:-1] for pack in both]
-    base = owner_sum(early, None, held((OWN, edge, edge), F32))
-    return owner_sum(list(packs[-1]), base, jax.ShapeDtypeStruct((OWN, edge, edge), F32))
+    near, far = [], []
+    first, after = 0, []
+    for pairs in stages:
+        (kept,) = ladder(pairs, [], after)
+        after = merge(pairs, first, kept, received)
+        for pair, pack in zip(pairs, after):
+            near.append(send(pair, pack, 0))
+            far.append(send(pair, pack, 1) if pair == rounds[-1] else swap(near[-1], "layer"))
+        first += len(pairs)
+    count = len(stages[0])
+    base = owner_sum(near[:count] + far[:count], None, held((OWN, edge, edge), F32))
+    return owner_sum(near[count:] + far[count:], base, jax.ShapeDtypeStruct((OWN, edge, edge), F32))
 
 
 def solution(mesh):

time: 43.4 us -> 38.7 us (0.89)
  local copies, waits for them, and re-layouts: 3.4 us -> 0.01 us
  starting transfers between devices: 13.3 us -> 12.6 us
  Pallas kernels: 22.3 us -> 21.8 us
    unnamed x12 -> x2, local copies, waits for them, and re-layouts: 3.4 us -> 0.01 us
    ppermute x9 -> x5, starting transfers between devices: 4.73 us -> 3.11 us  [swap(): return lax.ppermute(array, axis, [(i, i ^ 1) for i in range(size)])]
    ppermute x4 -> x5, starting transfers between devices: 8.58 us -> 9.47 us  [send(): return lax.ppermute(pack, ('layer', 'col'), route)]
    pallas_call x5 -> x3, Pallas kernels: 17.6 us -> 16.7 us  [ladder(): pl.pallas_call(functools.partial(ladder_kernel, bits, keeps, sends, len(a...]
    ppermute x4 -> x5, waiting for transfers between devices: 3.06 us -> 3.83 us  [send(): return lax.ppermute(pack, ('layer', 'col'), route)]
    ppermute x9 -> x5, waiting for transfers between devices: 0.77 us -> 0.24 us  [swap(): return lax.ppermute(array, axis, [(i, i ^ 1) for i in range(size)])]
  transfers between devices with their start and end apart: 13 -> 10, of which waited for: 3 -> 3; matrix products, arithmetic and copies ran while one was open for 0% -> 0% of each run, Pallas kernels for 44% -> 33%
where the time goes in v4:
time: 38.7 us; the launch traced here: 38.5 us
  Pallas kernels  21.8 us (56%)
  starting transfers between devices  12.6 us (33%)
  waiting for transfers between devices  4.07 us (11%)
    pallas_call x3, Pallas kernels, ladder(): pl.pallas_call(functools.partial(ladder_kernel, bits, keeps, sends, len(a...  16.7 us
    ppermute x5, starting transfers between devices, send(): return lax.ppermute(pack, ('layer', 'col'), route)  9.47 us
    ppermute x5, waiting for transfers between devices, send(): return lax.ppermute(pack, ('layer', 'col'), route)  3.83 us
    pallas_call x1, Pallas kernels, prepare(): pl.pallas_call(functools.partial(prepare_kernel, bits), out_shape=(held(s...  3.53 us
    ppermute x5, starting transfers between devices, swap(): return lax.ppermute(array, axis, [(i, i ^ 1) for i in range(size)])  3.11 us
    pallas_call x2, Pallas kernels, owner_sum(): pl.pallas_call(functools.partial(owner_kernel, len(packs)), out_shape=sha...  1.44 us
  transfers between devices with their start and end apart: 10, of which 3 were waited for; matrix products, arithmetic and copies ran while one was open for 0% of the time, Pallas kernels for 33%

profile of v4, /device:TPU:0, one launch (start us, length us, event | category | flops | bytes accessed | tf_op | source)
XLA Modules:
  0.0 38.5 jit_solution(196296557395750870)
XLA Ops:
  0.0 0.0 copy-start
  0.0 3.0 %collective-permute-start = (bf16[4,128,128]{2,1,0:T(8,128)(2,1)}, bf16[4,128,128]{2,1,0:T(8,128)(2,1)S(1)}, u32[]{:S(2)}, u32[]{:S(2)}) collective-permute-start(bf16[4,128,128]{2,1,0:T(8,128)(2,1)} %refs_1_.5), channel_id=1, source_target_pairs={{0,8},{8,0},{1,9},{9,1},{2,10},{10,2},{3,11},{11,3},{4,12},{12,4},... | collective-permute-start | bytes 393224 | tf_op jit(solution)/shard_map/ppermute | solution.py:191
  3.0 3.5 %load_and_flip.1 = (bf16[128,128,128]{2,1,0:T(8,128)(2,1)S(1)}, bf16[128,128,128]{2,1,0:T(8,128)(2,1)S(1)}, s32[16,48]{1,0:T(8,128)S(1)}, f32[8,16,128]{2,1,0:T(8,128)S(1)}) custom-call(bf16[128,128,128]{2,1,0:T(8,128)(2,1)} %source.1, s32[16,48]{1,0:T(8,128)} %amp_ids.1, s32[16,48]{1,0:T(8,128)} %left_ids.1, s32[16,48]{1,0:T(8,128)} %right_ids.1, ...), custom_call_target="tpu_custom_call" | custom-call | tf_op jit(solution)/shard_map/load_and_flip/pallas_call | solution.py:95
  6.5 0.2 collective-permute-done.refs_2_
  6.7 0.0 copy-done
  6.7 7.8 %ladder.4 = f32[8,128,128]{2,1,0:T(8,128)S(1)} custom-call(s32[16,48]{1,0:T(8,128)S(1)} %get-tuple-element.13.refs_0_, bf16[4,128,128]{2,1,0:T(8,128)(2,1)S(1)} %copy-done, bf16[4,128,128]{2,1,0:T(8,128)(2,1)S(1)} %collective-permute-done.refs_2_, bf16[128,128,128]{2,1,0:T(8,128)(2,1)S(1)} %get-tuple-element.14.refs_3_, ...), custom_call_target="tpu_custom_call" | custom-call | flops 3221225472 | bytes 1048576 | tf_op jit(solution)/shard_map/ladder/pallas_call | solution.py:211
  14.6 0.1 collective-permute-start.1
  14.7 4.5 %ladder.3.kept = f32[4,128,128]{2,1,0:T(8,128)S(1)} custom-call(s32[16,48]{1,0:T(8,128)S(1)} %get-tuple-element.13.refs_0_, bf16[4,128,128]{2,1,0:T(8,128)(2,1)S(1)} %copy-done, bf16[4,128,128]{2,1,0:T(8,128)(2,1)S(1)} %collective-permute-done.refs_2_, bf16[128,128,128]{2,1,0:T(8,128)(2,1)S(1)} %get-tuple-element.14.refs_3_, ...), custom_call_target="tpu_custom_call" | custom-call | flops 1610612736 | bytes 1048576 | tf_op jit(solution)/shard_map/ladder/pallas_call | solution.py:211
  19.2 0.0 collective-permute-done.1.received
  19.3 4.7 %collective-permute-start.6 = (bf16[272,128]{1,0:T(8,128)(2,1)S(1)}, bf16[272,128]{1,0:T(8,128)(2,1)S(1)}, u32[]{:S(2)}, u32[]{:S(2)}) collective-permute-start(bf16[272,128]{1,0:T(8,128)(2,1)S(1)} %get-tuple-element.17.refs_5_), channel_id=1, source_target_pairs={{0,7},{1,6},{2,5},{3,4},{4,3},{5,2},{6,1},{7,0},{16,22},{17,23},{1... | collective-permute-start | bytes 208904 | tf_op jit(solution)/shard_map/ppermute | solution.py:241
  24.0 0.0 collective-permute-start.7
  24.0 4.3 %ladder.5.kept = f32[4,128,128]{2,1,0:T(8,128)S(1)} custom-call(s32[16,48]{1,0:T(8,128)S(1)} %get-tuple-element.13.refs_0_, bf16[4,128,128]{2,1,0:T(8,128)(2,1)S(1)} %copy-done, bf16[4,128,128]{2,1,0:T(8,128)(2,1)S(1)} %collective-permute-done.refs_2_, bf16[128,128,128]{2,1,0:T(8,128)(2,1)S(1)} %get-tuple-element.14.refs_3_, ...), custom_call_target="tpu_custom_call" | custom-call | flops 1610612736 | bytes 1048576 | tf_op jit(solution)/shard_map/ladder/pallas_call | solution.py:211
  28.3 0.1 merge_layers.3
  28.4 0.7 %collective-permute-start.2 = (bf16[272,128]{1,0:T(8,128)(2,1)S(1)}, bf16[272,128]{1,0:T(8,128)(2,1)S(1)}, u32[]{:S(2)}, u32[]{:S(2)}) collective-permute-start(bf16[272,128]{1,0:T(8,128)(2,1)S(1)} %get-tuple-element.19), channel_id=1, source_target_pairs={{0,2},{1,3},{2,0},{3,1},{4,6},{5,7},{6,4},{7,5},{16,19},{17,18},{1... | collective-permute-start | bytes 208904 | tf_op jit(solution)/shard_map/ppermute | solution.py:241
  29.1 0.0 collective-permute-done.6.refs_0_
  29.1 0.0 collective-permute-start.8
  29.1 1.4 %collective-permute-done.7.refs_1_ = bf16[272,128]{1,0:T(8,128)(2,1)S(1)} collective-permute-done((bf16[272,128]{1,0:T(8,128)(2,1)S(1)}, bf16[272,128]{1,0:T(8,128)(2,1)S(1)}, u32[]{:S(2)}, u32[]{:S(2)}) %collective-permute-start.7) | collective-permute-done | bytes 69664 | tf_op jit(solution)/shard_map/ppermute | solution.py:241
  30.5 0.0 collective-permute-start.9
  30.5 0.8 %collective-permute-start.5 = (bf16[272,128]{1,0:T(8,128)(2,1)S(1)}, bf16[272,128]{1,0:T(8,128)(2,1)S(1)}, u32[]{:S(2)}, u32[]{:S(2)}) collective-permute-start(bf16[272,128]{1,0:T(8,128)(2,1)S(1)} %get-tuple-element.20), channel_id=1, source_target_pairs={{0,17},{1,16},{2,19},{3,18},{4,21},{5,20},{6,23},{7,22},{16,0},{17... | collective-permute-start | bytes 208904 | tf_op jit(solution)/shard_map/ppermute | solution.py:241
  31.2 3.3 %collective-permute-start.3 = (bf16[272,128]{1,0:T(8,128)(2,1)S(1)}, bf16[272,128]{1,0:T(8,128)(2,1)S(1)}, u32[]{:S(2)}, u32[]{:S(2)}) collective-permute-start(bf16[272,128]{1,0:T(8,128)(2,1)S(1)} %get-tuple-element.20), channel_id=1, source_target_pairs={{0,1},{1,0},{2,3},{3,2},{4,5},{5,4},{6,7},{7,6},{16,16},{17,17},{1... | collective-permute-start | bytes 208904 | tf_op jit(solution)/shard_map/ppermute | solution.py:241
  34.5 0.0 collective-permute-done.2.refs_0_
  34.5 0.1 collective-permute-start.4
  34.6 0.0 collective-permute-done.8.refs_2_
  34.6 0.0 collective-permute-done.9.refs_3_
  34.6 0.3 owner_sum.2.refs_4_
  34.9 0.0 collective-permute-done.5.refs_3_
  34.9 2.5 %collective-permute-done.3.refs_1_ = bf16[272,128]{1,0:T(8,128)(2,1)S(1)} collective-permute-done((bf16[272,128]{1,0:T(8,128)(2,1)S(1)}, bf16[272,128]{1,0:T(8,128)(2,1)S(1)}, u32[]{:S(2)}, u32[]{:S(2)}) %collective-permute-start.3) | collective-permute-done | bytes 69664 | tf_op jit(solution)/shard_map/ppermute | solution.py:241
  37.4 0.0 collective-permute-done.4.refs_2_
  37.4 1.1 %owner_sum.3 = f32[8,128,128]{2,1,0:T(8,128)} custom-call(bf16[272,128]{1,0:T(8,128)(2,1)S(1)} %collective-permute-done.2.refs_0_, bf16[272,128]{1,0:T(8,128)(2,1)S(1)} %collective-permute-done.3.refs_1_, bf16[272,128]{1,0:T(8,128)(2,1)S(1)} %collective-permute-done.4.refs_2_, bf16[272,128]{1,0:T(8,128)(2,1)S(1)} %collective-permute-done.5.refs_3_, ...), custom_call_target="tpu_custom_call" | custom-call | flops 16777216 | bytes 4194304 | tf_op jit(solution)/shard_map/owner_sum/pallas_call | solution.py:245
  (1 shorter events, 0.0 us)
Async XLA Ops:
  0.0 6.7 %copy-start = (bf16[4,128,128]{2,1,0:T(8,128)(2,1)S(1)}, bf16[4,128,128]{2,1,0:T(8,128)(2,1)}, u32[]{:S(2)}) copy-start(bf16[4,128,128]{2,1,0:T(8,128)(2,1)} %refs_1_.5) | copy-start | bytes 393220
  0.0 6.7 %collective-permute-start = (bf16[4,128,128]{2,1,0:T(8,128)(2,1)}, bf16[4,128,128]{2,1,0:T(8,128)(2,1)S(1)}, u32[]{:S(2)}, u32[]{:S(2)}) collective-permute-start(bf16[4,128,128]{2,1,0:T(8,128)(2,1)} %refs_1_.5), channel_id=1, source_target_pairs={{0,8},{8,0},{1,9},{9,1},{2,10},{10,2},{3,11},{11,3},{4,12},{12,4},... | collective-permute-start | bytes 393224 | tf_op jit(solution)/shard_map/ppermute | solution.py:191
  14.6 4.6 %collective-permute-start.1 = (f32[8,128,128]{2,1,0:T(8,128)S(1)}, f32[8,128,128]{2,1,0:T(8,128)S(1)}, u32[]{:S(2)}, u32[]{:S(2)}) collective-permute-start(f32[8,128,128]{2,1,0:T(8,128)S(1)} %ladder.4), channel_id=1, source_target_pairs={{0,16},{16,0},{1,17},{17,1},{2,18},{18,2},{3,19},{19,3},{4,20},{20... | collective-permute-start | bytes 1572872 | tf_op jit(solution)/shard_map/ppermute | solution.py:191
  19.3 9.8 %collective-permute-start.6 = (bf16[272,128]{1,0:T(8,128)(2,1)S(1)}, bf16[272,128]{1,0:T(8,128)(2,1)S(1)}, u32[]{:S(2)}, u32[]{:S(2)}) collective-permute-start(bf16[272,128]{1,0:T(8,128)(2,1)S(1)} %get-tuple-element.17.refs_5_), channel_id=1, source_target_pairs={{0,7},{1,6},{2,5},{3,4},{4,3},{5,2},{6,1},{7,0},{16,22},{17,23},{1... | collective-permute-start | bytes 208904 | tf_op jit(solution)/shard_map/ppermute | solution.py:241
  24.0 6.5 %collective-permute-start.7 = (bf16[272,128]{1,0:T(8,128)(2,1)S(1)}, bf16[272,128]{1,0:T(8,128)(2,1)S(1)}, u32[]{:S(2)}, u32[]{:S(2)}) collective-permute-start(bf16[272,128]{1,0:T(8,128)(2,1)S(1)} %get-tuple-element.18.refs_6_), channel_id=1, source_target_pairs={{0,5},{1,4},{2,7},{3,6},{4,1},{5,0},{6,3},{7,2},{16,20},{17,21},{1... | collective-permute-start | bytes 208904 | tf_op jit(solution)/shard_map/ppermute | solution.py:241
  28.4 6.1 %collective-permute-start.2 = (bf16[272,128]{1,0:T(8,128)(2,1)S(1)}, bf16[272,128]{1,0:T(8,128)(2,1)S(1)}, u32[]{:S(2)}, u32[]{:S(2)}) collective-permute-start(bf16[272,128]{1,0:T(8,128)(2,1)S(1)} %get-tuple-element.19), channel_id=1, source_target_pairs={{0,2},{1,3},{2,0},{3,1},{4,6},{5,7},{6,4},{7,5},{16,19},{17,18},{1... | collective-permute-start | bytes 208904 | tf_op jit(solution)/shard_map/ppermute | solution.py:241
  29.1 5.5 %collective-permute-start.8 = (bf16[272,128]{1,0:T(8,128)(2,1)S(1)}, bf16[272,128]{1,0:T(8,128)(2,1)S(1)}, u32[]{:S(2)}, u32[]{:S(2)}) collective-permute-start(bf16[272,128]{1,0:T(8,128)(2,1)S(1)} %collective-permute-done.6.refs_0_), channel_id=1, source_target_pairs={{0,16},{16,0},{1,17},{17,1},{2,18},{18,2},{3,19},{19,3},{4,20},{20... | collective-permute-start | bytes 208904 | tf_op jit(solution)/shard_map/ppermute | solution.py:191
  30.5 4.1 %collective-permute-start.9 = (bf16[272,128]{1,0:T(8,128)(2,1)S(1)}, bf16[272,128]{1,0:T(8,128)(2,1)S(1)}, u32[]{:S(2)}, u32[]{:S(2)}) collective-permute-start(bf16[272,128]{1,0:T(8,128)(2,1)S(1)} %collective-permute-done.7.refs_1_), channel_id=1, source_target_pairs={{0,16},{16,0},{1,17},{17,1},{2,18},{18,2},{3,19},{19,3},{4,20},{20... | collective-permute-start | bytes 208904 | tf_op jit(solution)/shard_map/ppermute | solution.py:191
  30.5 4.5 %collective-permute-start.5 = (bf16[272,128]{1,0:T(8,128)(2,1)S(1)}, bf16[272,128]{1,0:T(8,128)(2,1)S(1)}, u32[]{:S(2)}, u32[]{:S(2)}) collective-permute-start(bf16[272,128]{1,0:T(8,128)(2,1)S(1)} %get-tuple-element.20), channel_id=1, source_target_pairs={{0,17},{1,16},{2,19},{3,18},{4,21},{5,20},{6,23},{7,22},{16,0},{17... | collective-permute-start | bytes 208904 | tf_op jit(solution)/shard_map/ppermute | solution.py:241
  31.2 6.2 %collective-permute-start.3 = (bf16[272,128]{1,0:T(8,128)(2,1)S(1)}, bf16[272,128]{1,0:T(8,128)(2,1)S(1)}, u32[]{:S(2)}, u32[]{:S(2)}) collective-permute-start(bf16[272,128]{1,0:T(8,128)(2,1)S(1)} %get-tuple-element.20), channel_id=1, source_target_pairs={{0,1},{1,0},{2,3},{3,2},{4,5},{5,4},{6,7},{7,6},{16,16},{17,17},{1... | collective-permute-start | bytes 208904 | tf_op jit(solution)/shard_map/ppermute | solution.py:241
  34.5 2.9 %collective-permute-start.4 = (bf16[272,128]{1,0:T(8,128)(2,1)S(1)}, bf16[272,128]{1,0:T(8,128)(2,1)S(1)}, u32[]{:S(2)}, u32[]{:S(2)}) collective-permute-start(bf16[272,128]{1,0:T(8,128)(2,1)S(1)} %collective-permute-done.2.refs_0_), channel_id=1, source_target_pairs={{0,16},{16,0},{1,17},{17,1},{2,18},{18,2},{3,19},{19,3},{4,20},{20... | collective-permute-start | bytes 208904 | tf_op jit(solution)/shard_map/ppermute | solution.py:191

commit v5 on v4

v5 whole, which is shorter than its diff:
```python
import functools

import jax
import jax.numpy as jnp
from jax import lax
from jax.experimental import pallas as pl
from jax.experimental.pallas import tpu as pltpu
from jax.sharding import PartitionSpec as P

OWN = 8
CAP = 2
LABEL_ROWS = 8
F32 = jnp.float32
BF16 = jnp.bfloat16
VMEM_BYTES = 24 << 20


def smem():
    return pl.BlockSpec(memory_space=pltpu.SMEM)


def vmem():
    return pl.BlockSpec(memory_space=pltpu.VMEM)


def held(shape, dtype):
    return pltpu.VMEM(shape, dtype)


def in_vmem(array):
    return pltpu.with_memory_space_constraint(array, pltpu.VMEM)


def params():
    return pltpu.CompilerParams(vmem_limit_bytes=VMEM_BYTES)


def brief():
    return pl.CostEstimate(flops=1 << 20, bytes_accessed=1 << 10, transcendentals=0)


def exchange_rounds(columns):
    far = list(range(columns - 1, 3, -1))
    pairs = [(far[i], far[i + 1]) for i in range(0, len(far), 2)]
    return pairs + [(0, 3), (1, 2)]


def prepare_kernel(
    bits, source, amp_ids, left_ids, right_ids, dest_in, labels_in,
    tiles, flipped, table, label_blocks, ids, packed, sorted_ids, dest, labels, seen, arrived, ready,
):
    count = tiles.shape[0]
    chunks = arrived.shape[0]
    step = count // chunks
    columns = label_blocks.shape[0]
    small = [
        pltpu.make_async_copy(src, dst, ready.at[i])
        for i, (src, dst) in enumerate(
            [(dest_in, dest), (labels_in, labels)]
            + [(src, ids.at[i]) for i, src in enumerate((amp_ids, left_ids, right_ids))]
        )
    ]

    def copy(i):
        span = pl.ds(i * step, step)
        return pltpu.make_async_copy(source.at[span], tiles.at[span], arrived.at[i])

    for transfer in small:
        transfer.start()
    for i in range(chunks):
        copy(i).start()

    sorted_ids[...] = jnp.zeros(sorted_ids.shape, jnp.int32)
    label_blocks[...] = jnp.full(label_blocks.shape, OWN, F32)
    for d in range(columns):
        seen[d] = 0

    def flip(i):
        copy(i).wait()
        for j in range(step):
            flipped[i * step + j] = tiles[i * step + j].T

    for i in range(chunks // 2):
        flip(i)

    me = lax.axis_index("col")
    for transfer in small:
        transfer.wait()
    packed[...] = (ids[0] << (2 * bits)) | (ids[1] << bits) | ids[2]
    for k in range(packed.shape[0]):
        offset = dest[k] ^ me
        rank = seen[offset]
        seen[offset] = rank + 1
        sorted_ids[pl.ds(offset * CAP + rank, 1), :] = packed[pl.ds(k, 1), :]
        spot = pl.ds(pl.multiple_of(rank * LABEL_ROWS, LABEL_ROWS), LABEL_ROWS)
        label_blocks[offset, spot, :] = jnp.full((LABEL_ROWS, label_blocks.shape[2]), labels[k].astype(F32))
    publish = pltpu.make_async_copy(sorted_ids, table, ready.at[len(small)])
    publish.start()

    for i in range(chunks // 2, chunks):
        flip(i)
    publish.wait()


def prepare(columns, bits, integrals, amp_index, left_index, right_index, target, owner_slot):
    shape = integrals.shape
    slots, terms = amp_index.shape
    operands = (integrals, amp_index, left_index, right_index, target, owner_slot)
    return pl.pallas_call(
        functools.partial(prepare_kernel, bits),
        out_shape=(
            held(shape, BF16),
            held(shape, BF16),
            pltpu.SMEM((columns * CAP, terms), jnp.int32),
            held((columns, CAP * LABEL_ROWS, shape[2]), F32),
        ),
        in_specs=[pl.BlockSpec(memory_space=pltpu.HBM)] * len(operands),
        out_specs=(vmem(), vmem(), smem(), vmem()),
        scratch_shapes=[
            pltpu.VMEM((3, slots, terms), jnp.int32),
            pltpu.VMEM((slots, terms), jnp.int32),
            pltpu.VMEM((columns * CAP, terms), jnp.int32),
            pltpu.SMEM((slots,), jnp.int32),
            pltpu.SMEM((slots,), jnp.int32),
            pltpu.SMEM((columns,), jnp.int32),
            pltpu.SemaphoreType.DMA((8,)),
            pltpu.SemaphoreType.DMA((6,)),
        ],
        cost_estimate=brief(),
        compiler_params=params(),
        name="load_and_flip",
    )(*[pltpu.with_memory_space_constraint(array, pltpu.HBM) for array in operands])


def pick(pair, layer):
    return jnp.where(layer == 0, pair[0], pair[1])


def ladder_kernel(bits, keeps, sends, parts, waits, *refs):
    table = refs[0]
    amp_parts = refs[1 : 1 + parts]
    tiles, flipped = refs[1 + parts : 3 + parts]
    outs, amps = refs[3 + parts + waits : -1], refs[-1]
    terms = table.shape[1]
    layer = lax.axis_index("layer")
    amp_dev = amp_parts[0].shape[0]
    if parts == 1:
        amps[...] = amp_parts[0][...]
    else:
        row = lax.axis_index("row")
        amps[pl.ds(row * amp_dev, amp_dev)] = amp_parts[0][...]
        amps[pl.ds((1 - row) * amp_dev, amp_dev)] = amp_parts[1][...]
    mask = (1 << bits) - 1
    picked = [(outs[0], i, pick(pair, layer)) for i, pair in enumerate(keeps)]
    picked += [(outs[-1], i, pick(pair, 1 - layer)) for i, pair in enumerate(sends)]
    for out, i, offset in picked:
        for rank in range(CAP):
            slot = offset * CAP + rank
            lefts, middles = [], []
            for t in range(terms):
                word = table[slot, t]
                lefts.append(tiles[(word >> bits) & mask])
                middles.append(
                    jnp.dot(
                        amps[word >> (2 * bits)], flipped[word & mask], preferred_element_type=F32
                    ).astype(BF16)
                )
            out[i * CAP + rank] = jnp.dot(
                jnp.concatenate(lefts, axis=1),
                jnp.concatenate(middles, axis=0),
                preferred_element_type=F32,
            ).astype(out.dtype)


def merge_kernel(pairs, skip, kept, received, label_blocks, *packs):
    edge = kept.shape[1]
    layer = lax.axis_index("layer")
    for i, (pair, packed) in enumerate(zip(pairs, packs)):
        for rank in range(CAP):
            tile = i * CAP + rank
            other = received[tile] if skip is None else received[skip + tile * edge : skip + (tile + 1) * edge]
            packed[rank * edge : (rank + 1) * edge] = (kept[tile] + other.astype(F32)).astype(BF16)
        packed[CAP * edge :] = label_blocks[pick(pair, layer)].astype(BF16)


def join_kernel(*refs):
    packs, sent, joined = refs[:-2], refs[-2], refs[-1]
    start = 0
    for part in [*packs, *[sent.at[i] for i in range(sent.shape[0])]]:
        joined[start : start + part.shape[0]] = part[...]
        start += part.shape[0]


def late_join_kernel(local_layer, own, middle, last, joined):
    joined[0] = jnp.where(lax.axis_index("layer") == local_layer, own[...], middle[...])
    joined[1] = last[...]


def pieces(packs, rows, edge):
    for pack in packs:
        marks = pack[CAP * edge : CAP * (edge + LABEL_ROWS), :].astype(F32)
        for rank in range(CAP):
            mark = marks[rank * LABEL_ROWS : (rank + 1) * LABEL_ROWS].reshape(1, LABEL_ROWS, edge)
            tile = pack[pl.ds(rank * edge + rows.start, rows.size), :].astype(F32)
            yield mark, tile.reshape(rows.size // LABEL_ROWS, LABEL_ROWS, edge)


def add_owned(total, parts, s):
    for mark, tile in parts:
        term = jnp.where(mark == s, tile, 0.0)
        total = term if total is None else total + term
    return total


def early_owner_kernel(count, near, far, out):
    edge = out.shape[2]
    size = CAP * (edge + LABEL_ROWS)

    def packs(ref):
        return [ref.at[pl.ds(i * size, size)] for i in range(count)]

    for start in range(0, edge, 32):
        rows = pl.ds(start, 32)
        sides = [list(pieces(packs(ref), rows, edge)) for ref in (near, far)]
        for s in range(OWN):
            total = add_owned(None, sides[0], s) + add_owned(None, sides[1], s)
            out[s, rows, :] = total.reshape(32, edge)


def last_owner_kernel(base, near, far, out, total, sent):
    edge = out.shape[2]
    chunks = sent.shape[0]
    height = edge // chunks

    def copy(i):
        rows = pl.ds(i * height, height)
        return pltpu.make_async_copy(total.at[:, rows, :], out.at[:, rows, :], sent.at[i])

    for i in range(chunks):
        rows = pl.ds(i * height, height)
        sides = [list(pieces([ref.at[k] for k in range(ref.shape[0])], rows, edge)) for ref in (near, far)]
        for s in range(OWN):
            late = add_owned(None, sides[0], s) + add_owned(None, sides[1], s)
            total[s, rows, :] = base[s, rows, :] + late.reshape(height, edge)
        copy(i).start()
    for i in range(chunks):
        copy(i).wait()


def swap(array, axis):
    size = lax.axis_size(axis)
    return lax.ppermute(array, axis, [(i, i ^ 1) for i in range(size)])


def shards(amplitudes, integrals, amp_index, left_index, right_index, dest_col, owner_slot):
    columns = lax.axis_size("col")
    rows = lax.axis_size("row")
    edge = integrals.shape[1]
    bits = (integrals.shape[0] - 1).bit_length()
    if rows == 2:
        amp_parts = (amplitudes, swap(amplitudes, "row"))
    else:
        amp_parts = (lax.all_gather(amplitudes, "row", axis=0, tiled=True),)
    amp_total = rows * amplitudes.shape[0]
    tiles, flipped, table, label_blocks = prepare(
        columns, bits, integrals, amp_index, left_index, right_index, dest_col.reshape(-1), owner_slot
    )
    rounds = exchange_rounds(columns)

    def ladder(keeps, sends, after, sent_type=F32):
        groups = [(len(group) * CAP, kind) for group, kind in ((keeps, F32), (sends, sent_type)) if group]
        return pl.pallas_call(
            functools.partial(ladder_kernel, bits, keeps, sends, len(amp_parts), len(after)),
            out_shape=tuple(held((slots, edge, edge), kind) for slots, kind in groups),
            in_specs=[smem()] + [vmem()] * (len(amp_parts) + 2) + [pl.BlockSpec(memory_space=pl.ANY)] * len(after),
            out_specs=(vmem(),) * len(groups),
            scratch_shapes=[pltpu.VMEM((amp_total, edge, edge), BF16)],
            cost_estimate=brief(),
            compiler_params=params(),
            name="ladder",
        )(pltpu.with_memory_space_constraint(table, pltpu.SMEM), *[in_vmem(part) for part in amp_parts], in_vmem(tiles), in_vmem(flipped), *after)

    pack_shape = (CAP * (edge + LABEL_ROWS), edge)

    def merge(pairs, skip, kept, received):
        return pl.pallas_call(
            functools.partial(merge_kernel, pairs, skip),
            out_shape=(held(pack_shape, BF16),) * len(pairs),
            in_specs=[vmem()] * 3,
            out_specs=(vmem(),) * len(pairs),
            cost_estimate=brief(),
            compiler_params=params(),
            name="merge_layers",
        )(in_vmem(kept), in_vmem(received), in_vmem(label_blocks))

    def join(packs, sent):
        rows = len(packs) * pack_shape[0] + sent.shape[0] * edge
        return pl.pallas_call(
            join_kernel,
            out_shape=held((rows, edge), BF16),
            in_specs=[vmem()] * (len(packs) + 1),
            out_specs=vmem(),
            cost_estimate=brief(),
            compiler_params=params(),
            name="join_packs",
        )(*[in_vmem(pack) for pack in packs], in_vmem(sent))

    def late_join(*packs):
        return pl.pallas_call(
            functools.partial(late_join_kernel, late[0].index(0)),
            out_shape=held((2, *pack_shape), BF16),
            in_specs=[vmem()] * len(packs),
            out_specs=vmem(),
            cost_estimate=brief(),
            compiler_params=params(),
            name="join_late_packs",
        )(*[in_vmem(pack) for pack in packs])

    def send(pair, pack, cross):
        route = [
            (layer * columns + c, (layer ^ cross) * columns + (c ^ pair[layer]))
            for layer in range(2)
            for c in range(columns)
            if pair[layer]
        ]
        return lax.ppermute(pack, ("layer", "col"), route)

    owned = (OWN, edge, edge)

    def early_owner_sum(near, far):
        return pl.pallas_call(
            functools.partial(early_owner_kernel, len(early)),
            out_shape=held(owned, F32),
            in_specs=[vmem()] * 2,
            out_specs=vmem(),
            cost_estimate=brief(),
            compiler_params=params(),
            name="early_owner_sum",
        )(in_vmem(near), in_vmem(far))

    def last_owner_sum(*arrays):
        return pl.pallas_call(
            last_owner_kernel,
            out_shape=jax.ShapeDtypeStruct(owned, F32),
            in_specs=[vmem()] * len(arrays),
            out_specs=pl.BlockSpec(memory_space=pl.ANY),
            scratch_shapes=[pltpu.VMEM(owned, F32), pltpu.SemaphoreType.DMA((4,))],
            cost_estimate=brief(),
            compiler_params=params(),
            name="last_owner_sum",
        )(*[in_vmem(array) for array in arrays])

    early, late = rounds[:-2], rounds[-2:]
    (sent,) = ladder([], early, [])
    received = swap(sent, "layer")
    (kept,) = ladder(early, [], [sent])
    packs = merge(early, None, kept, received)
    near = [send(pair, pack, 0) for pair, pack in zip(early, packs)]

    kept, sent = ladder(late, late, packs, BF16)
    joined = join(near, sent)
    far_joined = swap(joined, "layer")
    packs = merge(late, len(near) * pack_shape[0], kept, far_joined)
    middle, last = [send(pair, pack, 0) for pair, pack in zip(late, packs)]
    base = early_owner_sum(joined, far_joined)
    near = late_join(packs[0], middle, last)
    return last_owner_sum(base, near, swap(near, "layer"))


def solution(mesh):
    placed = (
        P(("row", "col"), None, None),
        P(("layer", "row", "col"), None, None),
        P(("layer", "row", "col"), None),
        P(("layer", "row", "col"), None),
        P(("layer", "row", "col"), None),
        P(("row", "col"), None),
        P(("row", "col")),
    )
    return jax.shard_map(
        shards, mesh=mesh, in_specs=placed, out_specs=P(("row", "col"), None, None), check_vma=False
    )
```

time: 38.7 us -> 36.9 us (0.953)
  Pallas kernels: 21.8 us -> 18.9 us
  waiting for transfers between devices: 4.07 us -> 5.95 us
  starting transfers between devices: 12.6 us -> 11.7 us
    ppermute x5 -> x4, starting transfers between devices: 9.47 us -> 6.36 us  [send(): return lax.ppermute(pack, ('layer', 'col'), route)]
    ppermute x5 -> x4, waiting for transfers between devices: 0.24 us -> 3.19 us  [swap(): return lax.ppermute(array, axis, [(i, i ^ 1) for i in range(size)])]
    ppermute x5 -> x4, starting transfers between devices: 3.11 us -> 5.3 us  [swap(): return lax.ppermute(array, axis, [(i, i ^ 1) for i in range(size)])]
    pallas_call x3, Pallas kernels: 16.7 us -> 14.6 us  [ladder(): pl.pallas_call(functools.partial(ladder_kernel, bits, keeps, sends, len(a...]
    ppermute x5 -> x4, waiting for transfers between devices: 3.83 us -> 2.76 us  [send(): return lax.ppermute(pack, ('layer', 'col'), route)]
    pallas_call x1, Pallas kernels: 3.53 us -> 2.79 us  [prepare(): pl.pallas_call(functools.partial(prepare_kernel, bits), out_shape=(held(s...]
    pallas_call x4 -> x6, Pallas kernels: 1.52 us -> 1.44 us  [the longest x1 1.02 us: last_owner_sum(): pl.pallas_call(last_owner_kernel, out_shape=jax.ShapeDtypeStruct(owned, F...]
  transfers between devices with their start and end apart: 10 -> 8, of which waited for: 3 -> 4; matrix products, arithmetic and copies ran while one was open for 0% -> 0% of each run, Pallas kernels for 33% -> 38%
where the time goes in v5:
time: 36.9 us; the launch traced here: 36.8 us
  Pallas kernels  18.9 us (51%)
  starting transfers between devices  11.7 us (32%)
  waiting for transfers between devices  5.95 us (16%)
    pallas_call x3, Pallas kernels, ladder(): pl.pallas_call(functools.partial(ladder_kernel, bits, keeps, sends, len(a...  14.6 us
    ppermute x4, starting transfers between devices, send(): return lax.ppermute(pack, ('layer', 'col'), route)  6.36 us
    ppermute x4, starting transfers between devices, swap(): return lax.ppermute(array, axis, [(i, i ^ 1) for i in range(size)])  5.3 us
    ppermute x4, waiting for transfers between devices, swap(): return lax.ppermute(array, axis, [(i, i ^ 1) for i in range(size)])  3.19 us
    pallas_call x1, Pallas kernels, prepare(): pl.pallas_call(functools.partial(prepare_kernel, bits), out_shape=(held(s...  2.79 us
    ppermute x4, waiting for transfers between devices, send(): return lax.ppermute(pack, ('layer', 'col'), route)  2.76 us
    pallas_call x1, Pallas kernels, last_owner_sum(): pl.pallas_call(last_owner_kernel, out_shape=jax.ShapeDtypeStruct(owned, F...  1.02 us
  transfers between devices with their start and end apart: 8, of which 4 were waited for; matrix products, arithmetic and copies ran while one was open for 0% of the time, Pallas kernels for 38%

profile of v5, /device:TPU:0, one launch (start us, length us, event | category | flops | bytes accessed | tf_op | source)
XLA Modules:
  0.0 36.8 jit_solution(3599943931623541821)
XLA Ops:
  0.0 0.0 copy-start
  0.0 3.0 %collective-permute-start = (bf16[4,128,128]{2,1,0:T(8,128)(2,1)}, bf16[4,128,128]{2,1,0:T(8,128)(2,1)S(1)}, u32[]{:S(2)}, u32[]{:S(2)}) collective-permute-start(bf16[4,128,128]{2,1,0:T(8,128)(2,1)} %refs_1_.5), channel_id=1, source_target_pairs={{0,8},{8,0},{1,9},{9,1},{2,10},{10,2},{3,11},{11,3},{4,12},{12,4},... | collective-permute-start | bytes 393224 | tf_op jit(solution)/shard_map/ppermute | solution.py:252
  3.0 2.8 %load_and_flip.1 = (bf16[128,128,128]{2,1,0:T(8,128)(2,1)S(1)}, bf16[128,128,128]{2,1,0:T(8,128)(2,1)S(1)}, s32[16,48]{1,0:T(8,128)S(4)}, f32[8,16,128]{2,1,0:T(8,128)S(1)}) custom-call(bf16[128,128,128]{2,1,0:T(8,128)(2,1)} %source.1, s32[16,48]{1,0:T(8,128)} %amp_ids.1, s32[16,48]{1,0:T(8,128)} %left_ids.1, s32[16,48]{1,0:T(8,128)} %right_ids.1, ...), custom_call_target="tpu_custom_call" | custom-call | flops 1048576 | bytes 1024 | tf_op jit(solution)/shard_map/load_and_flip/pallas_call | solution.py:109
  5.8 1.0 %collective-permute-done.refs_2_ = bf16[4,128,128]{2,1,0:T(8,128)(2,1)S(1)} collective-permute-done((bf16[4,128,128]{2,1,0:T(8,128)(2,1)}, bf16[4,128,128]{2,1,0:T(8,128)(2,1)S(1)}, u32[]{:S(2)}, u32[]{:S(2)}) %collective-permute-start) | collective-permute-done | bytes 131104 | tf_op jit(solution)/shard_map/ppermute | solution.py:252
  6.7 0.0 copy-done
  6.7 3.7 %ladder.3.refs_5_ = f32[4,128,128]{2,1,0:T(8,128)S(1)} custom-call(s32[16,48]{1,0:T(8,128)S(4)} %get-tuple-element.15.refs_0_, bf16[4,128,128]{2,1,0:T(8,128)(2,1)S(1)} %copy-done, bf16[4,128,128]{2,1,0:T(8,128)(2,1)S(1)} %collective-permute-done.refs_2_, bf16[128,128,128]{2,1,0:T(8,128)(2,1)S(1)} %get-tuple-element.16.refs_3_, ...), custom_call_target="tpu_custom_call" | custom-call | flops 1048576 | bytes 1024 | tf_op jit(solution)/shard_map/ladder/pallas_call | solution.py:272
  10.4 0.1 collective-permute-start.1
  10.5 3.7 %ladder.4.kept = f32[4,128,128]{2,1,0:T(8,128)S(1)} custom-call(s32[16,48]{1,0:T(8,128)S(4)} %get-tuple-element.15.refs_0_, bf16[4,128,128]{2,1,0:T(8,128)(2,1)S(1)} %copy-done, bf16[4,128,128]{2,1,0:T(8,128)(2,1)S(1)} %collective-permute-done.refs_2_, bf16[128,128,128]{2,1,0:T(8,128)(2,1)S(1)} %get-tuple-element.16.refs_3_, ...), custom_call_target="tpu_custom_call" | custom-call | flops 1048576 | bytes 1024 | tf_op jit(solution)/shard_map/ladder/pallas_call | solution.py:272
  14.2 0.0 collective-permute-done.1.received
  14.2 4.7 %collective-permute-start.2 = (bf16[272,128]{1,0:T(8,128)(2,1)S(1)}, bf16[272,128]{1,0:T(8,128)(2,1)S(1)}, u32[]{:S(2)}, u32[]{:S(2)}) collective-permute-start(bf16[272,128]{1,0:T(8,128)(2,1)S(1)} %get-tuple-element.19.refs_5_), channel_id=1, source_target_pairs={{0,7},{1,6},{2,5},{3,4},{4,3},{5,2},{6,1},{7,0},{16,22},{17,23},{1... | collective-permute-start | bytes 208904 | tf_op jit(solution)/shard_map/ppermute | solution.py:326
  18.9 0.0 collective-permute-start.3
  19.0 7.3 %ladder.5 = (f32[4,128,128]{2,1,0:T(8,128)S(1)}, bf16[4,128,128]{2,1,0:T(8,128)(2,1)S(1)}) custom-call(s32[16,48]{1,0:T(8,128)S(4)} %get-tuple-element.15.refs_0_, bf16[4,128,128]{2,1,0:T(8,128)(2,1)S(1)} %copy-done, bf16[4,128,128]{2,1,0:T(8,128)(2,1)S(1)} %collective-permute-done.refs_2_, bf16[128,128,128]{2,1,0:T(8,128)(2,1)S(1)} %get-tuple-element.16.refs_3_, ...), custom_call_target="tpu_custom_call" | custom-call | flops 1048576 | bytes 1024 | tf_op jit(solution)/shard_map/ladder/pallas_call | solution.py:272
  26.3 0.0 collective-permute-done.2.refs_0_
  26.3 0.0 collective-permute-done.3.refs_1_
  26.3 0.1 collective-permute-start.4
  26.4 1.5 %collective-permute-done.4.far.received = bf16[1056,128]{1,0:T(8,128)(2,1)S(1)} collective-permute-done((bf16[1056,128]{1,0:T(8,128)(2,1)S(1)}, bf16[1056,128]{1,0:T(8,128)(2,1)S(1)}, u32[]{:S(2)}, u32[]{:S(2)}) %collective-permute-start.4) | collective-permute-done | bytes 270368 | tf_op jit(solution)/shard_map/ppermute | solution.py:252
  28.0 1.0 %collective-permute-start.6 = (bf16[272,128]{1,0:T(8,128)(2,1)S(1)}, bf16[272,128]{1,0:T(8,128)(2,1)S(1)}, u32[]{:S(2)}, u32[]{:S(2)}) collective-permute-start(bf16[272,128]{1,0:T(8,128)(2,1)S(1)} %get-tuple-element.24), channel_id=1, source_target_pairs={{0,1},{1,0},{2,3},{3,2},{4,5},{5,4},{6,7},{7,6},{16,18},{17,19},{1... | collective-permute-start | bytes 208904 | tf_op jit(solution)/shard_map/ppermute | solution.py:326
  28.9 0.7 %collective-permute-start.5 = (bf16[272,128]{1,0:T(8,128)(2,1)S(1)}, bf16[272,128]{1,0:T(8,128)(2,1)S(1)}, u32[]{:S(2)}, u32[]{:S(2)}) collective-permute-start(bf16[272,128]{1,0:T(8,128)(2,1)S(1)} %get-tuple-element.23.own), channel_id=1, source_target_pairs={{16,19},{17,18},{18,17},{19,16},{20,23},{21,22},{22,21},{23,20},{2... | collective-permute-start | bytes 208904 | tf_op jit(solution)/shard_map/ppermute | solution.py:326
  29.6 2.8 %collective-permute-done.6.last = bf16[272,128]{1,0:T(8,128)(2,1)S(1)} collective-permute-done((bf16[272,128]{1,0:T(8,128)(2,1)S(1)}, bf16[272,128]{1,0:T(8,128)(2,1)S(1)}, u32[]{:S(2)}, u32[]{:S(2)}) %collective-permute-start.6) | collective-permute-done | bytes 69664 | tf_op jit(solution)/shard_map/ppermute | solution.py:326
  32.4 0.0 collective-permute-done.5.middle
  32.4 2.2 %collective-permute-start.7 = (bf16[2,272,128]{2,1,0:T(8,128)(2,1)S(1)}, bf16[2,272,128]{2,1,0:T(8,128)(2,1)S(1)}, u32[]{:S(2)}, u32[]{:S(2)}) collective-permute-start(bf16[2,272,128]{2,1,0:T(8,128)(2,1)S(1)} %join_late_packs.1.near), channel_id=1, source_target_pairs={{0,16},{16,0},{1,17},{17,1},{2,18},{18,2},{3,19},{19,3},{4,20},{20... | collective-permute-start | bytes 417800 | tf_op jit(solution)/shard_map/ppermute | solution.py:252
  34.6 0.3 early_owner_sum.1.base
  34.9 0.7 %collective-permute-done.7.far = bf16[2,272,128]{2,1,0:T(8,128)(2,1)S(1)} collective-permute-done((bf16[2,272,128]{2,1,0:T(8,128)(2,1)S(1)}, bf16[2,272,128]{2,1,0:T(8,128)(2,1)S(1)}, u32[]{:S(2)}, u32[]{:S(2)}) %collective-permute-start.7) | collective-permute-done | bytes 139296 | tf_op jit(solution)/shard_map/ppermute | solution.py:252
  35.6 1.0 %last_owner_sum.1 = f32[8,128,128]{2,1,0:T(8,128)} custom-call(f32[8,128,128]{2,1,0:T(8,128)S(1)} %early_owner_sum.1.base, bf16[2,272,128]{2,1,0:T(8,128)(2,1)S(1)} %join_late_packs.1.near, bf16[2,272,128]{2,1,0:T(8,128)(2,1)S(1)} %collective-permute-done.7.far), custom_call_target="tpu_custom_call" | custom-call | flops 1048576 | bytes 1024 | tf_op jit(solution)/shard_map/last_owner_sum/pallas_call | solution.py:342
  (4 shorter events, 0.1 us)
Async XLA Ops:
  0.0 6.7 %copy-start = (bf16[4,128,128]{2,1,0:T(8,128)(2,1)S(1)}, bf16[4,128,128]{2,1,0:T(8,128)(2,1)}, u32[]{:S(2)}) copy-start(bf16[4,128,128]{2,1,0:T(8,128)(2,1)} %refs_1_.5) | copy-start | bytes 393220
  0.0 6.7 %collective-permute-start = (bf16[4,128,128]{2,1,0:T(8,128)(2,1)}, bf16[4,128,128]{2,1,0:T(8,128)(2,1)S(1)}, u32[]{:S(2)}, u32[]{:S(2)}) collective-permute-start(bf16[4,128,128]{2,1,0:T(8,128)(2,1)} %refs_1_.5), channel_id=1, source_target_pairs={{0,8},{8,0},{1,9},{9,1},{2,10},{10,2},{3,11},{11,3},{4,12},{12,4},... | collective-permute-start | bytes 393224 | tf_op jit(solution)/shard_map/ppermute | solution.py:252
  10.4 3.7 %collective-permute-start.1 = (f32[4,128,128]{2,1,0:T(8,128)S(1)}, f32[4,128,128]{2,1,0:T(8,128)S(1)}, u32[]{:S(2)}, u32[]{:S(2)}) collective-permute-start(f32[4,128,128]{2,1,0:T(8,128)S(1)} %ladder.3.refs_5_), channel_id=1, source_target_pairs={{0,16},{16,0},{1,17},{17,1},{2,18},{18,2},{3,19},{19,3},{4,20},{20... | collective-permute-start | bytes 786440 | tf_op jit(solution)/shard_map/ppermute | solution.py:252
  14.2 12.1 %collective-permute-start.2 = (bf16[272,128]{1,0:T(8,128)(2,1)S(1)}, bf16[272,128]{1,0:T(8,128)(2,1)S(1)}, u32[]{:S(2)}, u32[]{:S(2)}) collective-permute-start(bf16[272,128]{1,0:T(8,128)(2,1)S(1)} %get-tuple-element.19.refs_5_), channel_id=1, source_target_pairs={{0,7},{1,6},{2,5},{3,4},{4,3},{5,2},{6,1},{7,0},{16,22},{17,23},{1... | collective-permute-start | bytes 208904 | tf_op jit(solution)/shard_map/ppermute | solution.py:326
  18.9 7.4 %collective-permute-start.3 = (bf16[272,128]{1,0:T(8,128)(2,1)S(1)}, bf16[272,128]{1,0:T(8,128)(2,1)S(1)}, u32[]{:S(2)}, u32[]{:S(2)}) collective-permute-start(bf16[272,128]{1,0:T(8,128)(2,1)S(1)} %get-tuple-element.20.refs_6_), channel_id=1, source_target_pairs={{0,5},{1,4},{2,7},{3,6},{4,1},{5,0},{6,3},{7,2},{16,20},{17,21},{1... | collective-permute-start | bytes 208904 | tf_op jit(solution)/shard_map/ppermute | solution.py:326
  26.3 1.6 %collective-permute-start.4 = (bf16[1056,128]{1,0:T(8,128)(2,1)S(1)}, bf16[1056,128]{1,0:T(8,128)(2,1)S(1)}, u32[]{:S(2)}, u32[]{:S(2)}) collective-permute-start(bf16[1056,128]{1,0:T(8,128)(2,1)S(1)} %join_packs.1.near), channel_id=1, source_target_pairs={{0,16},{16,0},{1,17},{17,1},{2,18},{18,2},{3,19},{19,3},{4,20},{20... | collective-permute-start | bytes 811016 | tf_op jit(solution)/shard_map/ppermute | solution.py:252
  28.0 4.4 %collective-permute-start.6 = (bf16[272,128]{1,0:T(8,128)(2,1)S(1)}, bf16[272,128]{1,0:T(8,128)(2,1)S(1)}, u32[]{:S(2)}, u32[]{:S(2)}) collective-permute-start(bf16[272,128]{1,0:T(8,128)(2,1)S(1)} %get-tuple-element.24), channel_id=1, source_target_pairs={{0,1},{1,0},{2,3},{3,2},{4,5},{5,4},{6,7},{7,6},{16,18},{17,19},{1... | collective-permute-start | bytes 208904 | tf_op jit(solution)/shard_map/ppermute | solution.py:326
  28.9 3.4 %collective-permute-start.5 = (bf16[272,128]{1,0:T(8,128)(2,1)S(1)}, bf16[272,128]{1,0:T(8,128)(2,1)S(1)}, u32[]{:S(2)}, u32[]{:S(2)}) collective-permute-start(bf16[272,128]{1,0:T(8,128)(2,1)S(1)} %get-tuple-element.23.own), channel_id=1, source_target_pairs={{16,19},{17,18},{18,17},{19,16},{20,23},{21,22},{22,21},{23,20},{2... | collective-permute-start | bytes 208904 | tf_op jit(solution)/shard_map/ppermute | solution.py:326
  32.4 3.2 %collective-permute-start.7 = (bf16[2,272,128]{2,1,0:T(8,128)(2,1)S(1)}, bf16[2,272,128]{2,1,0:T(8,128)(2,1)S(1)}, u32[]{:S(2)}, u32[]{:S(2)}) collective-permute-start(bf16[2,272,128]{2,1,0:T(8,128)(2,1)S(1)} %join_late_packs.1.near), channel_id=1, source_target_pairs={{0,16},{16,0},{1,17},{17,1},{2,18},{18,2},{3,19},{19,3},{4,20},{20... | collective-permute-start | bytes 417800 | tf_op jit(solution)/shard_map/ppermute | solution.py:252

commit v6 on v5

--- a/solution.py
+++ b/solution.py
@@ -39,10 +39,12 @@
     return pl.CostEstimate(flops=1 << 20, bytes_accessed=1 << 10, transcendentals=0)
 
 
-def exchange_rounds(columns):
-    far = list(range(columns - 1, 3, -1))
-    pairs = [(far[i], far[i + 1]) for i in range(0, len(far), 2)]
-    return pairs + [(0, 3), (1, 2)]
+def round_slots(pair):
+    return [tuple(offset * CAP + rank for offset in pair) for rank in range(CAP)]
+
+
+def late_slots():
+    return [tuple(offset * CAP + rank for rank in range(CAP)) for offset in (1, 0)]
 
 
 def prepare_kernel(
@@ -151,55 +153,57 @@
         amps[pl.ds(row * amp_dev, amp_dev)] = amp_parts[0][...]
         amps[pl.ds((1 - row) * amp_dev, amp_dev)] = amp_parts[1][...]
     mask = (1 << bits) - 1
-    picked = [(outs[0], i, pick(pair, layer)) for i, pair in enumerate(keeps)]
-    picked += [(outs[-1], i, pick(pair, 1 - layer)) for i, pair in enumerate(sends)]
-    for out, i, offset in picked:
-        for rank in range(CAP):
-            slot = offset * CAP + rank
-            lefts, middles = [], []
-            for t in range(terms):
-                word = table[slot, t]
-                lefts.append(tiles[(word >> bits) & mask])
-                middles.append(
-                    jnp.dot(
-                        amps[word >> (2 * bits)], flipped[word & mask], preferred_element_type=F32
-                    ).astype(BF16)
-                )
-            out[i * CAP + rank] = jnp.dot(
-                jnp.concatenate(lefts, axis=1),
-                jnp.concatenate(middles, axis=0),
-                preferred_element_type=F32,
-            ).astype(out.dtype)
-
-
-def merge_kernel(pairs, skip, kept, received, label_blocks, *packs):
+    picked = [(outs[0], i, pick(slots, layer)) for i, slots in enumerate(keeps)]
+    picked += [(outs[-1], i, pick(slots, 1 - layer)) for i, slots in enumerate(sends)]
+    for out, i, slot in picked:
+        lefts, middles = [], []
+        for t in range(terms):
+            word = table[slot, t]
+            lefts.append(tiles[(word >> bits) & mask])
+            middles.append(
+                jnp.dot(
+                    amps[word >> (2 * bits)], flipped[word & mask], preferred_element_type=F32
+                ).astype(BF16)
+            )
+        out[i] = jnp.dot(
+            jnp.concatenate(lefts, axis=1),
+            jnp.concatenate(middles, axis=0),
+            preferred_element_type=F32,
+        ).astype(out.dtype)
+
+
+def merge_kernel(pairs, first, kept, received, label_blocks, *packs):
     edge = kept.shape[1]
     layer = lax.axis_index("layer")
     for i, (pair, packed) in enumerate(zip(pairs, packs)):
         for rank in range(CAP):
             tile = i * CAP + rank
-            other = received[tile] if skip is None else received[skip + tile * edge : skip + (tile + 1) * edge]
-            packed[rank * edge : (rank + 1) * edge] = (kept[tile] + other.astype(F32)).astype(BF16)
+            total = kept[tile] + received[first * CAP + tile]
+            packed[rank * edge : (rank + 1) * edge] = total.astype(BF16)
         packed[CAP * edge :] = label_blocks[pick(pair, layer)].astype(BF16)
 
 
+def late_merge_kernel(offset, kept_at, received_at, kept, received, label_blocks, packed):
+    edge = kept.shape[1]
+    spot = pl.ds(pl.multiple_of(lax.axis_index("layer") * LABEL_ROWS, LABEL_ROWS), LABEL_ROWS)
+    labels = label_blocks[offset, spot, :]
+    packed[:edge] = (kept[kept_at] + received[received_at]).astype(BF16)
+    packed[edge:] = jnp.concatenate([labels] * CAP, axis=0).astype(BF16)
+
+
 def join_kernel(*refs):
-    packs, sent, joined = refs[:-2], refs[-2], refs[-1]
+    joined = refs[-1]
     start = 0
-    for part in [*packs, *[sent.at[i] for i in range(sent.shape[0])]]:
+    for part in refs[:-1]:
         joined[start : start + part.shape[0]] = part[...]
         start += part.shape[0]
 
 
-def late_join_kernel(local_layer, own, middle, last, joined):
-    joined[0] = jnp.where(lax.axis_index("layer") == local_layer, own[...], middle[...])
-    joined[1] = last[...]
-
-
 def pieces(packs, rows, edge):
     for pack in packs:
-        marks = pack[CAP * edge : CAP * (edge + LABEL_ROWS), :].astype(F32)
-        for rank in range(CAP):
+        ranks = pack.shape[0] // edge
+        marks = pack[ranks * edge :, :].astype(F32)
+        for rank in range(ranks):
             mark = marks[rank * LABEL_ROWS : (rank + 1) * LABEL_ROWS].reshape(1, LABEL_ROWS, edge)
             tile = pack[pl.ds(rank * edge + rows.start, rows.size), :].astype(F32)
             yield mark, tile.reshape(rows.size // LABEL_ROWS, LABEL_ROWS, edge)
@@ -212,22 +216,21 @@
     return total
 
 
-def early_owner_kernel(count, near, far, out):
+def parts_of(joined, sizes):
+    starts = [sum(sizes[:i]) for i in range(len(sizes))]
+    return [joined.at[pl.ds(start, size)] for start, size in zip(starts, sizes)]
+
+
+def near_owner_kernel(sizes, near, out):
     edge = out.shape[2]
-    size = CAP * (edge + LABEL_ROWS)
-
-    def packs(ref):
-        return [ref.at[pl.ds(i * size, size)] for i in range(count)]
-
     for start in range(0, edge, 32):
         rows = pl.ds(start, 32)
-        sides = [list(pieces(packs(ref), rows, edge)) for ref in (near, far)]
+        side = list(pieces(parts_of(near, sizes), rows, edge))
         for s in range(OWN):
-            total = add_owned(None, sides[0], s) + add_owned(None, sides[1], s)
-            out[s, rows, :] = total.reshape(32, edge)
-
-
-def last_owner_kernel(base, near, far, out, total, sent):
+            out[s, rows, :] = add_owned(None, side, s).reshape(32, edge)
+
+
+def last_owner_kernel(sizes, near_sum, far, out, total, sent):
     edge = out.shape[2]
     chunks = sent.shape[0]
     height = edge // chunks
@@ -238,10 +241,9 @@
 
     for i in range(chunks):
         rows = pl.ds(i * height, height)
-        sides = [list(pieces([ref.at[k] for k in range(ref.shape[0])], rows, edge)) for ref in (near, far)]
+        side = list(pieces(parts_of(far, sizes), rows, edge))
         for s in range(OWN):
-            late = add_owned(None, sides[0], s) + add_owned(None, sides[1], s)
-            total[s, rows, :] = base[s, rows, :] + late.reshape(height, edge)
+            total[s, rows, :] = near_sum[s, rows, :] + add_owned(None, side, s).reshape(height, edge)
         copy(i).start()
     for i in range(chunks):
         copy(i).wait()
@@ -265,13 +267,12 @@
     tiles, flipped, table, label_blocks = prepare(
         columns, bits, integrals, amp_index, left_index, right_index, dest_col.reshape(-1), owner_slot
     )
-    rounds = exchange_rounds(columns)
-
-    def ladder(keeps, sends, after, sent_type=F32):
-        groups = [(len(group) * CAP, kind) for group, kind in ((keeps, F32), (sends, sent_type)) if group]
+
+    def ladder(keeps, sends, after):
+        groups = [len(group) for group in (keeps, sends) if group]
         return pl.pallas_call(
             functools.partial(ladder_kernel, bits, keeps, sends, len(amp_parts), len(after)),
-            out_shape=tuple(held((slots, edge, edge), kind) for slots, kind in groups),
+            out_shape=tuple(held((slots, edge, edge), F32) for slots in groups),
             in_specs=[smem()] + [vmem()] * (len(amp_parts) + 2) + [pl.BlockSpec(memory_space=pl.ANY)] * len(after),
             out_specs=(vmem(),) * len(groups),
             scratch_shapes=[pltpu.VMEM((amp_total, edge, edge), BF16)],
@@ -280,67 +281,50 @@
             name="ladder",
         )(pltpu.with_memory_space_constraint(table, pltpu.SMEM), *[in_vmem(part) for part in amp_parts], in_vmem(tiles), in_vmem(flipped), *after)
 
-    pack_shape = (CAP * (edge + LABEL_ROWS), edge)
-
-    def merge(pairs, skip, kept, received):
-        return pl.pallas_call(
-            functools.partial(merge_kernel, pairs, skip),
-            out_shape=(held(pack_shape, BF16),) * len(pairs),
-            in_specs=[vmem()] * 3,
-            out_specs=(vmem(),) * len(pairs),
+    def merge(kernel, rows, count, *arrays):
+        return pl.pallas_call(
+            kernel,
+            out_shape=(held((rows, edge), BF16),) * count,
+            in_specs=[vmem()] * len(arrays),
+            out_specs=(vmem(),) * count,
             cost_estimate=brief(),
             compiler_params=params(),
             name="merge_layers",
-        )(in_vmem(kept), in_vmem(received), in_vmem(label_blocks))
-
-    def join(packs, sent):
-        rows = len(packs) * pack_shape[0] + sent.shape[0] * edge
+        )(*[in_vmem(array) for array in arrays])
+
+    def join(*packs):
         return pl.pallas_call(
             join_kernel,
-            out_shape=held((rows, edge), BF16),
-            in_specs=[vmem()] * (len(packs) + 1),
-            out_specs=vmem(),
-            cost_estimate=brief(),
-            compiler_params=params(),
-            name="join_packs",
-        )(*[in_vmem(pack) for pack in packs], in_vmem(sent))
-
-    def late_join(*packs):
-        return pl.pallas_call(
-            functools.partial(late_join_kernel, late[0].index(0)),
-            out_shape=held((2, *pack_shape), BF16),
+            out_shape=held((sum(pack.shape[0] for pack in packs), edge), BF16),
             in_specs=[vmem()] * len(packs),
             out_specs=vmem(),
             cost_estimate=brief(),
             compiler_params=params(),
-            name="join_late_packs",
+            name="join_packs",
         )(*[in_vmem(pack) for pack in packs])
 
-    def send(pair, pack, cross):
+    def send(pair, pack):
         route = [
-            (layer * columns + c, (layer ^ cross) * columns + (c ^ pair[layer]))
-            for layer in range(2)
-            for c in range(columns)
-            if pair[layer]
+            (layer * columns + c, layer * columns + (c ^ pair[layer])) for layer in range(2) for c in range(columns)
         ]
         return lax.ppermute(pack, ("layer", "col"), route)
 
     owned = (OWN, edge, edge)
 
-    def early_owner_sum(near, far):
-        return pl.pallas_call(
-            functools.partial(early_owner_kernel, len(early)),
+    def near_owner_sum(sizes, near):
+        return pl.pallas_call(
+            functools.partial(near_owner_kernel, sizes),
             out_shape=held(owned, F32),
-            in_specs=[vmem()] * 2,
+            in_specs=[vmem()],
             out_specs=vmem(),
             cost_estimate=brief(),
             compiler_params=params(),
-            name="early_owner_sum",
-        )(in_vmem(near), in_vmem(far))
-
-    def last_owner_sum(*arrays):
-        return pl.pallas_call(
-            last_owner_kernel,
+            name="near_owner_sum",
+        )(in_vmem(near))
+
+    def last_owner_sum(sizes, *arrays):
+        return pl.pallas_call(
+            functools.partial(last_owner_kernel, sizes),
             out_shape=jax.ShapeDtypeStruct(owned, F32),
             in_specs=[vmem()] * len(arrays),
             out_specs=pl.BlockSpec(memory_space=pl.ANY),
@@ -350,21 +334,34 @@
             name="last_owner_sum",
         )(*[in_vmem(array) for array in arrays])
 
-    early, late = rounds[:-2], rounds[-2:]
-    (sent,) = ladder([], early, [])
+    pairs = [(d, d - 1) for d in range(columns - 1, 2, -2)]
+    slots = sum([round_slots(pair) for pair in pairs], [])
+    neighbour, local = late_slots()
+    split = len(slots) - CAP
+    pair_rows, late_rows = CAP * (edge + LABEL_ROWS), edge + CAP * LABEL_ROWS
+
+    def merge_pairs(first, group, kept):
+        kernel = functools.partial(merge_kernel, group, first)
+        return merge(kernel, pair_rows, len(group), kept, received, label_blocks)
+
+    def merge_late(offset, kept_at, kept):
+        kernel = functools.partial(late_merge_kernel, offset, kept_at, len(slots) + 1 - offset)
+        return merge(kernel, late_rows, 1, kept, received, label_blocks)
+
+    (sent,) = ladder([], slots + [neighbour, local], [])
     received = swap(sent, "layer")
-    (kept,) = ladder(early, [], [sent])
-    packs = merge(early, None, kept, received)
-    near = [send(pair, pack, 0) for pair, pack in zip(early, packs)]
-
-    kept, sent = ladder(late, late, packs, BF16)
-    joined = join(near, sent)
-    far_joined = swap(joined, "layer")
-    packs = merge(late, len(near) * pack_shape[0], kept, far_joined)
-    middle, last = [send(pair, pack, 0) for pair, pack in zip(late, packs)]
-    base = early_owner_sum(joined, far_joined)
-    near = late_join(packs[0], middle, last)
-    return last_owner_sum(base, near, swap(near, "layer"))
+    (kept,) = ladder(slots[:split], [], [sent])
+    packs = merge_pairs(0, pairs[:-1], kept)
+    near = [send(pair, pack) for pair, pack in zip(pairs, packs)]
+    (kept,) = ladder(slots[split:] + [neighbour], [], packs)
+    packs = merge_pairs(len(pairs) - 1, pairs[-1:], kept) + merge_late(1, CAP, kept)
+    near += [send(pair, pack) for pair, pack in zip([pairs[-1], (1, 1)], packs)]
+    (kept,) = ladder([local], [], packs)
+    near += merge_late(0, 0, kept)
+
+    sizes = [pack.shape[0] for pack in near]
+    joined = join(*near)
+    return last_owner_sum(sizes, near_owner_sum(sizes, joined), swap(joined, "layer"))
 
 
 def solution(mesh):

time: 36.9 us -> 33.5 us (0.908)
  starting transfers between devices: 11.7 us -> 10.1 us
  waiting for transfers between devices: 5.95 us -> 4.72 us
  Pallas kernels: 18.9 us -> 18.3 us
    ppermute x4 -> x3, starting transfers between devices: 5.3 us -> 3.11 us  [swap(): return lax.ppermute(array, axis, [(i, i ^ 1) for i in range(size)])]
    ppermute x4 -> x3, waiting for transfers between devices: 3.19 us -> 2.21 us  [swap(): return lax.ppermute(array, axis, [(i, i ^ 1) for i in range(size)])]
    ppermute x4, starting transfers between devices: 6.36 us -> 6.97 us  [send(): return lax.ppermute(pack, ('layer', 'col'), route)]
    pallas_call x3 -> x4, Pallas kernels: 14.6 us -> 14.1 us  [ladder(): pl.pallas_call(functools.partial(ladder_kernel, bits, keeps, sends, len(a...]
    pallas_call x6 -> x7, Pallas kernels: 1.44 us -> 1.47 us  [the longest x1 1.02 us: last_owner_sum(): pl.pallas_call(functools.partial(last_owner_kernel, sizes), out_shape=jax...]
  transfers between devices with their start and end apart: 8 -> 7, of which waited for: 4 -> 3; matrix products, arithmetic and copies ran while one was open for 0% -> 0% of each run, Pallas kernels for 38% -> 31%
where the time goes in v6:
time: 33.5 us; the launch traced here: 33.4 us
  Pallas kernels  18.3 us (55%)
  starting transfers between devices  10.1 us (30%)
  waiting for transfers between devices  4.72 us (14%)
    pallas_call x4, Pallas kernels, ladder(): pl.pallas_call(functools.partial(ladder_kernel, bits, keeps, sends, len(a...  14.1 us
    ppermute x4, starting transfers between devices, send(): return lax.ppermute(pack, ('layer', 'col'), route)  6.97 us
    ppermute x3, starting transfers between devices, swap(): return lax.ppermute(array, axis, [(i, i ^ 1) for i in range(size)])  3.11 us
    pallas_call x1, Pallas kernels, prepare(): pl.pallas_call(functools.partial(prepare_kernel, bits), out_shape=(held(s...  2.79 us
    ppermute x4, waiting for transfers between devices, send(): return lax.ppermute(pack, ('layer', 'col'), route)  2.51 us
    ppermute x3, waiting for transfers between devices, swap(): return lax.ppermute(array, axis, [(i, i ^ 1) for i in range(size)])  2.21 us
    pallas_call x1, Pallas kernels, last_owner_sum(): pl.pallas_call(functools.partial(last_owner_kernel, sizes), out_shape=jax...  1.02 us
  transfers between devices with their start and end apart: 7, of which 3 were waited for; matrix products, arithmetic and copies ran while one was open for 0% of the time, Pallas kernels for 31%

profile of v6, /device:TPU:0, one launch (start us, length us, event | category | flops | bytes accessed | tf_op | source)
XLA Modules:
  0.0 33.4 jit_solution(4964123753349625202)
XLA Ops:
  0.0 0.0 copy-start
  0.0 3.0 %collective-permute-start = (bf16[4,128,128]{2,1,0:T(8,128)(2,1)}, bf16[4,128,128]{2,1,0:T(8,128)(2,1)S(1)}, u32[]{:S(2)}, u32[]{:S(2)}) collective-permute-start(bf16[4,128,128]{2,1,0:T(8,128)(2,1)} %refs_1_.7), channel_id=1, source_target_pairs={{0,8},{8,0},{1,9},{9,1},{2,10},{10,2},{3,11},{11,3},{4,12},{12,4},... | collective-permute-start | bytes 393224 | tf_op jit(solution)/shard_map/ppermute | solution.py:254
  3.0 2.8 %load_and_flip.1 = (bf16[128,128,128]{2,1,0:T(8,128)(2,1)S(1)}, bf16[128,128,128]{2,1,0:T(8,128)(2,1)S(1)}, s32[16,48]{1,0:T(8,128)S(4)}, f32[8,16,128]{2,1,0:T(8,128)S(1)}) custom-call(bf16[128,128,128]{2,1,0:T(8,128)(2,1)} %source.1, s32[16,48]{1,0:T(8,128)} %amp_ids.1, s32[16,48]{1,0:T(8,128)} %left_ids.1, s32[16,48]{1,0:T(8,128)} %right_ids.1, ...), custom_call_target="tpu_custom_call" | custom-call | flops 1048576 | bytes 1024 | tf_op jit(solution)/shard_map/load_and_flip/pallas_call | solution.py:111
  5.8 1.0 %collective-permute-done.refs_2_ = bf16[4,128,128]{2,1,0:T(8,128)(2,1)S(1)} collective-permute-done((bf16[4,128,128]{2,1,0:T(8,128)(2,1)}, bf16[4,128,128]{2,1,0:T(8,128)(2,1)S(1)}, u32[]{:S(2)}, u32[]{:S(2)}) %collective-permute-start) | collective-permute-done | bytes 131104 | tf_op jit(solution)/shard_map/ppermute | solution.py:254
  6.7 0.0 copy-done
  6.7 6.7 %ladder.4.refs_5_ = f32[8,128,128]{2,1,0:T(8,128)S(1)} custom-call(s32[16,48]{1,0:T(8,128)S(4)} %get-tuple-element.11.refs_0_, bf16[4,128,128]{2,1,0:T(8,128)(2,1)S(1)} %copy-done, bf16[4,128,128]{2,1,0:T(8,128)(2,1)S(1)} %collective-permute-done.refs_2_, bf16[128,128,128]{2,1,0:T(8,128)(2,1)S(1)} %get-tuple-element.12.refs_3_, ...), custom_call_target="tpu_custom_call" | custom-call | flops 1048576 | bytes 1024 | tf_op jit(solution)/shard_map/ladder/pallas_call | solution.py:273
  13.5 0.1 collective-permute-start.1
  13.6 3.7 %ladder.5.kept = f32[4,128,128]{2,1,0:T(8,128)S(1)} custom-call(s32[16,48]{1,0:T(8,128)S(4)} %get-tuple-element.11.refs_0_, bf16[4,128,128]{2,1,0:T(8,128)(2,1)S(1)} %copy-done, bf16[4,128,128]{2,1,0:T(8,128)(2,1)S(1)} %collective-permute-done.refs_2_, bf16[128,128,128]{2,1,0:T(8,128)(2,1)S(1)} %get-tuple-element.12.refs_3_, ...), custom_call_target="tpu_custom_call" | custom-call | flops 1048576 | bytes 1024 | tf_op jit(solution)/shard_map/ladder/pallas_call | solution.py:273
  17.3 0.0 collective-permute-done.1.received
  17.3 0.1 merge_layers.4
  17.3 4.7 %collective-permute-start.2 = (bf16[272,128]{1,0:T(8,128)(2,1)S(1)}, bf16[272,128]{1,0:T(8,128)(2,1)S(1)}, u32[]{:S(2)}, u32[]{:S(2)}) collective-permute-start(bf16[272,128]{1,0:T(8,128)(2,1)S(1)} %get-tuple-element.15.refs_5_), channel_id=1, source_target_pairs={{0,7},{1,6},{2,5},{3,4},{4,3},{5,2},{6,1},{7,0},{16,22},{17,23},{1... | collective-permute-start | bytes 208904 | tf_op jit(solution)/shard_map/ppermute | solution.py:310
  22.1 0.0 collective-permute-start.3
  22.1 2.6 %ladder.6.kept = f32[3,128,128]{2,1,0:T(8,128)S(1)} custom-call(s32[16,48]{1,0:T(8,128)S(4)} %get-tuple-element.11.refs_0_, bf16[4,128,128]{2,1,0:T(8,128)(2,1)S(1)} %copy-done, bf16[4,128,128]{2,1,0:T(8,128)(2,1)S(1)} %collective-permute-done.refs_2_, bf16[128,128,128]{2,1,0:T(8,128)(2,1)S(1)} %get-tuple-element.12.refs_3_, ...), custom_call_target="tpu_custom_call" | custom-call | flops 1048576 | bytes 1024 | tf_op jit(solution)/shard_map/ladder/pallas_call | solution.py:273
  24.7 1.7 %collective-permute-start.4 = (bf16[272,128]{1,0:T(8,128)(2,1)S(1)}, bf16[272,128]{1,0:T(8,128)(2,1)S(1)}, u32[]{:S(2)}, u32[]{:S(2)}) collective-permute-start(bf16[272,128]{1,0:T(8,128)(2,1)S(1)} %merge_layers.5.refs_5_), channel_id=1, source_target_pairs={{0,3},{1,2},{2,1},{3,0},{4,7},{5,6},{6,5},{7,4},{16,18},{17,19},{1... | collective-permute-start | bytes 208904 | tf_op jit(solution)/shard_map/ppermute | solution.py:310
  26.5 0.5 %collective-permute-start.5 = (bf16[144,128]{1,0:T(8,128)(2,1)S(1)}, bf16[144,128]{1,0:T(8,128)(2,1)S(1)}, u32[]{:S(2)}, u32[]{:S(2)}) collective-permute-start(bf16[144,128]{1,0:T(8,128)(2,1)S(1)} %merge_layers.6.refs_6_), channel_id=1, source_target_pairs={{0,1},{1,0},{2,3},{3,2},{4,5},{5,4},{6,7},{7,6},{16,17},{17,16},{1... | collective-permute-start | bytes 110600 | tf_op jit(solution)/shard_map/ppermute | solution.py:310
  27.0 1.0 %ladder.7.kept = f32[1,128,128]{2,1,0:T(8,128)S(1)} custom-call(s32[16,48]{1,0:T(8,128)S(4)} %get-tuple-element.11.refs_0_, bf16[4,128,128]{2,1,0:T(8,128)(2,1)S(1)} %copy-done, bf16[4,128,128]{2,1,0:T(8,128)(2,1)S(1)} %collective-permute-done.refs_2_, bf16[128,128,128]{2,1,0:T(8,128)(2,1)S(1)} %get-tuple-element.12.refs_3_, ...), custom_call_target="tpu_custom_call" | custom-call | flops 1048576 | bytes 1024 | tf_op jit(solution)/shard_map/ladder/pallas_call | solution.py:273
  28.0 2.5 %collective-permute-done.5.refs_3_ = bf16[144,128]{1,0:T(8,128)(2,1)S(1)} collective-permute-done((bf16[144,128]{1,0:T(8,128)(2,1)S(1)}, bf16[144,128]{1,0:T(8,128)(2,1)S(1)}, u32[]{:S(2)}, u32[]{:S(2)}) %collective-permute-start.5) | collective-permute-done | bytes 36896 | tf_op jit(solution)/shard_map/ppermute | solution.py:310
  30.5 0.0 collective-permute-done.2.refs_0_
  30.5 0.0 collective-permute-done.3.refs_1_
  30.5 0.0 collective-permute-done.4.refs_2_
  30.6 0.1 collective-permute-start.6
  30.6 0.3 near_owner_sum.1.near_sum
  31.0 1.2 %collective-permute-done.6.far = bf16[1104,128]{1,0:T(8,128)(2,1)S(1)} collective-permute-done((bf16[1104,128]{1,0:T(8,128)(2,1)S(1)}, bf16[1104,128]{1,0:T(8,128)(2,1)S(1)}, u32[]{:S(2)}, u32[]{:S(2)}) %collective-permute-start.6) | collective-permute-done | bytes 282656 | tf_op jit(solution)/shard_map/ppermute | solution.py:254
  32.2 1.0 %last_owner_sum.1 = f32[8,128,128]{2,1,0:T(8,128)} custom-call(f32[8,128,128]{2,1,0:T(8,128)S(1)} %near_owner_sum.1.near_sum, bf16[1104,128]{1,0:T(8,128)(2,1)S(1)} %collective-permute-done.6.far), custom_call_target="tpu_custom_call" | custom-call | flops 1048576 | bytes 1024 | tf_op jit(solution)/shard_map/last_owner_sum/pallas_call | solution.py:326
  (4 shorter events, 0.1 us)
Async XLA Ops:
  0.0 6.7 %copy-start = (bf16[4,128,128]{2,1,0:T(8,128)(2,1)S(1)}, bf16[4,128,128]{2,1,0:T(8,128)(2,1)}, u32[]{:S(2)}) copy-start(bf16[4,128,128]{2,1,0:T(8,128)(2,1)} %refs_1_.7) | copy-start | bytes 393220
  0.0 6.7 %collective-permute-start = (bf16[4,128,128]{2,1,0:T(8,128)(2,1)}, bf16[4,128,128]{2,1,0:T(8,128)(2,1)S(1)}, u32[]{:S(2)}, u32[]{:S(2)}) collective-permute-start(bf16[4,128,128]{2,1,0:T(8,128)(2,1)} %refs_1_.7), channel_id=1, source_target_pairs={{0,8},{8,0},{1,9},{9,1},{2,10},{10,2},{3,11},{11,3},{4,12},{12,4},... | collective-permute-start | bytes 393224 | tf_op jit(solution)/shard_map/ppermute | solution.py:254
  13.5 3.8 %collective-permute-start.1 = (f32[8,128,128]{2,1,0:T(8,128)S(1)}, f32[8,128,128]{2,1,0:T(8,128)S(1)}, u32[]{:S(2)}, u32[]{:S(2)}) collective-permute-start(f32[8,128,128]{2,1,0:T(8,128)S(1)} %ladder.4.refs_5_), channel_id=1, source_target_pairs={{0,16},{16,0},{1,17},{17,1},{2,18},{18,2},{3,19},{19,3},{4,20},{20... | collective-permute-start | bytes 1572872 | tf_op jit(solution)/shard_map/ppermute | solution.py:254
  17.3 13.2 %collective-permute-start.2 = (bf16[272,128]{1,0:T(8,128)(2,1)S(1)}, bf16[272,128]{1,0:T(8,128)(2,1)S(1)}, u32[]{:S(2)}, u32[]{:S(2)}) collective-permute-start(bf16[272,128]{1,0:T(8,128)(2,1)S(1)} %get-tuple-element.15.refs_5_), channel_id=1, source_target_pairs={{0,7},{1,6},{2,5},{3,4},{4,3},{5,2},{6,1},{7,0},{16,22},{17,23},{1... | collective-permute-start | bytes 208904 | tf_op jit(solution)/shard_map/ppermute | solution.py:310
  22.1 8.5 %collective-permute-start.3 = (bf16[272,128]{1,0:T(8,128)(2,1)S(1)}, bf16[272,128]{1,0:T(8,128)(2,1)S(1)}, u32[]{:S(2)}, u32[]{:S(2)}) collective-permute-start(bf16[272,128]{1,0:T(8,128)(2,1)S(1)} %get-tuple-element.16.refs_6_), channel_id=1, source_target_pairs={{0,5},{1,4},{2,7},{3,6},{4,1},{5,0},{6,3},{7,2},{16,20},{17,21},{1... | collective-permute-start | bytes 208904 | tf_op jit(solution)/shard_map/ppermute | solution.py:310
  24.7 5.8 %collective-permute-start.4 = (bf16[272,128]{1,0:T(8,128)(2,1)S(1)}, bf16[272,128]{1,0:T(8,128)(2,1)S(1)}, u32[]{:S(2)}, u32[]{:S(2)}) collective-permute-start(bf16[272,128]{1,0:T(8,128)(2,1)S(1)} %merge_layers.5.refs_5_), channel_id=1, source_target_pairs={{0,3},{1,2},{2,1},{3,0},{4,7},{5,6},{6,5},{7,4},{16,18},{17,19},{1... | collective-permute-start | bytes 208904 | tf_op jit(solution)/shard_map/ppermute | solution.py:310
  26.5 4.0 %collective-permute-start.5 = (bf16[144,128]{1,0:T(8,128)(2,1)S(1)}, bf16[144,128]{1,0:T(8,128)(2,1)S(1)}, u32[]{:S(2)}, u32[]{:S(2)}) collective-permute-start(bf16[144,128]{1,0:T(8,128)(2,1)S(1)} %merge_layers.6.refs_6_), channel_id=1, source_target_pairs={{0,1},{1,0},{2,3},{3,2},{4,5},{5,4},{6,7},{7,6},{16,17},{17,16},{1... | collective-permute-start | bytes 110600 | tf_op jit(solution)/shard_map/ppermute | solution.py:310
  30.6 1.6 %collective-permute-start.6 = (bf16[1104,128]{1,0:T(8,128)(2,1)S(1)}, bf16[1104,128]{1,0:T(8,128)(2,1)S(1)}, u32[]{:S(2)}, u32[]{:S(2)}) collective-permute-start(bf16[1104,128]{1,0:T(8,128)(2,1)S(1)} %join_packs.1.near), channel_id=1, source_target_pairs={{0,16},{16,0},{1,17},{17,1},{2,18},{18,2},{3,19},{19,3},{4,20},{20... | collective-permute-start | bytes 847880 | tf_op jit(solution)/shard_map/ppermute | solution.py:254

commit v7 on v6

--- a/solution.py
+++ b/solution.py
@@ -41,10 +41,6 @@
 
 def round_slots(pair):
     return [tuple(offset * CAP + rank for offset in pair) for rank in range(CAP)]
-
-
-def late_slots():
-    return [tuple(offset * CAP + rank for rank in range(CAP)) for offset in (1, 0)]
 
 
 def prepare_kernel(
@@ -183,12 +179,19 @@
         packed[CAP * edge :] = label_blocks[pick(pair, layer)].astype(BF16)
 
 
-def late_merge_kernel(offset, kept_at, received_at, kept, received, label_blocks, packed):
+def neighbour_merge_kernel(kept_at, received_at, kept, received, label_blocks, packed):
     edge = kept.shape[1]
     spot = pl.ds(pl.multiple_of(lax.axis_index("layer") * LABEL_ROWS, LABEL_ROWS), LABEL_ROWS)
-    labels = label_blocks[offset, spot, :]
+    labels = label_blocks[1, spot, :]
     packed[:edge] = (kept[kept_at] + received[received_at]).astype(BF16)
     packed[edge:] = jnp.concatenate([labels] * CAP, axis=0).astype(BF16)
+
+
+def local_kernel(kept, label_blocks, packed):
+    edge = kept.shape[1]
+    for rank in range(CAP):
+        packed[rank * edge : (rank + 1) * edge] = kept[rank].astype(BF16)
+    packed[CAP * edge :] = label_blocks[0].astype(BF16)
 
 
 def join_kernel(*refs):
@@ -334,30 +337,30 @@
             name="last_owner_sum",
         )(*[in_vmem(array) for array in arrays])
 
-    pairs = [(d, d - 1) for d in range(columns - 1, 2, -2)]
+    pairs = [(d - 1, d) for d in range(columns - 1, 2, -2)]
     slots = sum([round_slots(pair) for pair in pairs], [])
-    neighbour, local = late_slots()
+    neighbour = tuple(CAP + rank for rank in range(CAP))
     split = len(slots) - CAP
-    pair_rows, late_rows = CAP * (edge + LABEL_ROWS), edge + CAP * LABEL_ROWS
+    pair_rows, half_rows = CAP * (edge + LABEL_ROWS), edge + CAP * LABEL_ROWS
 
     def merge_pairs(first, group, kept):
         kernel = functools.partial(merge_kernel, group, first)
         return merge(kernel, pair_rows, len(group), kept, received, label_blocks)
 
-    def merge_late(offset, kept_at, kept):
-        kernel = functools.partial(late_merge_kernel, offset, kept_at, len(slots) + 1 - offset)
-        return merge(kernel, late_rows, 1, kept, received, label_blocks)
-
-    (sent,) = ladder([], slots + [neighbour, local], [])
+    (sent,) = ladder([], slots + [neighbour], [])
     received = swap(sent, "layer")
     (kept,) = ladder(slots[:split], [], [sent])
     packs = merge_pairs(0, pairs[:-1], kept)
     near = [send(pair, pack) for pair, pack in zip(pairs, packs)]
+
     (kept,) = ladder(slots[split:] + [neighbour], [], packs)
-    packs = merge_pairs(len(pairs) - 1, pairs[-1:], kept) + merge_late(1, CAP, kept)
+    kernel = functools.partial(neighbour_merge_kernel, CAP, len(slots))
+    packs = merge_pairs(len(pairs) - 1, pairs[-1:], kept)
+    packs += merge(kernel, half_rows, 1, kept, received, label_blocks)
     near += [send(pair, pack) for pair, pack in zip([pairs[-1], (1, 1)], packs)]
-    (kept,) = ladder([local], [], packs)
-    near += merge_late(0, 0, kept)
+
+    (kept,) = ladder(round_slots((0, 0)), [], packs)
+    near += merge(local_kernel, pair_rows, 1, kept, label_blocks)
 
     sizes = [pack.shape[0] for pack in near]
     joined = join(*near)

time: 33.5 us -> 31.6 us (0.943)
  waiting for transfers between devices: 4.72 us -> 3.18 us
  starting transfers between devices: 10.1 us -> 9.65 us
    ppermute x4, waiting for transfers between devices: 2.51 us -> 1.28 us  [send(): return lax.ppermute(pack, ('layer', 'col'), route)]
    ppermute x4, starting transfers between devices: 6.97 us -> 6.21 us  [send(): return lax.ppermute(pack, ('layer', 'col'), route)]
  transfers between devices with their start and end apart: 7 -> 7, of which waited for: 3 -> 4; matrix products, arithmetic and copies ran while one was open for 0% -> 0% of each run, Pallas kernels for 31% -> 36%
where the time goes in v7:
time: 31.6 us; the launch traced here: 31.5 us
  Pallas kernels  18.4 us (58%)
  starting transfers between devices  9.65 us (31%)
  waiting for transfers between devices  3.18 us (10%)
    pallas_call x4, Pallas kernels, ladder(): pl.pallas_call(functools.partial(ladder_kernel, bits, keeps, sends, len(a...  14.1 us
    ppermute x4, starting transfers between devices, send(): return lax.ppermute(pack, ('layer', 'col'), route)  6.21 us
    ppermute x3, starting transfers between devices, swap(): return lax.ppermute(array, axis, [(i, i ^ 1) for i in range(size)])  3.43 us
    pallas_call x1, Pallas kernels, prepare(): pl.pallas_call(functools.partial(prepare_kernel, bits), out_shape=(held(s...  2.79 us
    ppermute x3, waiting for transfers between devices, swap(): return lax.ppermute(array, axis, [(i, i ^ 1) for i in range(size)])  1.9 us
    ppermute x4, waiting for transfers between devices, send(): return lax.ppermute(pack, ('layer', 'col'), route)  1.28 us
    pallas_call x1, Pallas kernels, last_owner_sum(): pl.pallas_call(functools.partial(last_owner_kernel, sizes), out_shape=jax...  1.06 us
  transfers between devices with their start and end apart: 7, of which 4 were waited for; matrix products, arithmetic and copies ran while one was open for 0% of the time, Pallas kernels for 36%

profile of v7, /device:TPU:0, one launch (start us, length us, event | category | flops | bytes accessed | tf_op | source)
XLA Modules:
  0.0 31.5 jit_solution(7849294365365245144)
XLA Ops:
  0.0 0.0 copy-start
  0.0 3.0 %collective-permute-start = (bf16[4,128,128]{2,1,0:T(8,128)(2,1)}, bf16[4,128,128]{2,1,0:T(8,128)(2,1)S(1)}, u32[]{:S(2)}, u32[]{:S(2)}) collective-permute-start(bf16[4,128,128]{2,1,0:T(8,128)(2,1)} %refs_1_.7), channel_id=1, source_target_pairs={{0,8},{8,0},{1,9},{9,1},{2,10},{10,2},{3,11},{11,3},{4,12},{12,4},... | collective-permute-start | bytes 393224 | tf_op jit(solution)/shard_map/ppermute | solution.py:257
  3.0 2.8 %load_and_flip.1 = (bf16[128,128,128]{2,1,0:T(8,128)(2,1)S(1)}, bf16[128,128,128]{2,1,0:T(8,128)(2,1)S(1)}, s32[16,48]{1,0:T(8,128)S(4)}, f32[8,16,128]{2,1,0:T(8,128)S(1)}) custom-call(bf16[128,128,128]{2,1,0:T(8,128)(2,1)} %source.1, s32[16,48]{1,0:T(8,128)} %amp_ids.1, s32[16,48]{1,0:T(8,128)} %left_ids.1, s32[16,48]{1,0:T(8,128)} %right_ids.1, ...), custom_call_target="tpu_custom_call" | custom-call | flops 1048576 | bytes 1024 | tf_op jit(solution)/shard_map/load_and_flip/pallas_call | solution.py:107
  5.8 1.0 %collective-permute-done.refs_2_ = bf16[4,128,128]{2,1,0:T(8,128)(2,1)S(1)} collective-permute-done((bf16[4,128,128]{2,1,0:T(8,128)(2,1)}, bf16[4,128,128]{2,1,0:T(8,128)(2,1)S(1)}, u32[]{:S(2)}, u32[]{:S(2)}) %collective-permute-start) | collective-permute-done | bytes 131104 | tf_op jit(solution)/shard_map/ppermute | solution.py:257
  6.7 0.0 copy-done
  6.7 5.9 %ladder.4.refs_5_ = f32[7,128,128]{2,1,0:T(8,128)S(1)} custom-call(s32[16,48]{1,0:T(8,128)S(4)} %get-tuple-element.11.refs_0_, bf16[4,128,128]{2,1,0:T(8,128)(2,1)S(1)} %copy-done, bf16[4,128,128]{2,1,0:T(8,128)(2,1)S(1)} %collective-permute-done.refs_2_, bf16[128,128,128]{2,1,0:T(8,128)(2,1)S(1)} %get-tuple-element.12.refs_3_, ...), custom_call_target="tpu_custom_call" | custom-call | flops 1048576 | bytes 1024 | tf_op jit(solution)/shard_map/ladder/pallas_call | solution.py:276
  12.7 0.1 collective-permute-start.1
  12.8 3.5 %ladder.5.kept = f32[4,128,128]{2,1,0:T(8,128)S(1)} custom-call(s32[16,48]{1,0:T(8,128)S(4)} %get-tuple-element.11.refs_0_, bf16[4,128,128]{2,1,0:T(8,128)(2,1)S(1)} %copy-done, bf16[4,128,128]{2,1,0:T(8,128)(2,1)S(1)} %collective-permute-done.refs_2_, bf16[128,128,128]{2,1,0:T(8,128)(2,1)S(1)} %get-tuple-element.12.refs_3_, ...), custom_call_target="tpu_custom_call" | custom-call | flops 1048576 | bytes 1024 | tf_op jit(solution)/shard_map/ladder/pallas_call | solution.py:276
  16.2 0.0 collective-permute-done.1.received
  16.2 0.1 merge_layers.4
  16.3 3.8 %collective-permute-start.2 = (bf16[272,128]{1,0:T(8,128)(2,1)S(1)}, bf16[272,128]{1,0:T(8,128)(2,1)S(1)}, u32[]{:S(2)}, u32[]{:S(2)}) collective-permute-start(bf16[272,128]{1,0:T(8,128)(2,1)S(1)} %get-tuple-element.15.refs_5_), channel_id=1, source_target_pairs={{0,6},{1,7},{2,4},{3,5},{4,2},{5,3},{6,0},{7,1},{16,23},{17,22},{1... | collective-permute-start | bytes 208904 | tf_op jit(solution)/shard_map/ppermute | solution.py:313
  20.1 0.0 collective-permute-start.3
  20.1 2.8 %ladder.6.kept = f32[3,128,128]{2,1,0:T(8,128)S(1)} custom-call(s32[16,48]{1,0:T(8,128)S(4)} %get-tuple-element.11.refs_0_, bf16[4,128,128]{2,1,0:T(8,128)(2,1)S(1)} %copy-done, bf16[4,128,128]{2,1,0:T(8,128)(2,1)S(1)} %collective-permute-done.refs_2_, bf16[128,128,128]{2,1,0:T(8,128)(2,1)S(1)} %get-tuple-element.12.refs_3_, ...), custom_call_target="tpu_custom_call" | custom-call | flops 1048576 | bytes 1024 | tf_op jit(solution)/shard_map/ladder/pallas_call | solution.py:276
  23.0 0.7 %collective-permute-start.4 = (bf16[272,128]{1,0:T(8,128)(2,1)S(1)}, bf16[272,128]{1,0:T(8,128)(2,1)S(1)}, u32[]{:S(2)}, u32[]{:S(2)}) collective-permute-start(bf16[272,128]{1,0:T(8,128)(2,1)S(1)} %merge_layers.5.refs_5_), channel_id=1, source_target_pairs={{0,2},{1,3},{2,0},{3,1},{4,6},{5,7},{6,4},{7,5},{16,19},{17,18},{1... | collective-permute-start | bytes 208904 | tf_op jit(solution)/shard_map/ppermute | solution.py:313
  23.7 1.7 %collective-permute-start.5 = (bf16[144,128]{1,0:T(8,128)(2,1)S(1)}, bf16[144,128]{1,0:T(8,128)(2,1)S(1)}, u32[]{:S(2)}, u32[]{:S(2)}) collective-permute-start(bf16[144,128]{1,0:T(8,128)(2,1)S(1)} %merge_layers.6.refs_6_), channel_id=1, source_target_pairs={{0,1},{1,0},{2,3},{3,2},{4,5},{5,4},{6,7},{7,6},{16,17},{17,16},{1... | collective-permute-start | bytes 110600 | tf_op jit(solution)/shard_map/ppermute | solution.py:313
  25.4 1.8 %ladder.7.kept = f32[2,128,128]{2,1,0:T(8,128)S(1)} custom-call(s32[16,48]{1,0:T(8,128)S(4)} %get-tuple-element.11.refs_0_, bf16[4,128,128]{2,1,0:T(8,128)(2,1)S(1)} %copy-done, bf16[4,128,128]{2,1,0:T(8,128)(2,1)S(1)} %collective-permute-done.refs_2_, bf16[128,128,128]{2,1,0:T(8,128)(2,1)S(1)} %get-tuple-element.12.refs_3_, ...), custom_call_target="tpu_custom_call" | custom-call | flops 1048576 | bytes 1024 | tf_op jit(solution)/shard_map/ladder/pallas_call | solution.py:276
  27.2 0.7 %collective-permute-done.5.refs_3_ = bf16[144,128]{1,0:T(8,128)(2,1)S(1)} collective-permute-done((bf16[144,128]{1,0:T(8,128)(2,1)S(1)}, bf16[144,128]{1,0:T(8,128)(2,1)S(1)}, u32[]{:S(2)}, u32[]{:S(2)}) %collective-permute-start.5) | collective-permute-done | bytes 36896 | tf_op jit(solution)/shard_map/ppermute | solution.py:313
  27.9 0.0 collective-permute-done.2.refs_0_
  27.9 0.0 collective-permute-done.3.refs_1_
  27.9 0.6 %collective-permute-done.4.refs_2_ = bf16[272,128]{1,0:T(8,128)(2,1)S(1)} collective-permute-done((bf16[272,128]{1,0:T(8,128)(2,1)S(1)}, bf16[272,128]{1,0:T(8,128)(2,1)S(1)}, u32[]{:S(2)}, u32[]{:S(2)}) %collective-permute-start.4) | collective-permute-done | bytes 69664 | tf_op jit(solution)/shard_map/ppermute | solution.py:313
  28.6 0.4 %collective-permute-start.6 = (bf16[1232,128]{1,0:T(8,128)(2,1)S(1)}, bf16[1232,128]{1,0:T(8,128)(2,1)S(1)}, u32[]{:S(2)}, u32[]{:S(2)}) collective-permute-start(bf16[1232,128]{1,0:T(8,128)(2,1)S(1)} %join_packs.1.near), channel_id=1, source_target_pairs={{0,16},{16,0},{1,17},{17,1},{2,18},{18,2},{3,19},{19,3},{4,20},{20... | collective-permute-start | bytes 946184 | tf_op jit(solution)/shard_map/ppermute | solution.py:257
  28.9 0.4 %near_owner_sum.1.near_sum = f32[8,128,128]{2,1,0:T(8,128)S(1)} custom-call(bf16[1232,128]{1,0:T(8,128)(2,1)S(1)} %join_packs.1.near), custom_call_target="tpu_custom_call" | custom-call | flops 1048576 | bytes 1024 | tf_op jit(solution)/shard_map/near_owner_sum/pallas_call | solution.py:318
  29.3 0.9 %collective-permute-done.6.far = bf16[1232,128]{1,0:T(8,128)(2,1)S(1)} collective-permute-done((bf16[1232,128]{1,0:T(8,128)(2,1)S(1)}, bf16[1232,128]{1,0:T(8,128)(2,1)S(1)}, u32[]{:S(2)}, u32[]{:S(2)}) %collective-permute-start.6) | collective-permute-done | bytes 315424 | tf_op jit(solution)/shard_map/ppermute | solution.py:257
  30.2 1.1 %last_owner_sum.1 = f32[8,128,128]{2,1,0:T(8,128)} custom-call(f32[8,128,128]{2,1,0:T(8,128)S(1)} %near_owner_sum.1.near_sum, bf16[1232,128]{1,0:T(8,128)(2,1)S(1)} %collective-permute-done.6.far), custom_call_target="tpu_custom_call" | custom-call | flops 1048576 | bytes 1024 | tf_op jit(solution)/shard_map/last_owner_sum/pallas_call | solution.py:329
  (4 shorter events, 0.1 us)
Async XLA Ops:
  0.0 6.7 %copy-start = (bf16[4,128,128]{2,1,0:T(8,128)(2,1)S(1)}, bf16[4,128,128]{2,1,0:T(8,128)(2,1)}, u32[]{:S(2)}) copy-start(bf16[4,128,128]{2,1,0:T(8,128)(2,1)} %refs_1_.7) | copy-start | bytes 393220
  0.0 6.7 %collective-permute-start = (bf16[4,128,128]{2,1,0:T(8,128)(2,1)}, bf16[4,128,128]{2,1,0:T(8,128)(2,1)S(1)}, u32[]{:S(2)}, u32[]{:S(2)}) collective-permute-start(bf16[4,128,128]{2,1,0:T(8,128)(2,1)} %refs_1_.7), channel_id=1, source_target_pairs={{0,8},{8,0},{1,9},{9,1},{2,10},{10,2},{3,11},{11,3},{4,12},{12,4},... | collective-permute-start | bytes 393224 | tf_op jit(solution)/shard_map/ppermute | solution.py:257
  12.7 3.5 %collective-permute-start.1 = (f32[7,128,128]{2,1,0:T(8,128)S(1)}, f32[7,128,128]{2,1,0:T(8,128)S(1)}, u32[]{:S(2)}, u32[]{:S(2)}) collective-permute-start(f32[7,128,128]{2,1,0:T(8,128)S(1)} %ladder.4.refs_5_), channel_id=1, source_target_pairs={{0,16},{16,0},{1,17},{17,1},{2,18},{18,2},{3,19},{19,3},{4,20},{20... | collective-permute-start | bytes 1376264 | tf_op jit(solution)/shard_map/ppermute | solution.py:257
  16.3 11.6 %collective-permute-start.2 = (bf16[272,128]{1,0:T(8,128)(2,1)S(1)}, bf16[272,128]{1,0:T(8,128)(2,1)S(1)}, u32[]{:S(2)}, u32[]{:S(2)}) collective-permute-start(bf16[272,128]{1,0:T(8,128)(2,1)S(1)} %get-tuple-element.15.refs_5_), channel_id=1, source_target_pairs={{0,6},{1,7},{2,4},{3,5},{4,2},{5,3},{6,0},{7,1},{16,23},{17,22},{1... | collective-permute-start | bytes 208904 | tf_op jit(solution)/shard_map/ppermute | solution.py:313
  20.1 7.8 %collective-permute-start.3 = (bf16[272,128]{1,0:T(8,128)(2,1)S(1)}, bf16[272,128]{1,0:T(8,128)(2,1)S(1)}, u32[]{:S(2)}, u32[]{:S(2)}) collective-permute-start(bf16[272,128]{1,0:T(8,128)(2,1)S(1)} %get-tuple-element.16.refs_6_), channel_id=1, source_target_pairs={{0,4},{1,5},{2,6},{3,7},{4,0},{5,1},{6,2},{7,3},{16,21},{17,20},{1... | collective-permute-start | bytes 208904 | tf_op jit(solution)/shard_map/ppermute | solution.py:313
  23.0 5.5 %collective-permute-start.4 = (bf16[272,128]{1,0:T(8,128)(2,1)S(1)}, bf16[272,128]{1,0:T(8,128)(2,1)S(1)}, u32[]{:S(2)}, u32[]{:S(2)}) collective-permute-start(bf16[272,128]{1,0:T(8,128)(2,1)S(1)} %merge_layers.5.refs_5_), channel_id=1, source_target_pairs={{0,2},{1,3},{2,0},{3,1},{4,6},{5,7},{6,4},{7,5},{16,19},{17,18},{1... | collective-permute-start | bytes 208904 | tf_op jit(solution)/shard_map/ppermute | solution.py:313
  23.7 4.2 %collective-permute-start.5 = (bf16[144,128]{1,0:T(8,128)(2,1)S(1)}, bf16[144,128]{1,0:T(8,128)(2,1)S(1)}, u32[]{:S(2)}, u32[]{:S(2)}) collective-permute-start(bf16[144,128]{1,0:T(8,128)(2,1)S(1)} %merge_layers.6.refs_6_), channel_id=1, source_target_pairs={{0,1},{1,0},{2,3},{3,2},{4,5},{5,4},{6,7},{7,6},{16,17},{17,16},{1... | collective-permute-start | bytes 110600 | tf_op jit(solution)/shard_map/ppermute | solution.py:313
  28.6 1.7 %collective-permute-start.6 = (bf16[1232,128]{1,0:T(8,128)(2,1)S(1)}, bf16[1232,128]{1,0:T(8,128)(2,1)S(1)}, u32[]{:S(2)}, u32[]{:S(2)}) collective-permute-start(bf16[1232,128]{1,0:T(8,128)(2,1)S(1)} %join_packs.1.near), channel_id=1, source_target_pairs={{0,16},{16,0},{1,17},{17,1},{2,18},{18,2},{3,19},{19,3},{4,20},{20... | collective-permute-start | bytes 946184 | tf_op jit(solution)/shard_map/ppermute | solution.py:257

commit v8 on v7

--- a/solution.py
+++ b/solution.py
@@ -353,9 +353,10 @@
     packs = merge_pairs(0, pairs[:-1], kept)
     near = [send(pair, pack) for pair, pack in zip(pairs, packs)]
 
-    (kept,) = ladder(slots[split:] + [neighbour], [], packs)
-    kernel = functools.partial(neighbour_merge_kernel, CAP, len(slots))
+    (kept,) = ladder(slots[split:], [], packs)
     packs = merge_pairs(len(pairs) - 1, pairs[-1:], kept)
+    (kept,) = ladder([neighbour], [], packs)
+    kernel = functools.partial(neighbour_merge_kernel, 0, len(slots))
     packs += merge(kernel, half_rows, 1, kept, received, label_blocks)
     near += [send(pair, pack) for pair, pack in zip([pairs[-1], (1, 1)], packs)]
 

time: 31.6 us -> 31.6 us (level)
    pallas_call x4 -> x5, Pallas kernels: 14.1 us -> 14.2 us  [ladder(): pl.pallas_call(functools.partial(ladder_kernel, bits, keeps, sends, len(a...]
  transfers between devices with their start and end apart: 7 -> 7, of which waited for: 4 -> 3; matrix products, arithmetic and copies ran while one was open for 0% -> 0% of each run, Pallas kernels for 36% -> 37%
where the time goes in v8:
time: 31.6 us; the launch traced here: 31.4 us
  Pallas kernels  18.6 us (59%)
  starting transfers between devices  9.71 us (31%)
  waiting for transfers between devices  2.92 us (9%)
    pallas_call x5, Pallas kernels, ladder(): pl.pallas_call(functools.partial(ladder_kernel, bits, keeps, sends, len(a...  14.2 us
    ppermute x4, starting transfers between devices, send(): return lax.ppermute(pack, ('layer', 'col'), route)  6.22 us
    ppermute x3, starting transfers between devices, swap(): return lax.ppermute(array, axis, [(i, i ^ 1) for i in range(size)])  3.49 us
    pallas_call x1, Pallas kernels, prepare(): pl.pallas_call(functools.partial(prepare_kernel, bits), out_shape=(held(s...  2.79 us
    ppermute x3, waiting for transfers between devices, swap(): return lax.ppermute(array, axis, [(i, i ^ 1) for i in range(size)])  1.86 us
    pallas_call x1, Pallas kernels, last_owner_sum(): pl.pallas_call(functools.partial(last_owner_kernel, sizes), out_shape=jax...  1.06 us
    ppermute x4, waiting for transfers between devices, send(): return lax.ppermute(pack, ('layer', 'col'), route)  1.06 us
  transfers between devices with their start and end apart: 7, of which 3 were waited for; matrix products, arithmetic and copies ran while one was open for 0% of the time, Pallas kernels for 37%

profile of v8, /device:TPU:0, one launch (start us, length us, event | category | flops | bytes accessed | tf_op | source)
XLA Modules:
  0.0 31.4 jit_solution(6790701939850982160)
XLA Ops:
  0.0 0.0 copy-start
  0.0 3.0 %collective-permute-start = (bf16[4,128,128]{2,1,0:T(8,128)(2,1)}, bf16[4,128,128]{2,1,0:T(8,128)(2,1)S(1)}, u32[]{:S(2)}, u32[]{:S(2)}) collective-permute-start(bf16[4,128,128]{2,1,0:T(8,128)(2,1)} %refs_1_.9), channel_id=1, source_target_pairs={{0,8},{8,0},{1,9},{9,1},{2,10},{10,2},{3,11},{11,3},{4,12},{12,4},... | collective-permute-start | bytes 393224 | tf_op jit(solution)/shard_map/ppermute | solution.py:257
  3.0 2.8 %load_and_flip.1 = (bf16[128,128,128]{2,1,0:T(8,128)(2,1)S(1)}, bf16[128,128,128]{2,1,0:T(8,128)(2,1)S(1)}, s32[16,48]{1,0:T(8,128)S(4)}, f32[8,16,128]{2,1,0:T(8,128)S(1)}) custom-call(bf16[128,128,128]{2,1,0:T(8,128)(2,1)} %source.1, s32[16,48]{1,0:T(8,128)} %amp_ids.1, s32[16,48]{1,0:T(8,128)} %left_ids.1, s32[16,48]{1,0:T(8,128)} %right_ids.1, ...), custom_call_target="tpu_custom_call" | custom-call | flops 1048576 | bytes 1024 | tf_op jit(solution)/shard_map/load_and_flip/pallas_call | solution.py:107
  5.8 1.0 %collective-permute-done.refs_2_ = bf16[4,128,128]{2,1,0:T(8,128)(2,1)S(1)} collective-permute-done((bf16[4,128,128]{2,1,0:T(8,128)(2,1)}, bf16[4,128,128]{2,1,0:T(8,128)(2,1)S(1)}, u32[]{:S(2)}, u32[]{:S(2)}) %collective-permute-start) | collective-permute-done | bytes 131104 | tf_op jit(solution)/shard_map/ppermute | solution.py:257
  6.7 0.0 copy-done
  6.7 5.9 %ladder.5.refs_5_ = f32[7,128,128]{2,1,0:T(8,128)S(1)} custom-call(s32[16,48]{1,0:T(8,128)S(4)} %get-tuple-element.11.refs_0_, bf16[4,128,128]{2,1,0:T(8,128)(2,1)S(1)} %copy-done, bf16[4,128,128]{2,1,0:T(8,128)(2,1)S(1)} %collective-permute-done.refs_2_, bf16[128,128,128]{2,1,0:T(8,128)(2,1)S(1)} %get-tuple-element.12.refs_3_, ...), custom_call_target="tpu_custom_call" | custom-call | flops 1048576 | bytes 1024 | tf_op jit(solution)/shard_map/ladder/pallas_call | solution.py:276
  12.7 0.1 collective-permute-start.1
  12.8 3.5 %ladder.6.kept = f32[4,128,128]{2,1,0:T(8,128)S(1)} custom-call(s32[16,48]{1,0:T(8,128)S(4)} %get-tuple-element.11.refs_0_, bf16[4,128,128]{2,1,0:T(8,128)(2,1)S(1)} %copy-done, bf16[4,128,128]{2,1,0:T(8,128)(2,1)S(1)} %collective-permute-done.refs_2_, bf16[128,128,128]{2,1,0:T(8,128)(2,1)S(1)} %get-tuple-element.12.refs_3_, ...), custom_call_target="tpu_custom_call" | custom-call | flops 1048576 | bytes 1024 | tf_op jit(solution)/shard_map/ladder/pallas_call | solution.py:276
  16.2 0.0 collective-permute-done.1.received
  16.2 0.1 merge_layers.4
  16.3 3.8 %collective-permute-start.2 = (bf16[272,128]{1,0:T(8,128)(2,1)S(1)}, bf16[272,128]{1,0:T(8,128)(2,1)S(1)}, u32[]{:S(2)}, u32[]{:S(2)}) collective-permute-start(bf16[272,128]{1,0:T(8,128)(2,1)S(1)} %get-tuple-element.15.refs_5_), channel_id=1, source_target_pairs={{0,6},{1,7},{2,4},{3,5},{4,2},{5,3},{6,0},{7,1},{16,23},{17,22},{1... | collective-permute-start | bytes 208904 | tf_op jit(solution)/shard_map/ppermute | solution.py:313
  20.1 0.0 collective-permute-start.3
  20.1 2.0 %ladder.7.kept = f32[2,128,128]{2,1,0:T(8,128)S(1)} custom-call(s32[16,48]{1,0:T(8,128)S(4)} %get-tuple-element.11.refs_0_, bf16[4,128,128]{2,1,0:T(8,128)(2,1)S(1)} %copy-done, bf16[4,128,128]{2,1,0:T(8,128)(2,1)S(1)} %collective-permute-done.refs_2_, bf16[128,128,128]{2,1,0:T(8,128)(2,1)S(1)} %get-tuple-element.12.refs_3_, ...), custom_call_target="tpu_custom_call" | custom-call | flops 1048576 | bytes 1024 | tf_op jit(solution)/shard_map/ladder/pallas_call | solution.py:276
  22.2 0.7 %collective-permute-start.4 = (bf16[272,128]{1,0:T(8,128)(2,1)S(1)}, bf16[272,128]{1,0:T(8,128)(2,1)S(1)}, u32[]{:S(2)}, u32[]{:S(2)}) collective-permute-start(bf16[272,128]{1,0:T(8,128)(2,1)S(1)} %merge_layers.5.refs_5_), channel_id=1, source_target_pairs={{0,2},{1,3},{2,0},{3,1},{4,6},{5,7},{6,4},{7,5},{16,19},{17,18},{1... | collective-permute-start | bytes 208904 | tf_op jit(solution)/shard_map/ppermute | solution.py:313
  22.9 1.0 %ladder.8.kept = f32[1,128,128]{2,1,0:T(8,128)S(1)} custom-call(s32[16,48]{1,0:T(8,128)S(4)} %get-tuple-element.11.refs_0_, bf16[4,128,128]{2,1,0:T(8,128)(2,1)S(1)} %copy-done, bf16[4,128,128]{2,1,0:T(8,128)(2,1)S(1)} %collective-permute-done.refs_2_, bf16[128,128,128]{2,1,0:T(8,128)(2,1)S(1)} %get-tuple-element.12.refs_3_, ...), custom_call_target="tpu_custom_call" | custom-call | flops 1048576 | bytes 1024 | tf_op jit(solution)/shard_map/ladder/pallas_call | solution.py:276
  23.9 1.7 %collective-permute-start.5 = (bf16[144,128]{1,0:T(8,128)(2,1)S(1)}, bf16[144,128]{1,0:T(8,128)(2,1)S(1)}, u32[]{:S(2)}, u32[]{:S(2)}) collective-permute-start(bf16[144,128]{1,0:T(8,128)(2,1)S(1)} %merge_layers.6.refs_6_), channel_id=1, source_target_pairs={{0,1},{1,0},{2,3},{3,2},{4,5},{5,4},{6,7},{7,6},{16,17},{17,16},{1... | collective-permute-start | bytes 110600 | tf_op jit(solution)/shard_map/ppermute | solution.py:313
  25.6 1.8 %ladder.9.kept = f32[2,128,128]{2,1,0:T(8,128)S(1)} custom-call(s32[16,48]{1,0:T(8,128)S(4)} %get-tuple-element.11.refs_0_, bf16[4,128,128]{2,1,0:T(8,128)(2,1)S(1)} %copy-done, bf16[4,128,128]{2,1,0:T(8,128)(2,1)S(1)} %collective-permute-done.refs_2_, bf16[128,128,128]{2,1,0:T(8,128)(2,1)S(1)} %get-tuple-element.12.refs_3_, ...), custom_call_target="tpu_custom_call" | custom-call | flops 1048576 | bytes 1024 | tf_op jit(solution)/shard_map/ladder/pallas_call | solution.py:276
  27.4 1.0 %collective-permute-done.5.refs_3_ = bf16[144,128]{1,0:T(8,128)(2,1)S(1)} collective-permute-done((bf16[144,128]{1,0:T(8,128)(2,1)S(1)}, bf16[144,128]{1,0:T(8,128)(2,1)S(1)}, u32[]{:S(2)}, u32[]{:S(2)}) %collective-permute-start.5) | collective-permute-done | bytes 36896 | tf_op jit(solution)/shard_map/ppermute | solution.py:313
  28.5 0.0 collective-permute-done.2.refs_0_
  28.5 0.0 collective-permute-done.3.refs_1_
  28.5 0.0 collective-permute-done.4.refs_2_
  28.5 0.5 %collective-permute-start.6 = (bf16[1232,128]{1,0:T(8,128)(2,1)S(1)}, bf16[1232,128]{1,0:T(8,128)(2,1)S(1)}, u32[]{:S(2)}, u32[]{:S(2)}) collective-permute-start(bf16[1232,128]{1,0:T(8,128)(2,1)S(1)} %join_packs.1.near), channel_id=1, source_target_pairs={{0,16},{16,0},{1,17},{17,1},{2,18},{18,2},{3,19},{19,3},{4,20},{20... | collective-permute-start | bytes 946184 | tf_op jit(solution)/shard_map/ppermute | solution.py:257
  29.0 0.4 %near_owner_sum.1.near_sum = f32[8,128,128]{2,1,0:T(8,128)S(1)} custom-call(bf16[1232,128]{1,0:T(8,128)(2,1)S(1)} %join_packs.1.near), custom_call_target="tpu_custom_call" | custom-call | flops 1048576 | bytes 1024 | tf_op jit(solution)/shard_map/near_owner_sum/pallas_call | solution.py:318
  29.3 0.9 %collective-permute-done.6.far = bf16[1232,128]{1,0:T(8,128)(2,1)S(1)} collective-permute-done((bf16[1232,128]{1,0:T(8,128)(2,1)S(1)}, bf16[1232,128]{1,0:T(8,128)(2,1)S(1)}, u32[]{:S(2)}, u32[]{:S(2)}) %collective-permute-start.6) | collective-permute-done | bytes 315424 | tf_op jit(solution)/shard_map/ppermute | solution.py:257
  30.2 1.1 %last_owner_sum.1 = f32[8,128,128]{2,1,0:T(8,128)} custom-call(f32[8,128,128]{2,1,0:T(8,128)S(1)} %near_owner_sum.1.near_sum, bf16[1232,128]{1,0:T(8,128)(2,1)S(1)} %collective-permute-done.6.far), custom_call_target="tpu_custom_call" | custom-call | flops 1048576 | bytes 1024 | tf_op jit(solution)/shard_map/last_owner_sum/pallas_call | solution.py:329
  (4 shorter events, 0.1 us)
Async XLA Ops:
  0.0 6.7 %copy-start = (bf16[4,128,128]{2,1,0:T(8,128)(2,1)S(1)}, bf16[4,128,128]{2,1,0:T(8,128)(2,1)}, u32[]{:S(2)}) copy-start(bf16[4,128,128]{2,1,0:T(8,128)(2,1)} %refs_1_.9) | copy-start | bytes 393220
  0.0 6.7 %collective-permute-start = (bf16[4,128,128]{2,1,0:T(8,128)(2,1)}, bf16[4,128,128]{2,1,0:T(8,128)(2,1)S(1)}, u32[]{:S(2)}, u32[]{:S(2)}) collective-permute-start(bf16[4,128,128]{2,1,0:T(8,128)(2,1)} %refs_1_.9), channel_id=1, source_target_pairs={{0,8},{8,0},{1,9},{9,1},{2,10},{10,2},{3,11},{11,3},{4,12},{12,4},... | collective-permute-start | bytes 393224 | tf_op jit(solution)/shard_map/ppermute | solution.py:257
  12.7 3.5 %collective-permute-start.1 = (f32[7,128,128]{2,1,0:T(8,128)S(1)}, f32[7,128,128]{2,1,0:T(8,128)S(1)}, u32[]{:S(2)}, u32[]{:S(2)}) collective-permute-start(f32[7,128,128]{2,1,0:T(8,128)S(1)} %ladder.5.refs_5_), channel_id=1, source_target_pairs={{0,16},{16,0},{1,17},{17,1},{2,18},{18,2},{3,19},{19,3},{4,20},{20... | collective-permute-start | bytes 1376264 | tf_op jit(solution)/shard_map/ppermute | solution.py:257
  16.3 12.2 %collective-permute-start.2 = (bf16[272,128]{1,0:T(8,128)(2,1)S(1)}, bf16[272,128]{1,0:T(8,128)(2,1)S(1)}, u32[]{:S(2)}, u32[]{:S(2)}) collective-permute-start(bf16[272,128]{1,0:T(8,128)(2,1)S(1)} %get-tuple-element.15.refs_5_), channel_id=1, source_target_pairs={{0,6},{1,7},{2,4},{3,5},{4,2},{5,3},{6,0},{7,1},{16,23},{17,22},{1... | collective-permute-start | bytes 208904 | tf_op jit(solution)/shard_map/ppermute | solution.py:313
  20.1 8.4 %collective-permute-start.3 = (bf16[272,128]{1,0:T(8,128)(2,1)S(1)}, bf16[272,128]{1,0:T(8,128)(2,1)S(1)}, u32[]{:S(2)}, u32[]{:S(2)}) collective-permute-start(bf16[272,128]{1,0:T(8,128)(2,1)S(1)} %get-tuple-element.16.refs_6_), channel_id=1, source_target_pairs={{0,4},{1,5},{2,6},{3,7},{4,0},{5,1},{6,2},{7,3},{16,21},{17,20},{1... | collective-permute-start | bytes 208904 | tf_op jit(solution)/shard_map/ppermute | solution.py:313
  22.2 6.3 %collective-permute-start.4 = (bf16[272,128]{1,0:T(8,128)(2,1)S(1)}, bf16[272,128]{1,0:T(8,128)(2,1)S(1)}, u32[]{:S(2)}, u32[]{:S(2)}) collective-permute-start(bf16[272,128]{1,0:T(8,128)(2,1)S(1)} %merge_layers.5.refs_5_), channel_id=1, source_target_pairs={{0,2},{1,3},{2,0},{3,1},{4,6},{5,7},{6,4},{7,5},{16,19},{17,18},{1... | collective-permute-start | bytes 208904 | tf_op jit(solution)/shard_map/ppermute | solution.py:313
  23.9 4.6 %collective-permute-start.5 = (bf16[144,128]{1,0:T(8,128)(2,1)S(1)}, bf16[144,128]{1,0:T(8,128)(2,1)S(1)}, u32[]{:S(2)}, u32[]{:S(2)}) collective-permute-start(bf16[144,128]{1,0:T(8,128)(2,1)S(1)} %merge_layers.6.refs_6_), channel_id=1, source_target_pairs={{0,1},{1,0},{2,3},{3,2},{4,5},{5,4},{6,7},{7,6},{16,17},{17,16},{1... | collective-permute-start | bytes 110600 | tf_op jit(solution)/shard_map/ppermute | solution.py:313
  28.5 1.7 %collective-permute-start.6 = (bf16[1232,128]{1,0:T(8,128)(2,1)S(1)}, bf16[1232,128]{1,0:T(8,128)(2,1)S(1)}, u32[]{:S(2)}, u32[]{:S(2)}) collective-permute-start(bf16[1232,128]{1,0:T(8,128)(2,1)S(1)} %join_packs.1.near), channel_id=1, source_target_pairs={{0,16},{16,0},{1,17},{17,1},{2,18},{18,2},{3,19},{19,3},{4,20},{20... | collective-permute-start | bytes 946184 | tf_op jit(solution)/shard_map/ppermute | solution.py:257
